TPU v7x, 32 devices: a whole 2x2x4 slice. The times are simulated.
32 devices in a mesh: outer: 2 (over y), shard: 16 (over z, x, core).
Axes of the slice: x: 2, y: 2, z: 4, core: 2. Of those that a mesh axis runs over, the one named last changes fastest.
Arguments:
- grad_values: bfloat16 [2, 16, 256, 14848], P('outer', 'shard'), may hold values from -6 to 6
- grad_scales: bfloat16 [2, 16, 256, 116], P('outer', 'shard'), may hold values from 0.029907227 to 0.29882812
- block_owner: int32 [256], replicated, may hold values from 0 to 15, as said below
- projector: bfloat16 [8192, 256], P(('outer', 'shard')), may hold values from -0.375 to 0.375
- weights: bfloat16 [8192, 14848], P(('outer', 'shard')), may hold values from -6 to 6
- first_moment: float32 [256, 14848], P('shard'), may hold values from -6 to 6
- second_moment: float32 [256, 14848], P('shard'), may hold values from 0.5 to 4
Outputs:
- new_weights: bfloat16 [8192, 14848], P(('outer', 'shard'))
- new_first: float32 [256, 14848], P('shard')
- new_second: float32 [256, 14848], P('shard')
Inputs may be any that keep to these rules, and one draw needn't show every extreme that they name: `block_owner`: every index of shard owns exactly 16 rows.
All inputs are finite; a program needn't handle non-finite values.
Results may differ from a plain program's by a relative error of at most 0.0015.
Values may be sent and summed in bfloat16 or wider, within the bound.
No kernel may reach another device: no remote copies, remote signals or barrier semaphores. Data moves between devices by JAX's collectives and lax.ppermute only.
A program may use at most 128 MiB of HBM per device.

v0:
```python
import jax
import jax.numpy as jnp
from jax import lax
from jax.sharding import PartitionSpec as P

first_decay = 0.9
second_decay = 0.999
step_count = 100.0
update_scale = 0.25


def per_device(
    grad_values, grad_scales, block_owner, projector, weights, first_moment, second_moment
):
    shards = lax.axis_size("shard")
    rank_rows = block_owner.shape[0]
    owned_rows = rank_rows // shards
    values = grad_values[0, 0]
    scales = grad_scales[0, 0]
    col_blocks = scales.shape[1]
    block_width = values.shape[1] // col_blocks
    row_index = jnp.arange(rank_rows, dtype=jnp.int32)
    sort_keys = block_owner * rank_rows + row_index
    position = jnp.sum((sort_keys[None, :] < sort_keys[:, None]).astype(jnp.int32), axis=1)
    placing = (position[None, :] == row_index[:, None]).astype(jnp.bfloat16)
    sent_values = jnp.dot(placing, values, preferred_element_type=jnp.float32).astype(jnp.bfloat16)
    sent_scales = jnp.dot(placing, scales, preferred_element_type=jnp.float32).astype(jnp.bfloat16)
    partial_terms = (
        sent_values.reshape(rank_rows, col_blocks, block_width).astype(jnp.float32)
        * sent_scales.astype(jnp.float32)[..., None]
    )
    pod_sum = lax.psum_scatter(
        partial_terms.astype(jnp.bfloat16), "shard", scatter_dimension=0, tiled=True
    ).astype(jnp.float32)
    pod_low = pod_sum.reshape(owned_rows, -1).astype(jnp.bfloat16)
    all_rows = lax.all_gather(pod_low[None], "outer", axis=0, tiled=True)
    owned = jnp.sum(all_rows.astype(jnp.float32), axis=0)
    new_first = first_decay * first_moment + (1.0 - first_decay) * owned
    new_second = second_decay * second_moment + (1.0 - second_decay) * owned * owned
    corrected = new_first / (1.0 - first_decay**step_count)
    spread = jnp.sqrt(new_second / (1.0 - second_decay**step_count)) + 1e-08
    update = (corrected / spread).astype(jnp.bfloat16)
    gathered = lax.all_gather(update, "shard", axis=0, tiled=True)
    reordered = jnp.dot(projector, placing.T, preferred_element_type=jnp.float32).astype(
        jnp.bfloat16
    )
    change = jnp.dot(reordered, gathered, preferred_element_type=jnp.float32)
    new_weights = (weights.astype(jnp.float32) - update_scale * change).astype(jnp.bfloat16)
    return (new_weights, new_first, new_second)


def solution(mesh):
    placed = (
        P("outer", "shard", None, None),
        P("outer", "shard", None, None),
        P(),
        P(("outer", "shard"), None),
        P(("outer", "shard"), None),
        P("shard", None),
        P("shard", None),
    )
    return jax.shard_map(
        per_device,
        mesh=mesh,
        in_specs=placed,
        out_specs=(P(("outer", "shard"), None), P("shard", None), P("shard", None)),
        check_vma=False,
    )
```

profile of v0, /device:TPU:0, one launch (start us, length us, event | category | flops | bytes accessed | tf_op | source)
XLA Modules:
  0.0 257.0 jit_solution(17594136081369365301)
XLA Ops:
  7.2 0.0 copy-start
  7.2 0.0 reduce-scatter.2.cloned.1.call-start
  7.2 0.7 iota_add_fusion
  7.9 0.2 convert_reduce_fusion.1
  8.1 10.7 %fusion.2 = f32[256,14848]{1,0:T(8,128)} fusion(bf16[1,1,256,14848]{3,2,1,0:T(8,128)(2,1)} %param.7, s32[256]{0:T(256)S(1)} %convert_reduce_fusion.1), kind=kOutput, calls=%fused_computation.4 | convolution fusion | flops 1953824768 | bytes 22807552 | tf_op jit(solution)/shard_map/dot_general | solution.py:26
  18.8 0.0 copy-start.3
  18.8 15.6 %copy.15 = f32[256,14848]{0,1:T(8,128)} copy(f32[256,14848]{1,0:T(8,128)} %fusion.2) | data formatting | bytes 30408704 | tf_op jit(solution)/shard_map/convert_element_type | solution.py:29
  34.4 0.0 copy-done.3
  34.4 0.2 fusion.4
  34.6 11.1 %multiply_convert_fusion = bf16[256,116,128]{0,2,1:T(8,128)(2,1)} fusion(f32[256,116,128]{0,2,1:T(8,128)} %bitcast.9, f32[256,116]{0,1:T(8,128)S(1)} %fusion.4), kind=kLoop, calls=%fused_computation.5 | loop fusion | flops 7602176 | bytes 22925312 | tf_op jit(solution)/shard_map/convert_element_type | solution.py:33
  45.6 10.8 %copy.16 = bf16[256,116,128]{2,1,0:T(8,128)(2,1)} copy(bf16[256,116,128]{0,2,1:T(8,128)(2,1)} %multiply_convert_fusion) | data formatting | bytes 15204352 | tf_op jit(solution)/shard_map/convert_element_type | solution.py:33
  56.4 0.0 copy-start.1
  56.4 0.0 copy-start.2
  56.4 0.0 reduce-scatter.2.cloned.1.call-update
  56.4 0.0 all-gather.2.cloned.1.call-start
  56.5 98.2 %reduce-scatter.2.cloned.1.call-done = bf16[16,116,128]{2,1,0:T(8,128)(2,1)} async-done(((bf16[256,116,128]{2,1,0:T(8,128)(2,1)}), bf16[16,116,128]{2,1,0:T(8,128)(2,1)}) %reduce-scatter.2.cloned.1.call-update) | async-done | bytes 475152 | tf_op jit(solution)/shard_map/reduce_scatter | solution.py:32
  154.7 1.3 convert_element_type.59
  155.9 13.0 %all_gather.6 = bf16[2,16,14848]{2,1,0:T(8,128)(2,1)S(1)} all-gather(bf16[1,16,14848]{2,1,0:T(8,128)(2,1)S(1)} %convert_element_type.59), channel_id=1, replica_groups=mesh['outer'=2,'shard'=16] {'outer'}, dimensions={0}, use_global_device_ids=true | all-gather | bytes 1425408 | tf_op jit(solution)/shard_map/all_gather | solution.py:36
  168.9 0.1 convert_reduce_fusion
  169.1 0.0 copy-done.1
  169.1 0.0 copy-done.2
  169.1 1.7 divide_convert_fusion
  170.9 0.0 all-gather.2.cloned.1.call-update
  170.9 70.2 %all-gather.2.cloned.1.call-done = bf16[256,14848]{1,0:T(8,128)(2,1)} async-done(((bf16[16,14848]{1,0:T(8,128)(2,1)}), bf16[256,14848]{1,0:T(8,128)(2,1)}) %all-gather.2.cloned.1.call-update) | async-done | bytes 7602192 | tf_op jit(solution)/shard_map/all_gather | solution.py:43
  241.1 0.0 copy-done
  241.1 9.1 %fusion.1 = bf16[256,14848]{1,0:T(8,128)(2,1)} fusion(bf16[256,14848]{1,0:T(8,128)(2,1)} %all-gather.2.cloned.1.call-done, bf16[256,14848]{1,0:T(8,128)(2,1)} %param.11, bf16[256,256]{1,0:T(8,128)(2,1)S(1)} %copy-done, s32[256]{0:T(256)S(1)} %convert_reduce_fusion.1), kind=kOutput, calls=%fused_computation.2 | convolution fusion | flops 1995046912 | bytes 22938624 | tf_op jit(solution)/shard_map/dot_general | solution.py:47
Async XLA Ops:
  7.2 233.9 %copy-start = (bf16[256,256]{1,0:T(8,128)(2,1)S(1)}, bf16[256,256]{1,0:T(8,128)(2,1)}, u32[]{:S(2)}) copy-start(bf16[256,256]{1,0:T(8,128)(2,1)} %param.10) | copy-start | bytes 393220
  7.2 147.5 %reduce-scatter.2.cloned.1.call-start = ((), (), s32[]{:S(2)}) async-start(), calls=%async_computation.1 | async-start | bytes 8355840 | tf_op jit(solution)/shard_map/reduce_scatter | solution.py:32
  18.8 15.6 %copy-start.3 = (bf16[1,1,256,116]{2,3,1,0:T(8,128)(2,1)S(1)}, bf16[1,1,256,116]{2,3,1,0:T(8,128)(2,1)}, u32[]{:S(2)}) copy-start(bf16[1,1,256,116]{2,3,1,0:T(8,128)(2,1)} %param.8) | copy-start | bytes 178180
  56.4 112.7 %copy-start.1 = (f32[16,14848]{1,0:T(8,128)S(1)}, f32[16,14848]{1,0:T(8,128)}, u32[]{:S(2)}) copy-start(f32[16,14848]{1,0:T(8,128)} %param.12) | copy-start | bytes 2850820
  56.4 112.7 %copy-start.2 = (f32[16,14848]{1,0:T(8,128)S(1)}, f32[16,14848]{1,0:T(8,128)}, u32[]{:S(2)}) copy-start(f32[16,14848]{1,0:T(8,128)} %param.13) | copy-start | bytes 2850820
  56.4 184.6 %all-gather.2.cloned.1.call-start = ((), (), s32[]{:S(2)}) async-start(), calls=%async_computation.2 | async-start | bytes 8077312 | tf_op jit(solution)/shard_map/all_gather | solution.py:43
Sparse Core Ops, SparseCore 0:
  56.6 98.0 reduce-scatter.1
  171.0 70.0 all-gather.1
where the time goes:
time: 258 us; the launch traced here: 257 us
  waiting for transfers between devices  168 us (65%)
  local copies, waits for them, and re-layouts  27.6 us (11%)
  matrix products  19.9 us (8%)
  between operations  14.1 us (5%)
  other arithmetic  13.9 us (5%)
  blocking collectives  13 us (5%)
    reduce_scatter x1, waiting for transfers between devices, per_device(): lax.psum_scatter(partial_terms.astype(jnp.bfloat16), 'shard', scatter_dim...  98.2 us
    all_gather x1, waiting for transfers between devices, per_device(): gathered = lax.all_gather(update, 'shard', axis=0, tiled=True)  70.2 us
    convert_element_type x1, local copies, waits for them, and re-layouts, per_device(): sent_values.reshape(rank_rows, col_blocks, block_width).astype(jnp.float32)  15.6 us
    all_gather x1, blocking collectives, per_device(): all_rows = lax.all_gather(pod_low[None], 'outer', axis=0, tiled=True)  13 us
    convert_element_type x1, other arithmetic, per_device(): partial_terms.astype(jnp.bfloat16)  11.1 us
    convert_element_type x1, local copies, waits for them, and re-layouts, per_device(): partial_terms.astype(jnp.bfloat16)  10.8 us
    dot_general x1, matrix products, per_device(): jnp.dot(placing, values, preferred_element_type=jnp.float32)  10.7 us
    dot_general x1, matrix products, per_device(): change = jnp.dot(reordered, gathered, preferred_element_type=jnp.float32)  9.09 us
  transfers between devices with their start and end apart: 2, of which 2 were waited for; matrix products, arithmetic and copies ran while one was open for 0% of the time, Pallas kernels for 0%

commit v1 on v0

v1 whole, which is shorter than its diff:
```python
import functools
import math

import jax
import jax.numpy as jnp
from jax import lax
from jax.experimental import pallas as pl
from jax.experimental.pallas import tpu as pltpu
from jax.sharding import PartitionSpec as P

first_decay = 0.9
second_decay = 0.999
step_count = 100.0
update_scale = 0.25


def bits_of(count):
    return range(count.bit_length() - 1)


def largest_divisor(count, limit):
    return max(d for d in range(1, limit + 1) if count % d == 0)


def swap(array, stage):
    axis, bit = stage
    size = lax.axis_size(axis)
    return lax.ppermute(array, axis, [(i, i ^ (1 << bit)) for i in range(size)])


def prepare_kernel(first_block, position_ref, values_ref, scales_ref, keep_ref, send_ref):
    rows, width = values_ref.shape
    blocks = scales_ref.shape[1]
    block_width = 128
    step_blocks = width // block_width
    placing = (
        lax.broadcasted_iota(jnp.int32, (rows, rows), 0) == position_ref[...]
    ).astype(jnp.bfloat16)
    block = lax.broadcasted_iota(jnp.int32, (blocks, width), 1) // block_width
    block = block + first_block + pl.program_id(0) * step_blocks
    spread = (block == lax.broadcasted_iota(jnp.int32, (blocks, width), 0)).astype(jnp.bfloat16)
    scales = jnp.dot(scales_ref[...], spread, preferred_element_type=jnp.float32)
    terms = (values_ref[...].astype(jnp.float32) * scales).astype(jnp.bfloat16)
    placed = jnp.dot(placing, terms, preferred_element_type=jnp.float32).astype(jnp.bfloat16)
    keep_ref[...] = placed[: rows // 2]
    send_ref[...] = placed[rows // 2 :]


def prepare(values, scales, position, start, count, block_width):
    rows = values.shape[0]
    step = largest_divisor(math.gcd(start, count), 8)
    assert block_width == 128
    half = jax.ShapeDtypeStruct((rows // 2, count * block_width), jnp.bfloat16)
    out = pl.BlockSpec((rows // 2, step * block_width), lambda i: (0, i))
    return pl.pallas_call(
        functools.partial(prepare_kernel, start),
        grid=(count // step,),
        in_specs=[
            pl.BlockSpec((1, rows), lambda i: (0, 0)),
            pl.BlockSpec((rows, step * block_width), lambda i: (0, start // step + i)),
            pl.BlockSpec(scales.shape, lambda i: (0, 0)),
        ],
        out_specs=[out, out],
        out_shape=[half, half],
        compiler_params=pltpu.CompilerParams(vmem_limit_bytes=48 * 1024 * 1024),
        cost_estimate=pl.CostEstimate(
            flops=2 * rows * rows * count * block_width,
            bytes_accessed=4 * rows * count * block_width,
            transcendentals=0,
        ),
        name="prepare",
    )(position, values, scales)


def apply_kernel(projector_ref, weights_ref, *refs):
    pieces, out_ref = refs[:4], refs[-1]
    direction = jnp.concatenate([piece[...] for piece in pieces], axis=0)
    change = jnp.dot(projector_ref[...], direction, preferred_element_type=jnp.float32)
    out_ref[...] = (weights_ref[...].astype(jnp.float32) - update_scale * change).astype(
        out_ref.dtype
    )


def apply_update(projector, weights, pieces, so_far, start, count, block_width):
    rows = weights.shape[0]
    rank = projector.shape[1]
    step = largest_divisor(math.gcd(start, count), 8)
    width = step * block_width
    aliased = [] if so_far is None else [so_far]
    return pl.pallas_call(
        apply_kernel,
        grid=(count // step,),
        in_specs=[
            pl.BlockSpec(projector.shape, lambda i: (0, 0)),
            pl.BlockSpec((rows, width), lambda i: (0, start // step + i)),
        ]
        + [pl.BlockSpec((piece.shape[0], width), lambda i: (0, i)) for piece in pieces]
        + [pl.BlockSpec(memory_space=pl.ANY) for _ in aliased],
        out_specs=pl.BlockSpec((rows, width), lambda i: (0, start // step + i)),
        out_shape=jax.ShapeDtypeStruct(weights.shape, weights.dtype),
        input_output_aliases={} if so_far is None else {2 + len(pieces): 0},
        compiler_params=pltpu.CompilerParams(vmem_limit_bytes=48 * 1024 * 1024),
        cost_estimate=pl.CostEstimate(
            flops=2 * rows * rank * count * block_width,
            bytes_accessed=6 * rows * count * block_width,
            transcendentals=0,
        ),
        name="apply_update",
    )(projector, weights, *pieces, *aliased)


def added(left, right):
    return (left.astype(jnp.float32) + right.astype(jnp.float32)).astype(jnp.bfloat16)


def per_device(
    grad_values, grad_scales, block_owner, projector, weights, first_moment, second_moment
):
    shards, outers = lax.axis_size("shard"), lax.axis_size("outer")
    shard, outer = lax.axis_index("shard"), lax.axis_index("outer")
    rank_rows = block_owner.shape[0]
    owned_rows = rank_rows // shards
    leaf_rows = owned_rows // outers
    values = grad_values[0, 0]
    scales = grad_scales[0, 0]
    col_blocks = scales.shape[1]
    block_width = values.shape[1] // col_blocks

    row_index = jnp.arange(rank_rows, dtype=jnp.int32)
    earlier = (block_owner[None, :] == block_owner[:, None]) & (
        row_index[None, :] < row_index[:, None]
    )
    rank_in_owner = jnp.sum(earlier.astype(jnp.int32), axis=1)
    away = {"shard": block_owner ^ shard, "outer": (rank_in_owner // leaf_rows) ^ outer}

    shard_stages = [("shard", bit) for bit in bits_of(shards)]
    outer_stages = [("outer", bit) for bit in bits_of(outers)]
    core, inner, last = shard_stages[0], shard_stages[1:-1], shard_stages[-1]
    turning = inner[:1] + outer_stages + inner[1:]
    orders = [turning[turn:] + turning[:turn] + [last] for turn in range(3)]
    unit = largest_divisor(col_blocks, 4)
    units = col_blocks // unit
    counts = [unit * ((units + 2 - turn) // 3) for turn in range(3)]
    starts = [sum(counts[:turn]) for turn in range(3)]

    placings, held = [], []
    for order, start, count in zip(orders, starts, counts):
        position = jnp.zeros_like(block_owner)
        for axis, bit in [core] + order:
            position = 2 * position + ((away[axis] >> bit) & 1)
        position = position * leaf_rows + rank_in_owner % leaf_rows
        placings.append((position[None, :] == row_index[:, None]).astype(jnp.bfloat16))
        held.append(prepare(values, scales, position[None, :], start, count, block_width))

    partial = []
    for keep, send in held:
        partial.append((keep, swap(send, core)))
    for step in range(len(orders[0])):
        for turn, order in enumerate(orders):
            mine, came = partial[turn]
            half = mine.shape[0] // 2
            send = added(mine[half:], came[half:])
            keep = added(mine[:half], came[:half])
            partial[turn] = (keep, swap(send, order[step]))
    owned_parts = [added(mine, came) for mine, came in partial]

    def normalized(owned, first, second):
        new_first = first_decay * first + (1.0 - first_decay) * owned
        new_second = second_decay * second + (1.0 - second_decay) * owned * owned
        return new_first, new_second

    gathered = []
    for owned, start, count in zip(owned_parts, starts, counts):
        own = (outer * leaf_rows, start * block_width)
        shape = (leaf_rows, count * block_width)
        new_first, new_second = normalized(
            owned.astype(jnp.float32),
            lax.dynamic_slice(first_moment, own, shape),
            lax.dynamic_slice(second_moment, own, shape),
        )
        corrected = new_first / (1.0 - first_decay**step_count)
        spread = jnp.sqrt(new_second / (1.0 - second_decay**step_count)) + 1e-08
        gathered.append((corrected / spread).astype(jnp.bfloat16))
    steps = len(orders[0])
    for step in reversed(range(1, steps)):
        for turn, order in enumerate(orders):
            mine = gathered[turn]
            gathered[turn] = jnp.concatenate([mine, swap(mine, order[step])], axis=0)
    pieces = []
    for mine, order in zip(gathered, orders):
        pieces.append((mine, swap(mine, order[0]), swap(mine, core)))

    owned = jnp.concatenate(owned_parts, axis=1)
    for stage in outer_stages:
        other = swap(owned, stage)
        low = ((outer >> stage[1]) & 1) == 0
        owned = jnp.where(
            low,
            jnp.concatenate([owned, other], axis=0),
            jnp.concatenate([other, owned], axis=0),
        )
    new_first, new_second = normalized(owned.astype(jnp.float32), first_moment, second_moment)

    new_weights = None
    for turn in range(3):
        mine, came, beside = pieces[turn]
        reordered = jnp.dot(
            projector, placings[turn].T, preferred_element_type=jnp.float32
        ).astype(jnp.bfloat16)
        new_weights = apply_update(
            reordered,
            weights,
            (mine, came, beside, swap(came, core)),
            new_weights,
            starts[turn],
            counts[turn],
            block_width,
        )
    return (new_weights, new_first, new_second)


def solution(mesh):
    placed = (
        P("outer", "shard", None, None),
        P("outer", "shard", None, None),
        P(),
        P(("outer", "shard"), None),
        P(("outer", "shard"), None),
        P("shard", None),
        P("shard", None),
    )
    return jax.shard_map(
        per_device,
        mesh=mesh,
        in_specs=placed,
        out_specs=(P(("outer", "shard"), None), P("shard", None), P("shard", None)),
        check_vma=False,
    )
```

time: 258 us -> 157 us (0.61)
  waiting for transfers between devices: 168 us -> 54.1 us
  starting transfers between devices: 0.08 us -> 48 us
  Pallas kernels: 0 us -> 36.9 us
  local copies, waits for them, and re-layouts: 27.6 us -> 2 us
  matrix products: 19.9 us -> 1.33 us
  between operations: 14.1 us -> 0.84 us
  blocking collectives: 13 us -> 0 us
    reduce_scatter x1 -> x0, waiting for transfers between devices: 98.2 us -> none  [per_device(): lax.psum_scatter(partial_terms.astype(jnp.bfloat16), 'shard', scatter_dim...]
    all_gather x1 -> x0, waiting for transfers between devices: 70.2 us -> none  [per_device(): gathered = lax.all_gather(update, 'shard', axis=0, tiled=True)]
    ppermute x0 -> x34, waiting for transfers between devices: none -> 54.1 us  [swap(): return lax.ppermute(array, axis, [(i, i ^ 1 << bit) for i in range(size)])]
    ppermute x0 -> x34, starting transfers between devices: none -> 48 us  [swap(): return lax.ppermute(array, axis, [(i, i ^ 1 << bit) for i in range(size)])]
    pallas_call x0 -> x6, Pallas kernels: none -> 36.9 us  [the longest x3 19 us: prepare(): pl.pallas_call(functools.partial(prepare_kernel, start), grid=(count // s...]
    convert_element_type x3 -> x0, local copies, waits for them, and re-layouts: 27.6 us -> none  [the longest x1 15.6 us: per_device(): sent_values.reshape(rank_rows, col_blocks, block_width).astype(jnp.float32)]
    dot_general x3, matrix products: 19.9 us -> 1.33 us  [per_device(): jnp.dot(projector, placings[turn].T, preferred_element_type=jnp.float32)]
    all_gather x1 -> x0, blocking collectives: 13 us -> none  [per_device(): all_rows = lax.all_gather(pod_low[None], 'outer', axis=0, tiled=True)]
  transfers between devices with their start and end apart: 2 -> 34, of which waited for: 2 -> 15; matrix products, arithmetic and copies ran while one was open for 0% -> 8% of each run, Pallas kernels for 0% -> 14%
where the time goes in v1:
time: 157 us; the launch traced here: 156 us
  waiting for transfers between devices  54.1 us (34%)
  starting transfers between devices  48 us (31%)
  Pallas kernels  36.9 us (24%)
  other arithmetic  12.9 us (8%)
  local copies, waits for them, and re-layouts  2 us (1%)
    ppermute x34, waiting for transfers between devices, swap(): return lax.ppermute(array, axis, [(i, i ^ 1 << bit) for i in range(size)])  54.1 us
    ppermute x34, starting transfers between devices, swap(): return lax.ppermute(array, axis, [(i, i ^ 1 << bit) for i in range(size)])  48 us
    pallas_call x3, Pallas kernels, prepare(): pl.pallas_call(functools.partial(prepare_kernel, start), grid=(count // s...  19 us
    pallas_call x3, Pallas kernels, apply_update(): pl.pallas_call(apply_kernel, grid=(count // step,), in_specs=[pl.BlockSpe...  17.9 us
    convert_element_type x12, other arithmetic, added(): (left.astype(jnp.float32) + right.astype(jnp.float32)).astype(jnp.bfloat16)  5.94 us
    add x1, other arithmetic, normalized(): new_second = second_decay * second + (1.0 - second_decay) * owned * owned  3.28 us
  transfers between devices with their start and end apart: 34, of which 15 were waited for; matrix products, arithmetic and copies ran while one was open for 8% of the time, Pallas kernels for 14%

profile of v1, /device:TPU:0, one launch (start us, length us, event | category | flops | bytes accessed | tf_op | source)
XLA Modules:
  0.0 156.0 jit_solution(10734314155868057628)
XLA Ops:
  0.7 0.9 convert_reduce_fusion
  3.0 0.9 copy.17
  3.9 7.8 %prepare.3 = (bf16[128,4608]{1,0:T(8,128)(2,1)S(1)}, bf16[128,4608]{1,0:T(8,128)(2,1)}) custom-call(s32[1,256]{1,0:T(1,128)S(1)} %bitcast.18, bf16[256,14848]{1,0:T(8,128)(2,1)} %bitcast.20, bf16[256,116]{1,0:T(8,128)(2,1)S(1)} %bitcast.14), custom_call_target="tpu_custom_call" | custom-call | flops 603979776 | bytes 4718592 | tf_op jit(solution)/shard_map/prepare/pallas_call | solution.py:55
  11.8 1.0 copy-done.1
  13.3 5.6 %prepare.4 = (bf16[128,5120]{1,0:T(8,128)(2,1)S(1)}, bf16[128,5120]{1,0:T(8,128)(2,1)}) custom-call(s32[1,256]{1,0:T(1,128)S(1)} %bitcast.19, bf16[256,14848]{1,0:T(8,128)(2,1)} %bitcast.21, bf16[256,116]{1,0:T(8,128)(2,1)S(1)} %bitcast.15), custom_call_target="tpu_custom_call" | custom-call | flops 671088640 | bytes 5242880 | tf_op jit(solution)/shard_map/prepare/pallas_call | solution.py:55
  18.9 5.6 %prepare.5 = (bf16[128,5120]{1,0:T(8,128)(2,1)S(1)}, bf16[128,5120]{1,0:T(8,128)(2,1)}) custom-call(s32[1,256]{1,0:T(1,128)S(1)} %bitcast.17, bf16[256,14848]{1,0:T(8,128)(2,1)} %bitcast.22, bf16[256,116]{1,0:T(8,128)(2,1)S(1)} %bitcast.16), custom_call_target="tpu_custom_call" | custom-call | flops 671088640 | bytes 5242880 | tf_op jit(solution)/shard_map/prepare/pallas_call | solution.py:55
  25.2 1.9 %add_convert_fusion.5 = (bf16[64,4608]{1,0:T(8,128)(2,1)S(1)}, bf16[64,4608]{1,0:T(8,128)(2,1)S(1)}) fusion(bf16[128,4608]{1,0:T(8,128)(2,1)} %collective-permute-done, bf16[128,4608]{1,0:T(8,128)(2,1)} %copy-done.1), kind=kLoop, calls=%fused_computation.7 | loop fusion | flops 2359296 | bytes 3538944 | tf_op jit(solution)/shard_map/convert_element_type | solution.py:113
  27.1 2.6 %collective-permute-start.1 = (bf16[64,4608]{1,0:T(8,128)(2,1)S(1)}, bf16[64,4608]{1,0:T(8,128)(2,1)S(1)}, u32[]{:S(2)}, u32[]{:S(2)}) collective-permute-start(bf16[64,4608]{1,0:T(8,128)(2,1)S(1)} %get-tuple-element.28), channel_id=1, source_target_pairs={{0,4},{1,5},{2,6},{3,7},{4,0},{5,1},{6,2},{7,3},{8,12},{9,13},{10,... | collective-permute-start | bytes 1769480 | tf_op jit(solution)/shard_map/ppermute | solution.py:28
  29.7 1.6 %add_convert_fusion.3 = (bf16[64,5120]{1,0:T(8,128)(2,1)S(1)}, bf16[64,5120]{1,0:T(8,128)(2,1)S(1)}) fusion(bf16[128,5120]{1,0:T(8,128)(2,1)} %collective-permute-done.11, bf16[128,5120]{1,0:T(8,128)(2,1)S(1)} %get-tuple-element.11), kind=kLoop, calls=%fused_computation.4 | loop fusion | flops 2621440 | bytes 3932160 | tf_op jit(solution)/shard_map/convert_element_type | solution.py:113
  31.3 1.6 %collective-permute-start.12 = (bf16[64,5120]{1,0:T(8,128)(2,1)S(1)}, bf16[64,5120]{1,0:T(8,128)(2,1)S(1)}, u32[]{:S(2)}, u32[]{:S(2)}) collective-permute-start(bf16[64,5120]{1,0:T(8,128)(2,1)S(1)} %get-tuple-element.26), channel_id=1, source_target_pairs={{0,16},{16,0},{1,17},{17,1},{2,18},{18,2},{3,19},{19,3},{4,20},{20... | collective-permute-start | bytes 1966088 | tf_op jit(solution)/shard_map/ppermute | solution.py:28
  32.9 10.8 %collective-permute-done.1 = bf16[64,4608]{1,0:T(8,128)(2,1)S(1)} collective-permute-done((bf16[64,4608]{1,0:T(8,128)(2,1)S(1)}, bf16[64,4608]{1,0:T(8,128)(2,1)S(1)}, u32[]{:S(2)}, u32[]{:S(2)}) %collective-permute-start.1) | collective-permute-done | bytes 589856 | tf_op jit(solution)/shard_map/ppermute | solution.py:28
  43.8 1.7 %collective-permute-start.2 = (bf16[32,4608]{1,0:T(8,128)(2,1)S(1)}, bf16[32,4608]{1,0:T(8,128)(2,1)S(1)}, u32[]{:S(2)}, u32[]{:S(2)}) collective-permute-start(bf16[32,4608]{1,0:T(8,128)(2,1)S(1)} %get-tuple-element.36), channel_id=1, source_target_pairs={{0,2},{1,3},{2,0},{3,1},{4,6},{5,7},{6,4},{7,5},{8,10},{9,11},{10,... | collective-permute-start | bytes 884744 | tf_op jit(solution)/shard_map/ppermute | solution.py:28
  45.6 1.7 %add_convert_fusion.1 = (bf16[64,5120]{1,0:T(8,128)(2,1)S(1)}, bf16[64,5120]{1,0:T(8,128)(2,1)S(1)}) fusion(bf16[128,5120]{1,0:T(8,128)(2,1)} %collective-permute-done.22, bf16[128,5120]{1,0:T(8,128)(2,1)S(1)} %get-tuple-element.13), kind=kLoop, calls=%fused_computation.2 | loop fusion | flops 2621440 | bytes 3932160 | tf_op jit(solution)/shard_map/convert_element_type | solution.py:113
  47.7 6.1 %collective-permute-done.2 = bf16[32,4608]{1,0:T(8,128)(2,1)S(1)} collective-permute-done((bf16[32,4608]{1,0:T(8,128)(2,1)S(1)}, bf16[32,4608]{1,0:T(8,128)(2,1)S(1)}, u32[]{:S(2)}, u32[]{:S(2)}) %collective-permute-start.2) | collective-permute-done | bytes 294944 | tf_op jit(solution)/shard_map/ppermute | solution.py:28
  53.9 1.8 %collective-permute-start.3 = (bf16[16,4608]{1,0:T(8,128)(2,1)S(1)}, bf16[16,4608]{1,0:T(8,128)(2,1)S(1)}, u32[]{:S(2)}, u32[]{:S(2)}) collective-permute-start(bf16[16,4608]{1,0:T(8,128)(2,1)S(1)} %get-tuple-element.42), channel_id=1, source_target_pairs={{0,16},{16,0},{1,17},{17,1},{2,18},{18,2},{3,19},{19,3},{4,20},{20... | collective-permute-start | bytes 442376 | tf_op jit(solution)/shard_map/ppermute | solution.py:28
  55.8 1.6 %collective-permute-start.13 = (bf16[32,5120]{1,0:T(8,128)(2,1)S(1)}, bf16[32,5120]{1,0:T(8,128)(2,1)S(1)}, u32[]{:S(2)}, u32[]{:S(2)}) collective-permute-start(bf16[32,5120]{1,0:T(8,128)(2,1)S(1)} %get-tuple-element.34), channel_id=1, source_target_pairs={{0,4},{1,5},{2,6},{3,7},{4,0},{5,1},{6,2},{7,3},{8,12},{9,13},{10,... | collective-permute-start | bytes 983048 | tf_op jit(solution)/shard_map/ppermute | solution.py:28
  57.5 1.6 %collective-permute-done.3 = bf16[16,4608]{1,0:T(8,128)(2,1)S(1)} collective-permute-done((bf16[16,4608]{1,0:T(8,128)(2,1)S(1)}, bf16[16,4608]{1,0:T(8,128)(2,1)S(1)}, u32[]{:S(2)}, u32[]{:S(2)}) %collective-permute-start.3) | collective-permute-done | bytes 147488 | tf_op jit(solution)/shard_map/ppermute | solution.py:28
  59.1 2.8 %collective-permute-start.4 = (bf16[8,4608]{1,0:T(8,128)(2,1)S(1)}, bf16[8,4608]{1,0:T(8,128)(2,1)S(1)}, u32[]{:S(2)}, u32[]{:S(2)}) collective-permute-start(bf16[8,4608]{1,0:T(8,128)(2,1)S(1)} %add_convert_fusion.25), channel_id=1, source_target_pairs={{0,8},{1,9},{2,10},{3,11},{4,12},{5,13},{6,14},{7,15},{8,0},{9,1},... | collective-permute-start | bytes 221192 | tf_op jit(solution)/shard_map/ppermute | solution.py:28
  61.9 4.8 %collective-permute-done.23 = bf16[64,5120]{1,0:T(8,128)(2,1)S(1)} collective-permute-done((bf16[64,5120]{1,0:T(8,128)(2,1)S(1)}, bf16[64,5120]{1,0:T(8,128)(2,1)S(1)}, u32[]{:S(2)}, u32[]{:S(2)}) %collective-permute-start.23) | collective-permute-done | bytes 655392 | tf_op jit(solution)/shard_map/ppermute | solution.py:28
  66.9 1.5 collective-permute-start.24
  68.6 2.7 %collective-permute-start.5 = (bf16[8,4608]{1,0:T(8,128)(2,1)S(1)}, bf16[8,4608]{1,0:T(8,128)(2,1)S(1)}, u32[]{:S(2)}, u32[]{:S(2)}) collective-permute-start(bf16[8,4608]{1,0:T(8,128)(2,1)S(1)} %get-tuple-element.21), channel_id=1, source_target_pairs={{0,8},{1,9},{2,10},{3,11},{4,12},{5,13},{6,14},{7,15},{8,0},{9,1},... | collective-permute-start | bytes 221192 | tf_op jit(solution)/shard_map/ppermute | solution.py:28
  71.4 1.6 collective-permute-start.14
  72.9 2.7 %collective-permute-done.24 = bf16[32,5120]{1,0:T(8,128)(2,1)S(1)} collective-permute-done((bf16[32,5120]{1,0:T(8,128)(2,1)S(1)}, bf16[32,5120]{1,0:T(8,128)(2,1)S(1)}, u32[]{:S(2)}, u32[]{:S(2)}) %collective-permute-start.24) | collective-permute-done | bytes 327712 | tf_op jit(solution)/shard_map/ppermute | solution.py:28
  75.8 1.4 collective-permute-start.25
  77.2 2.7 %collective-permute-start.15 = (bf16[8,5120]{1,0:T(8,128)(2,1)S(1)}, bf16[8,5120]{1,0:T(8,128)(2,1)S(1)}, u32[]{:S(2)}, u32[]{:S(2)}) collective-permute-start(bf16[8,5120]{1,0:T(8,128)(2,1)S(1)} %add_convert_fusion.22), channel_id=1, source_target_pairs={{0,8},{1,9},{2,10},{3,11},{4,12},{5,13},{6,14},{7,15},{8,0},{9,1},... | collective-permute-start | bytes 245768 | tf_op jit(solution)/shard_map/ppermute | solution.py:28
  79.8 1.3 collective-permute-done.25
  81.2 2.4 %collective-permute-start.26 = (bf16[8,5120]{1,0:T(8,128)(2,1)S(1)}, bf16[8,5120]{1,0:T(8,128)(2,1)S(1)}, u32[]{:S(2)}, u32[]{:S(2)}) collective-permute-start(bf16[8,5120]{1,0:T(8,128)(2,1)S(1)} %add_convert_fusion.19), channel_id=1, source_target_pairs={{0,8},{1,9},{2,10},{3,11},{4,12},{5,13},{6,14},{7,15},{8,0},{9,1},... | collective-permute-start | bytes 245768 | tf_op jit(solution)/shard_map/ppermute | solution.py:28
  83.6 1.6 %collective-permute-start.6 = (bf16[16,4608]{1,0:T(8,128)(2,1)S(1)}, bf16[16,4608]{1,0:T(8,128)(2,1)S(1)}, u32[]{:S(2)}, u32[]{:S(2)}) collective-permute-start(bf16[16,4608]{1,0:T(8,128)(2,1)S(1)} %pad_maximum_fusion.9), channel_id=1, source_target_pairs={{0,16},{16,0},{1,17},{17,1},{2,18},{18,2},{3,19},{19,3},{4,20},{20... | collective-permute-start | bytes 442376 | tf_op jit(solution)/shard_map/ppermute | solution.py:28
  85.2 1.4 collective-permute-done.26
  86.9 2.4 %collective-permute-start.27 = (bf16[8,5120]{1,0:T(8,128)(2,1)S(1)}, bf16[8,5120]{1,0:T(8,128)(2,1)S(1)}, u32[]{:S(2)}, u32[]{:S(2)}) collective-permute-start(bf16[8,5120]{1,0:T(8,128)(2,1)S(1)} %get-tuple-element.15), channel_id=1, source_target_pairs={{0,8},{1,9},{2,10},{3,11},{4,12},{5,13},{6,14},{7,15},{8,0},{9,1},... | collective-permute-start | bytes 245768 | tf_op jit(solution)/shard_map/ppermute | solution.py:28
  89.3 1.6 collective-permute-start.7
  91.3 1.1 collective-permute-done.27
  92.4 3.6 %collective-permute-start.28 = (bf16[16,5120]{1,0:T(8,128)(2,1)S(1)}, bf16[16,5120]{1,0:T(8,128)(2,1)S(1)}, u32[]{:S(2)}, u32[]{:S(2)}) collective-permute-start(bf16[16,5120]{1,0:T(8,128)(2,1)S(1)} %pad_maximum_fusion.8), channel_id=1, source_target_pairs={{0,4},{1,5},{2,6},{3,7},{4,0},{5,1},{6,2},{7,3},{8,12},{9,13},{10,... | collective-permute-start | bytes 491528 | tf_op jit(solution)/shard_map/ppermute | solution.py:28
  96.2 1.3 collective-permute-start.17
  97.6 1.7 %collective-permute-done.28 = bf16[16,5120]{1,0:T(8,128)(2,1)S(1)} collective-permute-done((bf16[16,5120]{1,0:T(8,128)(2,1)S(1)}, bf16[16,5120]{1,0:T(8,128)(2,1)S(1)}, u32[]{:S(2)}, u32[]{:S(2)}) %collective-permute-start.28) | collective-permute-done | bytes 163872 | tf_op jit(solution)/shard_map/ppermute | solution.py:28
  99.3 1.3 collective-permute-start.29
  100.6 1.0 collective-permute-done.17
  101.6 3.5 %collective-permute-start.18 = (bf16[32,5120]{1,0:T(8,128)(2,1)S(1)}, bf16[32,5120]{1,0:T(8,128)(2,1)S(1)}, u32[]{:S(2)}, u32[]{:S(2)}) collective-permute-start(bf16[32,5120]{1,0:T(8,128)(2,1)S(1)} %pad_maximum_fusion.3), channel_id=1, source_target_pairs={{0,4},{1,5},{2,6},{3,7},{4,0},{5,1},{6,2},{7,3},{8,12},{9,13},{10,... | collective-permute-start | bytes 983048 | tf_op jit(solution)/shard_map/ppermute | solution.py:28
  105.3 1.2 collective-permute-done.29
  106.5 3.2 %collective-permute-start.30 = (bf16[64,5120]{1,0:T(8,128)(2,1)S(1)}, bf16[64,5120]{1,0:T(8,128)(2,1)S(1)}, u32[]{:S(2)}, u32[]{:S(2)}) collective-permute-start(bf16[64,5120]{1,0:T(8,128)(2,1)S(1)} %pad_maximum_fusion.1.refs_0_), channel_id=1, source_target_pairs={{0,2},{1,3},{2,0},{3,1},{4,6},{5,7},{6,4},{7,5},{8,10},{9,11},{10,... | collective-permute-start | bytes 1966088 | tf_op jit(solution)/shard_map/ppermute | solution.py:28
  109.7 4.0 %collective-permute-done.18 = bf16[32,5120]{1,0:T(8,128)(2,1)S(1)} collective-permute-done((bf16[32,5120]{1,0:T(8,128)(2,1)S(1)}, bf16[32,5120]{1,0:T(8,128)(2,1)S(1)}, u32[]{:S(2)}, u32[]{:S(2)}) %collective-permute-start.18) | collective-permute-done | bytes 327712 | tf_op jit(solution)/shard_map/ppermute | solution.py:28
  113.8 1.8 %collective-permute-start.19 = (bf16[64,5120]{1,0:T(8,128)(2,1)S(1)}, bf16[64,5120]{1,0:T(8,128)(2,1)}, u32[]{:S(2)}, u32[]{:S(2)}) collective-permute-start(bf16[64,5120]{1,0:T(8,128)(2,1)S(1)} %pad_maximum_fusion.refs_0_), channel_id=1, source_target_pairs={{0,16},{16,0},{1,17},{17,1},{2,18},{18,2},{3,19},{19,3},{4,20},{20... | collective-permute-start | bytes 1966088 | tf_op jit(solution)/shard_map/ppermute | solution.py:28
  117.7 14.8 %collective-permute-done.33 = bf16[8,14848]{1,0:T(8,128)(2,1)} collective-permute-done((bf16[8,14848]{1,0:T(8,128)(2,1)}, bf16[8,14848]{1,0:T(8,128)(2,1)}, u32[]{:S(2)}, u32[]{:S(2)}) %collective-permute-start.33) | collective-permute-done | bytes 237600 | tf_op jit(solution)/shard_map/ppermute | solution.py:28
  133.6 3.3 %fusion.4 = (f32[16,14848]{1,0:T(8,128)}, f32[16,14848]{1,0:T(8,128)}) fusion(f32[16,14848]{1,0:T(8,128)} %param.13, bf16[8,4608]{1,0:T(8,128)(2,1)S(1)} %get-tuple-element.22, bf16[8,5120]{1,0:T(8,128)(2,1)} %copy-done.6, bf16[8,5120]{1,0:T(8,128)(2,1)} %copy-done.5, bf16[8,14848]{1,0:T(8,128)(2,1)} %collective-permute-done.33, pred[]{:T(512)S(6)} %eq.62, ...), kind=kLoop, calls=%fused_computation.15 | loop fusion | flops 5939200 | bytes 4276225 | tf_op jit(solution)/shard_map/add | solution.py:169
  136.9 1.3 collective-permute-done.32.refs_3_
  138.1 5.3 %apply_update.3.refs_4_ = bf16[256,14848]{1,0:T(8,128)(2,1)} custom-call(bf16[256,256]{1,0:T(8,128)(2,1)S(1)} %fusion.2.projector_ref, bf16[256,14848]{1,0:T(8,128)(2,1)} %weights_ref.5, bf16[64,5120]{1,0:T(8,128)(2,1)S(1)} %pad_maximum_fusion.1.refs_0_, bf16[64,5120]{1,0:T(8,128)(2,1)S(1)} %collective-permute-done.30.refs_1_, ...), custom_call_target="tpu_custom_call" | custom-call | flops 671088640 | bytes 7864320 | tf_op jit(solution)/shard_map/apply_update/pallas_call | solution.py:90
  143.5 5.4 %apply_update.4.refs_4_ = bf16[256,14848]{1,0:T(8,128)(2,1)} custom-call(bf16[256,256]{1,0:T(8,128)(2,1)S(1)} %copy-done.2, bf16[256,14848]{1,0:T(8,128)(2,1)} %weights_ref.5, bf16[64,5120]{1,0:T(8,128)(2,1)S(1)} %pad_maximum_fusion.refs_0_, bf16[64,5120]{1,0:T(8,128)(2,1)} %collective-permute-done.19.refs_1_, ...), custom_call_target="tpu_custom_call", output_to_operand_aliasing={{}: (6, {})} | custom-call | flops 671088640 | bytes 7864320 | tf_op jit(solution)/shard_map/apply_update/pallas_call | solution.py:90
  148.9 7.1 %apply_update.5 = bf16[256,14848]{1,0:T(8,128)(2,1)} custom-call(bf16[256,256]{1,0:T(8,128)(2,1)S(1)} %fusion.projector_ref, bf16[256,14848]{1,0:T(8,128)(2,1)} %weights_ref.5, bf16[64,4608]{1,0:T(8,128)(2,1)S(1)} %pad_maximum_fusion.2.refs_0_, bf16[64,4608]{1,0:T(8,128)(2,1)} %collective-permute-done.8.refs_1_, ...), custom_call_target="tpu_custom_call", output_to_operand_aliasing={{}: (6, {})} | custom-call | flops 603979776 | bytes 7077888 | tf_op jit(solution)/shard_map/apply_update/pallas_call | solution.py:90
  (72 shorter events, 8.4 us)
Async XLA Ops:
  0.6 24.3 %copy-start = (bf16[256,256]{1,0:T(8,128)(2,1)S(1)}, bf16[256,256]{1,0:T(8,128)(2,1)}, u32[]{:S(2)}) copy-start(bf16[256,256]{1,0:T(8,128)(2,1)} %param.10) | copy-start | bytes 393220
  11.8 1.0 copy-start.1
  12.8 12.4 %collective-permute-start = (bf16[128,4608]{1,0:T(8,128)(2,1)}, bf16[128,4608]{1,0:T(8,128)(2,1)}, u32[]{:S(2)}, u32[]{:S(2)}) collective-permute-start(bf16[128,4608]{1,0:T(8,128)(2,1)} %get-tuple-element.10), channel_id=1, source_target_pairs={{0,1},{1,0},{2,3},{3,2},{4,5},{5,4},{6,7},{7,6},{8,9},{9,8},{10,11... | collective-permute-start | bytes 3538952 | tf_op jit(solution)/shard_map/ppermute | solution.py:28
  18.9 10.8 %collective-permute-start.11 = (bf16[128,5120]{1,0:T(8,128)(2,1)}, bf16[128,5120]{1,0:T(8,128)(2,1)}, u32[]{:S(2)}, u32[]{:S(2)}) collective-permute-start(bf16[128,5120]{1,0:T(8,128)(2,1)} %get-tuple-element.12), channel_id=1, source_target_pairs={{0,1},{1,0},{2,3},{3,2},{4,5},{5,4},{6,7},{7,6},{8,9},{9,8},{10,11... | collective-permute-start | bytes 3932168 | tf_op jit(solution)/shard_map/ppermute | solution.py:28
  24.5 21.1 %collective-permute-start.22 = (bf16[128,5120]{1,0:T(8,128)(2,1)}, bf16[128,5120]{1,0:T(8,128)(2,1)}, u32[]{:S(2)}, u32[]{:S(2)}) collective-permute-start(bf16[128,5120]{1,0:T(8,128)(2,1)} %get-tuple-element.14), channel_id=1, source_target_pairs={{0,1},{1,0},{2,3},{3,2},{4,5},{5,4},{6,7},{7,6},{8,9},{9,8},{10,11... | collective-permute-start | bytes 3932168 | tf_op jit(solution)/shard_map/ppermute | solution.py:28
  27.1 16.6 %collective-permute-start.1 = (bf16[64,4608]{1,0:T(8,128)(2,1)S(1)}, bf16[64,4608]{1,0:T(8,128)(2,1)S(1)}, u32[]{:S(2)}, u32[]{:S(2)}) collective-permute-start(bf16[64,4608]{1,0:T(8,128)(2,1)S(1)} %get-tuple-element.28), channel_id=1, source_target_pairs={{0,4},{1,5},{2,6},{3,7},{4,0},{5,1},{6,2},{7,3},{8,12},{9,13},{10,... | collective-permute-start | bytes 1769480 | tf_op jit(solution)/shard_map/ppermute | solution.py:28
  31.3 24.3 %collective-permute-start.12 = (bf16[64,5120]{1,0:T(8,128)(2,1)S(1)}, bf16[64,5120]{1,0:T(8,128)(2,1)S(1)}, u32[]{:S(2)}, u32[]{:S(2)}) collective-permute-start(bf16[64,5120]{1,0:T(8,128)(2,1)S(1)} %get-tuple-element.26), channel_id=1, source_target_pairs={{0,16},{16,0},{1,17},{17,1},{2,18},{18,2},{3,19},{19,3},{4,20},{20... | collective-permute-start | bytes 1966088 | tf_op jit(solution)/shard_map/ppermute | solution.py:28
  43.8 9.9 %collective-permute-start.2 = (bf16[32,4608]{1,0:T(8,128)(2,1)S(1)}, bf16[32,4608]{1,0:T(8,128)(2,1)S(1)}, u32[]{:S(2)}, u32[]{:S(2)}) collective-permute-start(bf16[32,4608]{1,0:T(8,128)(2,1)S(1)} %get-tuple-element.36), channel_id=1, source_target_pairs={{0,2},{1,3},{2,0},{3,1},{4,6},{5,7},{6,4},{7,5},{8,10},{9,11},{10,... | collective-permute-start | bytes 884744 | tf_op jit(solution)/shard_map/ppermute | solution.py:28
  47.3 19.5 %collective-permute-start.23 = (bf16[64,5120]{1,0:T(8,128)(2,1)S(1)}, bf16[64,5120]{1,0:T(8,128)(2,1)S(1)}, u32[]{:S(2)}, u32[]{:S(2)}) collective-permute-start(bf16[64,5120]{1,0:T(8,128)(2,1)S(1)} %get-tuple-element.24), channel_id=1, source_target_pairs={{0,2},{1,3},{2,0},{3,1},{4,6},{5,7},{6,4},{7,5},{8,10},{9,11},{10,... | collective-permute-start | bytes 1966088 | tf_op jit(solution)/shard_map/ppermute | solution.py:28
  53.9 5.2 %collective-permute-start.3 = (bf16[16,4608]{1,0:T(8,128)(2,1)S(1)}, bf16[16,4608]{1,0:T(8,128)(2,1)S(1)}, u32[]{:S(2)}, u32[]{:S(2)}) collective-permute-start(bf16[16,4608]{1,0:T(8,128)(2,1)S(1)} %get-tuple-element.42), channel_id=1, source_target_pairs={{0,16},{16,0},{1,17},{17,1},{2,18},{18,2},{3,19},{19,3},{4,20},{20... | collective-permute-start | bytes 442376 | tf_op jit(solution)/shard_map/ppermute | solution.py:28
  55.8 12.7 %copy-start.3 = (f32[16,14848]{1,0:T(8,128)S(1)}, f32[16,14848]{1,0:T(8,128)}, u32[]{:S(2)}) copy-start(f32[16,14848]{1,0:T(8,128)} %param.13) | copy-start | bytes 2850820
  55.8 12.7 %copy-start.4 = (f32[16,14848]{1,0:T(8,128)S(1)}, f32[16,14848]{1,0:T(8,128)}, u32[]{:S(2)}) copy-start(f32[16,14848]{1,0:T(8,128)} %param.12) | copy-start | bytes 2850820
  55.8 15.5 %collective-permute-start.13 = (bf16[32,5120]{1,0:T(8,128)(2,1)S(1)}, bf16[32,5120]{1,0:T(8,128)(2,1)S(1)}, u32[]{:S(2)}, u32[]{:S(2)}) collective-permute-start(bf16[32,5120]{1,0:T(8,128)(2,1)S(1)} %get-tuple-element.34), channel_id=1, source_target_pairs={{0,4},{1,5},{2,6},{3,7},{4,0},{5,1},{6,2},{7,3},{8,12},{9,13},{10,... | collective-permute-start | bytes 983048 | tf_op jit(solution)/shard_map/ppermute | solution.py:28
  59.1 9.4 %collective-permute-start.4 = (bf16[8,4608]{1,0:T(8,128)(2,1)S(1)}, bf16[8,4608]{1,0:T(8,128)(2,1)S(1)}, u32[]{:S(2)}, u32[]{:S(2)}) collective-permute-start(bf16[8,4608]{1,0:T(8,128)(2,1)S(1)} %add_convert_fusion.25), channel_id=1, source_target_pairs={{0,8},{1,9},{2,10},{3,11},{4,12},{5,13},{6,14},{7,15},{8,0},{9,1},... | collective-permute-start | bytes 221192 | tf_op jit(solution)/shard_map/ppermute | solution.py:28
  66.9 8.7 %collective-permute-start.24 = (bf16[32,5120]{1,0:T(8,128)(2,1)S(1)}, bf16[32,5120]{1,0:T(8,128)(2,1)S(1)}, u32[]{:S(2)}, u32[]{:S(2)}) collective-permute-start(bf16[32,5120]{1,0:T(8,128)(2,1)S(1)} %get-tuple-element.32), channel_id=1, source_target_pairs={{0,16},{16,0},{1,17},{17,1},{2,18},{18,2},{3,19},{19,3},{4,20},{20... | collective-permute-start | bytes 983048 | tf_op jit(solution)/shard_map/ppermute | solution.py:28
  68.6 14.9 %collective-permute-start.5 = (bf16[8,4608]{1,0:T(8,128)(2,1)S(1)}, bf16[8,4608]{1,0:T(8,128)(2,1)S(1)}, u32[]{:S(2)}, u32[]{:S(2)}) collective-permute-start(bf16[8,4608]{1,0:T(8,128)(2,1)S(1)} %get-tuple-element.21), channel_id=1, source_target_pairs={{0,8},{1,9},{2,10},{3,11},{4,12},{5,13},{6,14},{7,15},{8,0},{9,1},... | collective-permute-start | bytes 221192 | tf_op jit(solution)/shard_map/ppermute | solution.py:28
  71.4 5.8 %collective-permute-start.14 = (bf16[16,5120]{1,0:T(8,128)(2,1)S(1)}, bf16[16,5120]{1,0:T(8,128)(2,1)S(1)}, u32[]{:S(2)}, u32[]{:S(2)}) collective-permute-start(bf16[16,5120]{1,0:T(8,128)(2,1)S(1)} %get-tuple-element.40), channel_id=1, source_target_pairs={{0,2},{1,3},{2,0},{3,1},{4,6},{5,7},{6,4},{7,5},{8,10},{9,11},{10,... | collective-permute-start | bytes 491528 | tf_op jit(solution)/shard_map/ppermute | solution.py:28
  75.8 5.4 %collective-permute-start.25 = (bf16[16,5120]{1,0:T(8,128)(2,1)S(1)}, bf16[16,5120]{1,0:T(8,128)(2,1)S(1)}, u32[]{:S(2)}, u32[]{:S(2)}) collective-permute-start(bf16[16,5120]{1,0:T(8,128)(2,1)S(1)} %get-tuple-element.38), channel_id=1, source_target_pairs={{0,4},{1,5},{2,6},{3,7},{4,0},{5,1},{6,2},{7,3},{8,12},{9,13},{10,... | collective-permute-start | bytes 491528 | tf_op jit(solution)/shard_map/ppermute | solution.py:28
  77.2 8.0 %collective-permute-start.15 = (bf16[8,5120]{1,0:T(8,128)(2,1)S(1)}, bf16[8,5120]{1,0:T(8,128)(2,1)S(1)}, u32[]{:S(2)}, u32[]{:S(2)}) collective-permute-start(bf16[8,5120]{1,0:T(8,128)(2,1)S(1)} %add_convert_fusion.22), channel_id=1, source_target_pairs={{0,8},{1,9},{2,10},{3,11},{4,12},{5,13},{6,14},{7,15},{8,0},{9,1},... | collective-permute-start | bytes 245768 | tf_op jit(solution)/shard_map/ppermute | solution.py:28
  81.2 5.4 %collective-permute-start.26 = (bf16[8,5120]{1,0:T(8,128)(2,1)S(1)}, bf16[8,5120]{1,0:T(8,128)(2,1)S(1)}, u32[]{:S(2)}, u32[]{:S(2)}) collective-permute-start(bf16[8,5120]{1,0:T(8,128)(2,1)S(1)} %add_convert_fusion.19), channel_id=1, source_target_pairs={{0,8},{1,9},{2,10},{3,11},{4,12},{5,13},{6,14},{7,15},{8,0},{9,1},... | collective-permute-start | bytes 245768 | tf_op jit(solution)/shard_map/ppermute | solution.py:28
  83.6 5.7 %collective-permute-start.6 = (bf16[16,4608]{1,0:T(8,128)(2,1)S(1)}, bf16[16,4608]{1,0:T(8,128)(2,1)S(1)}, u32[]{:S(2)}, u32[]{:S(2)}) collective-permute-start(bf16[16,4608]{1,0:T(8,128)(2,1)S(1)} %pad_maximum_fusion.9), channel_id=1, source_target_pairs={{0,16},{16,0},{1,17},{17,1},{2,18},{18,2},{3,19},{19,3},{4,20},{20... | collective-permute-start | bytes 442376 | tf_op jit(solution)/shard_map/ppermute | solution.py:28
  86.8 28.8 %copy-start.5 = (bf16[8,5120]{1,0:T(8,128)(2,1)}, bf16[8,5120]{1,0:T(8,128)(2,1)S(1)}, u32[]{:S(2)}) copy-start(bf16[8,5120]{1,0:T(8,128)(2,1)S(1)} %get-tuple-element.16) | copy-start | bytes 245764
  86.9 28.8 %copy-start.6 = (bf16[8,5120]{1,0:T(8,128)(2,1)}, bf16[8,5120]{1,0:T(8,128)(2,1)S(1)}, u32[]{:S(2)}) copy-start(bf16[8,5120]{1,0:T(8,128)(2,1)S(1)} %get-tuple-element.30) | copy-start | bytes 245764
  86.9 5.5 %collective-permute-start.27 = (bf16[8,5120]{1,0:T(8,128)(2,1)S(1)}, bf16[8,5120]{1,0:T(8,128)(2,1)S(1)}, u32[]{:S(2)}, u32[]{:S(2)}) collective-permute-start(bf16[8,5120]{1,0:T(8,128)(2,1)S(1)} %get-tuple-element.15), channel_id=1, source_target_pairs={{0,8},{1,9},{2,10},{3,11},{4,12},{5,13},{6,14},{7,15},{8,0},{9,1},... | collective-permute-start | bytes 245768 | tf_op jit(solution)/shard_map/ppermute | solution.py:28
  89.3 15.8 %collective-permute-start.7 = (bf16[32,4608]{1,0:T(8,128)(2,1)S(1)}, bf16[32,4608]{1,0:T(8,128)(2,1)S(1)}, u32[]{:S(2)}, u32[]{:S(2)}) collective-permute-start(bf16[32,4608]{1,0:T(8,128)(2,1)S(1)} %pad_maximum_fusion.5), channel_id=1, source_target_pairs={{0,2},{1,3},{2,0},{3,1},{4,6},{5,7},{6,4},{7,5},{8,10},{9,11},{10,... | collective-permute-start | bytes 884744 | tf_op jit(solution)/shard_map/ppermute | solution.py:28
  90.8 5.4 %collective-permute-start.16 = (bf16[8,5120]{1,0:T(8,128)(2,1)S(1)}, bf16[8,5120]{1,0:T(8,128)(2,1)S(1)}, u32[]{:S(2)}, u32[]{:S(2)}) collective-permute-start(bf16[8,5120]{1,0:T(8,128)(2,1)S(1)} %get-tuple-element.29), channel_id=1, source_target_pairs={{0,8},{1,9},{2,10},{3,11},{4,12},{5,13},{6,14},{7,15},{8,0},{9,1},... | collective-permute-start | bytes 245768 | tf_op jit(solution)/shard_map/ppermute | solution.py:28
  92.4 6.9 %collective-permute-start.28 = (bf16[16,5120]{1,0:T(8,128)(2,1)S(1)}, bf16[16,5120]{1,0:T(8,128)(2,1)S(1)}, u32[]{:S(2)}, u32[]{:S(2)}) collective-permute-start(bf16[16,5120]{1,0:T(8,128)(2,1)S(1)} %pad_maximum_fusion.8), channel_id=1, source_target_pairs={{0,4},{1,5},{2,6},{3,7},{4,0},{5,1},{6,2},{7,3},{8,12},{9,13},{10,... | collective-permute-start | bytes 491528 | tf_op jit(solution)/shard_map/ppermute | solution.py:28
  96.2 5.4 %collective-permute-start.17 = (bf16[16,5120]{1,0:T(8,128)(2,1)S(1)}, bf16[16,5120]{1,0:T(8,128)(2,1)S(1)}, u32[]{:S(2)}, u32[]{:S(2)}) collective-permute-start(bf16[16,5120]{1,0:T(8,128)(2,1)S(1)} %pad_maximum_fusion.7), channel_id=1, source_target_pairs={{0,2},{1,3},{2,0},{3,1},{4,6},{5,7},{6,4},{7,5},{8,10},{9,11},{10,... | collective-permute-start | bytes 491528 | tf_op jit(solution)/shard_map/ppermute | solution.py:28
  99.3 7.1 %collective-permute-start.29 = (bf16[32,5120]{1,0:T(8,128)(2,1)S(1)}, bf16[32,5120]{1,0:T(8,128)(2,1)S(1)}, u32[]{:S(2)}, u32[]{:S(2)}) collective-permute-start(bf16[32,5120]{1,0:T(8,128)(2,1)S(1)} %pad_maximum_fusion.4), channel_id=1, source_target_pairs={{0,16},{16,0},{1,17},{17,1},{2,18},{18,2},{3,19},{19,3},{4,20},{20... | collective-permute-start | bytes 983048 | tf_op jit(solution)/shard_map/ppermute | solution.py:28
  101.6 12.1 %collective-permute-start.18 = (bf16[32,5120]{1,0:T(8,128)(2,1)S(1)}, bf16[32,5120]{1,0:T(8,128)(2,1)S(1)}, u32[]{:S(2)}, u32[]{:S(2)}) collective-permute-start(bf16[32,5120]{1,0:T(8,128)(2,1)S(1)} %pad_maximum_fusion.3), channel_id=1, source_target_pairs={{0,4},{1,5},{2,6},{3,7},{4,0},{5,1},{6,2},{7,3},{8,12},{9,13},{10,... | collective-permute-start | bytes 983048 | tf_op jit(solution)/shard_map/ppermute | solution.py:28
  105.2 27.3 %collective-permute-start.8 = (bf16[64,4608]{1,0:T(8,128)(2,1)S(1)}, bf16[64,4608]{1,0:T(8,128)(2,1)}, u32[]{:S(2)}, u32[]{:S(2)}) collective-permute-start(bf16[64,4608]{1,0:T(8,128)(2,1)S(1)} %pad_maximum_fusion.2.refs_0_), channel_id=1, source_target_pairs={{0,4},{1,5},{2,6},{3,7},{4,0},{5,1},{6,2},{7,3},{8,12},{9,13},{10,... | collective-permute-start | bytes 1769480 | tf_op jit(solution)/shard_map/ppermute | solution.py:28
  106.5 26.5 %collective-permute-start.30 = (bf16[64,5120]{1,0:T(8,128)(2,1)S(1)}, bf16[64,5120]{1,0:T(8,128)(2,1)S(1)}, u32[]{:S(2)}, u32[]{:S(2)}) collective-permute-start(bf16[64,5120]{1,0:T(8,128)(2,1)S(1)} %pad_maximum_fusion.1.refs_0_), channel_id=1, source_target_pairs={{0,2},{1,3},{2,0},{3,1},{4,6},{5,7},{6,4},{7,5},{8,10},{9,11},{10,... | collective-permute-start | bytes 1966088 | tf_op jit(solution)/shard_map/ppermute | solution.py:28
  109.7 23.3 %collective-permute-start.31 = (bf16[64,5120]{1,0:T(8,128)(2,1)S(1)}, bf16[64,5120]{1,0:T(8,128)(2,1)S(1)}, u32[]{:S(2)}, u32[]{:S(2)}) collective-permute-start(bf16[64,5120]{1,0:T(8,128)(2,1)S(1)} %pad_maximum_fusion.1.refs_0_), channel_id=1, source_target_pairs={{0,1},{1,0},{2,3},{3,2},{4,5},{5,4},{6,7},{7,6},{8,9},{9,8},{10,11... | collective-permute-start | bytes 1966088 | tf_op jit(solution)/shard_map/ppermute | solution.py:28
  113.8 19.7 %collective-permute-start.19 = (bf16[64,5120]{1,0:T(8,128)(2,1)S(1)}, bf16[64,5120]{1,0:T(8,128)(2,1)}, u32[]{:S(2)}, u32[]{:S(2)}) collective-permute-start(bf16[64,5120]{1,0:T(8,128)(2,1)S(1)} %pad_maximum_fusion.refs_0_), channel_id=1, source_target_pairs={{0,16},{16,0},{1,17},{17,1},{2,18},{18,2},{3,19},{19,3},{4,20},{20... | collective-permute-start | bytes 1966088 | tf_op jit(solution)/shard_map/ppermute | solution.py:28
  116.3 16.2 %collective-permute-start.33 = (bf16[8,14848]{1,0:T(8,128)(2,1)}, bf16[8,14848]{1,0:T(8,128)(2,1)}, u32[]{:S(2)}, u32[]{:S(2)}) collective-permute-start(bf16[8,14848]{1,0:T(8,128)(2,1)} %pad_maximum_fusion.6), channel_id=1, source_target_pairs={{0,16},{16,0},{1,17},{17,1},{2,18},{18,2},{3,19},{19,3},{4,20},{20... | collective-permute-start | bytes 712712 | tf_op jit(solution)/shard_map/ppermute | solution.py:28
  132.5 16.4 %collective-permute-start.9 = (bf16[64,4608]{1,0:T(8,128)(2,1)S(1)}, bf16[64,4608]{1,0:T(8,128)(2,1)S(1)}, u32[]{:S(2)}, u32[]{:S(2)}) collective-permute-start(bf16[64,4608]{1,0:T(8,128)(2,1)S(1)} %pad_maximum_fusion.2.refs_0_), channel_id=1, source_target_pairs={{0,1},{1,0},{2,3},{3,2},{4,5},{5,4},{6,7},{7,6},{8,9},{9,8},{10,11... | collective-permute-start | bytes 1769480 | tf_op jit(solution)/shard_map/ppermute | solution.py:28
  132.5 11.0 %collective-permute-start.20 = (bf16[64,5120]{1,0:T(8,128)(2,1)S(1)}, bf16[64,5120]{1,0:T(8,128)(2,1)S(1)}, u32[]{:S(2)}, u32[]{:S(2)}) collective-permute-start(bf16[64,5120]{1,0:T(8,128)(2,1)S(1)} %pad_maximum_fusion.refs_0_), channel_id=1, source_target_pairs={{0,1},{1,0},{2,3},{3,2},{4,5},{5,4},{6,7},{7,6},{8,9},{9,8},{10,11... | collective-permute-start | bytes 1966088 | tf_op jit(solution)/shard_map/ppermute | solution.py:28
  133.0 15.9 %collective-permute-start.10 = (bf16[64,4608]{1,0:T(8,128)(2,1)}, bf16[64,4608]{1,0:T(8,128)(2,1)S(1)}, u32[]{:S(2)}, u32[]{:S(2)}) collective-permute-start(bf16[64,4608]{1,0:T(8,128)(2,1)} %collective-permute-done.8.refs_1_), channel_id=1, source_target_pairs={{0,1},{1,0},{2,3},{3,2},{4,5},{5,4},{6,7},{7,6},{8,9},{9,8},{10,11... | collective-permute-start | bytes 1769480 | tf_op jit(solution)/shard_map/ppermute | solution.py:28
  133.1 5.1 %collective-permute-start.32 = (bf16[64,5120]{1,0:T(8,128)(2,1)S(1)}, bf16[64,5120]{1,0:T(8,128)(2,1)S(1)}, u32[]{:S(2)}, u32[]{:S(2)}) collective-permute-start(bf16[64,5120]{1,0:T(8,128)(2,1)S(1)} %collective-permute-done.30.refs_1_), channel_id=1, source_target_pairs={{0,1},{1,0},{2,3},{3,2},{4,5},{5,4},{6,7},{7,6},{8,9},{9,8},{10,11... | collective-permute-start | bytes 1966088 | tf_op jit(solution)/shard_map/ppermute | solution.py:28
  133.5 9.9 %collective-permute-start.21 = (bf16[64,5120]{1,0:T(8,128)(2,1)}, bf16[64,5120]{1,0:T(8,128)(2,1)S(1)}, u32[]{:S(2)}, u32[]{:S(2)}) collective-permute-start(bf16[64,5120]{1,0:T(8,128)(2,1)} %collective-permute-done.19.refs_1_), channel_id=1, source_target_pairs={{0,1},{1,0},{2,3},{3,2},{4,5},{5,4},{6,7},{7,6},{8,9},{9,8},{10,11... | collective-permute-start | bytes 1966088 | tf_op jit(solution)/shard_map/ppermute | solution.py:28
  136.9 6.6 %copy-start.2 = (bf16[256,256]{1,0:T(8,128)(2,1)S(1)}, bf16[256,256]{1,0:T(8,128)(2,1)}, u32[]{:S(2)}) copy-start(bf16[256,256]{1,0:T(8,128)(2,1)} %fusion.1.projector_ref) | copy-start | bytes 393220

commit v2 on v0

v2 whole, which is shorter than its diff:
```python
import functools

import jax
import jax.numpy as jnp
from jax import lax
from jax.experimental import pallas as pl
from jax.experimental.pallas import tpu as pltpu
from jax.sharding import PartitionSpec as P

first_decay = 0.9
second_decay = 0.999
step_count = 100.0
update_scale = 0.25
both = ("outer", "shard")
chains = ((1, 0, 1), (1, 2, 0), (1, 1, 2), (1, 0, 1))


def bits_of(count):
    return list(range(count.bit_length() - 1))


def largest_divisor(count, limit):
    return max(d for d in range(1, limit + 1) if count % d == 0)


def swap(array, bits):
    size = lax.axis_size("outer") * lax.axis_size("shard")
    return lax.ppermute(array, both, [(i, i ^ (1 << bits[i % 2])) for i in range(size)])


def axis_orders():
    shard_bits = bits_of(lax.axis_size("shard"))
    outer_bits = [len(shard_bits) + bit for bit in bits_of(lax.axis_size("outer"))]
    turning = shard_bits[1:2] + outer_bits + shard_bits[2:-1]
    return [turning[t:] + turning[:t] + shard_bits[-1:] for t in range(3)]


def prepare_kernel(
    first_block,
    block_width,
    orders,
    shards,
    leaf_rows,
    me_ref,
    owner_hbm,
    scales_hbm,
    values_ref,
    keep_ref,
    send_ref,
    placing_out_ref,
    owner_ref,
    scales_ref,
    wide_scales_ref,
    placing_ref,
    semaphores,
):
    rows, width = values_ref.shape
    step_blocks = width // block_width

    @pl.when(pl.program_id(0) == 0)
    def _():
        copies = [
            pltpu.make_async_copy(owner_hbm, owner_ref, semaphores.at[0]),
            pltpu.make_async_copy(scales_hbm, scales_ref, semaphores.at[1]),
        ]
        for copy in copies:
            copy.start()
        copies[0].wait()
        down = lax.broadcasted_iota(jnp.int32, (rows, rows), 0)
        across = lax.broadcasted_iota(jnp.int32, (rows, rows), 1)
        owner = owner_ref[...]
        owner_across = jnp.broadcast_to(owner, (rows, rows))
        earlier = (owner_across == owner_across.T) & (down < across)
        rank = jnp.sum(earlier.astype(jnp.int32), axis=0, keepdims=True)
        me = me_ref[0]
        away = ((rank // leaf_rows) * shards + owner) ^ me
        position = away & 1
        for bits in zip(*orders):
            bit = jnp.where(owner % 2 == 0, bits[0], bits[1])
            position = 2 * position + ((away >> bit) & 1)
        position = position * leaf_rows + rank % leaf_rows
        placing = (down == position).astype(jnp.bfloat16)
        placing_ref[...] = placing
        placing_out_ref[...] = placing
        copies[1].wait()
        wide_scales_ref[...] = scales_ref[...].astype(jnp.float32)

    placing = placing_ref[...]
    first = first_block + pl.program_id(0) * step_blocks
    for part in range(step_blocks):
        columns = slice(part * block_width, (part + 1) * block_width)
        scaled = placing * wide_scales_ref[pl.ds(first + part, 1), :].astype(jnp.bfloat16)
        placed = jnp.dot(
            scaled, values_ref[:, columns], preferred_element_type=jnp.float32
        ).astype(jnp.bfloat16)
        keep_ref[:, columns] = placed[: rows // 2]
        send_ref[:, columns] = placed[rows // 2 :]


def step_blocks(count):
    return largest_divisor(count, 30)


def columns_from(rows, width, first):
    return pl.BlockSpec(
        (pl.Element(rows), pl.Element(width)),
        lambda i, *_: (0, pl.multiple_of(first + i * width, 128)),
    )


def prepare(me, owner, values, scales, orders, start, count, shards, leaf_rows):
    rows = values.shape[0]
    block_width = values.shape[1] // scales.shape[0]
    step = step_blocks(count)
    width = step * block_width
    half = jax.ShapeDtypeStruct((rows // 2, count * block_width), jnp.bfloat16)
    out = pl.BlockSpec((rows // 2, width), lambda i, me: (0, i))
    return pl.pallas_call(
        functools.partial(prepare_kernel, start, block_width, orders, shards, leaf_rows),
        grid_spec=pltpu.PrefetchScalarGridSpec(
            num_scalar_prefetch=1,
            grid=(count // step,),
            in_specs=[
                pl.BlockSpec(memory_space=pltpu.HBM),
                pl.BlockSpec(memory_space=pltpu.HBM),
                columns_from(rows, width, start * block_width),
            ],
            out_specs=[out, out, pl.BlockSpec((rows, rows), lambda i, me: (0, 0))],
            scratch_shapes=[
                pltpu.VMEM(owner.shape, jnp.int32),
                pltpu.VMEM(scales.shape, scales.dtype),
                pltpu.VMEM(scales.shape, jnp.float32),
                pltpu.VMEM((rows, rows), jnp.bfloat16),
                pltpu.SemaphoreType.DMA((2,)),
            ],
        ),
        out_shape=[half, half, jax.ShapeDtypeStruct((rows, rows), jnp.bfloat16)],
        compiler_params=pltpu.CompilerParams(vmem_limit_bytes=20 * 1024 * 1024),
        cost_estimate=pl.CostEstimate(flops=1024, bytes_accessed=1024, transcendentals=0),
        name="prepare",
    )(me, owner, scales, values)


def apply_kernel(sub_width, projector_ref, placing_ref, weights_ref, *refs):
    pieces, out_ref, reordered_ref = refs[:4], refs[-2], refs[-1]

    @pl.when(pl.program_id(0) == 0)
    def _():
        reordered_ref[...] = lax.dot_general(
            projector_ref[...],
            placing_ref[...],
            (((1,), (1,)), ((), ())),
            preferred_element_type=jnp.float32,
        ).astype(jnp.bfloat16)

    for part in range(weights_ref.shape[1] // sub_width):
        columns = slice(part * sub_width, (part + 1) * sub_width)
        direction = jnp.concatenate([piece[:, columns] for piece in pieces], axis=0)
        change = jnp.dot(reordered_ref[...], direction, preferred_element_type=jnp.float32)
        out_ref[:, columns] = (
            weights_ref[:, columns].astype(jnp.float32) - update_scale * change
        ).astype(out_ref.dtype)


def apply_update(projector, placing, weights, pieces, so_far, start, count, block_width):
    rows = weights.shape[0]
    step = step_blocks(count)
    width = step * block_width
    sub_width = block_width * largest_divisor(step, 2)
    aliased = [] if so_far is None else [so_far]
    return pl.pallas_call(
        functools.partial(apply_kernel, sub_width),
        grid=(count // step,),
        in_specs=[
            pl.BlockSpec(projector.shape, lambda i: (0, 0)),
            pl.BlockSpec(placing.shape, lambda i: (0, 0)),
            columns_from(rows, width, start * block_width),
        ]
        + [pl.BlockSpec((piece.shape[0], width), lambda i: (0, i)) for piece in pieces]
        + [pl.BlockSpec(memory_space=pl.ANY) for _ in aliased],
        out_specs=columns_from(rows, width, start * block_width),
        out_shape=jax.ShapeDtypeStruct(weights.shape, weights.dtype),
        scratch_shapes=[pltpu.VMEM(projector.shape, jnp.bfloat16)],
        input_output_aliases={} if so_far is None else {3 + len(pieces): 0},
        compiler_params=pltpu.CompilerParams(vmem_limit_bytes=20 * 1024 * 1024),
        cost_estimate=pl.CostEstimate(flops=1024, bytes_accessed=1024, transcendentals=0),
        name="apply_update",
    )(projector, placing, weights, *pieces, *aliased)


def added(left, right):
    return (left.astype(jnp.float32) + right.astype(jnp.float32)).astype(jnp.bfloat16)


def normalized(owned, first, second):
    new_first = first_decay * first + (1.0 - first_decay) * owned
    new_second = second_decay * second + (1.0 - second_decay) * owned * owned
    return new_first, new_second


def per_device(
    grad_values, grad_scales, block_owner, projector, weights, first_moment, second_moment
):
    shards, outers = lax.axis_size("shard"), lax.axis_size("outer")
    outer = lax.axis_index("outer")
    rank_rows = block_owner.shape[0]
    leaf_rows = rank_rows // shards // outers
    values = grad_values[0, 0]
    scales = grad_scales[0, 0].T
    col_blocks = scales.shape[0]
    block_width = values.shape[1] // col_blocks
    me = lax.axis_index(both).astype(jnp.int32)[None]

    turns = axis_orders()
    stages = len(turns[0])
    unit = largest_divisor(col_blocks, 4)
    units = col_blocks // unit
    total = sum(share for share, _, _ in chains)
    ends = [
        unit * round(units * sum(share for share, _, _ in chains[: i + 1]) / total)
        for i in range(len(chains))
    ]
    starts = [0] + ends[:-1]
    counts = [end - start for start, end in zip(starts, ends)]
    orders = [(turns[left], turns[right]) for _, left, right in chains]
    every = range(len(chains))

    last = [me]

    def turn_of(*arrays):
        return lax.optimization_barrier((*arrays, last[0]))[:-1]

    bits = [list(zip(*order)) for order in orders]
    partial, placing, gathered, owned_parts = {}, {}, {}, {}

    def prepare_chain(i):
        (turned_owner,) = turn_of(block_owner)
        keep, send, placing[i] = prepare(
            me,
            turned_owner[None, :],
            values,
            scales,
            orders[i],
            starts[i],
            counts[i],
            shards,
            leaf_rows,
        )
        partial[i] = (keep, swap(send, (0, 0)))
        last[0] = send

    def reduce_stage(i, stage):
        mine, came = turn_of(*partial[i])
        half = mine.shape[0] // 2
        send = added(mine[half:], came[half:])
        partial[i] = (None, swap(send, bits[i][stage]))
        mine, came, _ = lax.optimization_barrier((mine, came, send))
        keep = added(mine[:half], came[:half])
        partial[i] = (keep, partial[i][1])
        last[0] = send

    def update_stage(i):
        mine, came = turn_of(*partial[i])
        owned_parts[i] = added(mine, came)
        own = (outer * leaf_rows, starts[i] * block_width)
        shape = (leaf_rows, counts[i] * block_width)
        new_first, new_second = normalized(
            owned_parts[i].astype(jnp.float32),
            lax.dynamic_slice(first_moment, own, shape),
            lax.dynamic_slice(second_moment, own, shape),
        )
        corrected = new_first / (1.0 - first_decay**step_count)
        spread = jnp.sqrt(new_second / (1.0 - second_decay**step_count)) + 1e-08
        update = (corrected / spread).astype(jnp.bfloat16)
        gathered[i] = (update, swap(update, bits[i][-1]))
        last[0] = update

    def gather_stage(i, stage):
        mine = jnp.concatenate(turn_of(*gathered[i]), axis=0)
        gathered[i] = (mine, swap(mine, bits[i][stage]))
        last[0] = mine

    def owned_by_shard():
        owned = jnp.concatenate([owned_parts[i] for i in every], axis=1)
        for bit in bits_of(outers):
            other = swap(owned, (len(bits_of(shards)) + bit,) * 2)
            low = ((outer >> bit) & 1) == 0
            owned = jnp.where(
                low,
                jnp.concatenate([owned, other], axis=0),
                jnp.concatenate([other, owned], axis=0),
            )
        return owned

    def moments(owned):
        (owned,) = turn_of(owned)
        moved = normalized(owned.astype(jnp.float32), first_moment, second_moment)
        last[0] = moved[0]
        return moved

    for i in every:
        prepare_chain(i)
    for stage in range(stages):
        for i in every:
            reduce_stage(i, stage)
    for i in every:
        update_stage(i)
    owned = owned_by_shard()
    for stage in reversed(range(stages - 1)):
        if stage == 0:
            new_first, new_second = moments(owned)
        for i in every:
            gather_stage(i, stage)
    new_weights = None
    forwarded = {}
    for i in every:
        mine, came = gathered[i]
        beside = swap(mine, (0, 0))
        (came,) = turn_of(came)
        forwarded[i] = (mine, came, beside, swap(came, (0, 0)))
        last[0] = came
    for i in every:
        new_weights = apply_update(
            projector,
            placing[i],
            weights,
            turn_of(*forwarded[i]),
            new_weights,
            starts[i],
            counts[i],
            block_width,
        )
        last[0] = new_weights
    return (new_weights, new_first, new_second)


def solution(mesh):
    placed = (
        P("outer", "shard", None, None),
        P("outer", "shard", None, None),
        P(),
        P(("outer", "shard"), None),
        P(("outer", "shard"), None),
        P("shard", None),
        P("shard", None),
    )
    return jax.shard_map(
        per_device,
        mesh=mesh,
        in_specs=placed,
        out_specs=(P(("outer", "shard"), None), P("shard", None), P("shard", None)),
        check_vma=False,
    )
```

time: 258 us -> 112 us (0.43)
  waiting for transfers between devices: 168 us -> 24.3 us
  starting transfers between devices: 0.08 us -> 49.9 us
  local copies, waits for them, and re-layouts: 27.6 us -> 4.95 us
  matrix products: 19.9 us -> 0 us
  Pallas kernels: 0 us -> 18.9 us
  blocking collectives: 13 us -> 0 us
  between operations: 14.1 us -> 1.12 us
    reduce_scatter x1 -> x0, waiting for transfers between devices: 98.2 us -> none  [per_device(): lax.psum_scatter(partial_terms.astype(jnp.bfloat16), 'shard', scatter_dim...]
    all_gather x1 -> x0, waiting for transfers between devices: 70.2 us -> none  [per_device(): gathered = lax.all_gather(update, 'shard', axis=0, tiled=True)]
    ppermute x0 -> x45, starting transfers between devices: none -> 49.9 us  [swap(): lax.ppermute(array, both, [(i, i ^ 1 << bits[i % 2]) for i in range(size)])]
    convert_element_type x3 -> x0, local copies, waits for them, and re-layouts: 27.6 us -> none  [the longest x1 15.6 us: per_device(): sent_values.reshape(rank_rows, col_blocks, block_width).astype(jnp.float32)]
    ppermute x0 -> x45, waiting for transfers between devices: none -> 24.3 us  [swap(): lax.ppermute(array, both, [(i, i ^ 1 << bits[i % 2]) for i in range(size)])]
    dot_general x3 -> x0, matrix products: 19.9 us -> none  [the longest x1 10.7 us: per_device(): jnp.dot(placing, values, preferred_element_type=jnp.float32)]
    pallas_call x0 -> x8, Pallas kernels: none -> 18.9 us  [the longest x4 10.2 us: prepare(): pl.pallas_call(functools.partial(prepare_kernel, start, block_width, orde...]
    all_gather x1 -> x0, blocking collectives: 13 us -> none  [per_device(): all_rows = lax.all_gather(pod_low[None], 'outer', axis=0, tiled=True)]
  transfers between devices with their start and end apart: 2 -> 45, of which waited for: 2 -> 15; matrix products, arithmetic and copies ran while one was open for 0% -> 11% of each run, Pallas kernels for 0% -> 13%
where the time goes in v2:
time: 112 us; the launch traced here: 111 us
  starting transfers between devices  49.9 us (45%)
  waiting for transfers between devices  24.3 us (22%)
  Pallas kernels  18.9 us (17%)
  other arithmetic  11.6 us (10%)
  local copies, waits for them, and re-layouts  4.95 us (4%)
  between operations  1.12 us (1%)
    ppermute x45, starting transfers between devices, swap(): lax.ppermute(array, both, [(i, i ^ 1 << bits[i % 2]) for i in range(size)])  49.9 us
    ppermute x45, waiting for transfers between devices, swap(): lax.ppermute(array, both, [(i, i ^ 1 << bits[i % 2]) for i in range(size)])  24.3 us
    pallas_call x4, Pallas kernels, prepare(): pl.pallas_call(functools.partial(prepare_kernel, start, block_width, orde...  10.2 us
    convert_element_type x31, other arithmetic, added(): (left.astype(jnp.float32) + right.astype(jnp.float32)).astype(jnp.bfloat16)  9.5 us
    pallas_call x4, Pallas kernels, apply_update(): pl.pallas_call(functools.partial(apply_kernel, sub_width), grid=(count //...  8.7 us
    unnamed x30, local copies, waits for them, and re-layouts  4.81 us
  transfers between devices with their start and end apart: 45, of which 15 were waited for; matrix products, arithmetic and copies ran while one was open for 11% of the time, Pallas kernels for 13%

profile of v2, /device:TPU:0, one launch (start us, length us, event | category | flops | bytes accessed | tf_op | source)
XLA Modules:
  0.0 110.7 jit_solution(1215831993084241021)
XLA Ops:
  0.6 3.1 %copy-done = bf16[1,1,256,14848]{3,2,1,0:T(8,128)(2,1)S(1)} copy-done((bf16[1,1,256,14848]{3,2,1,0:T(8,128)(2,1)S(1)}, bf16[1,1,256,14848]{3,2,1,0:T(8,128)(2,1)}, u32[]{:S(2)}) %copy-start) | copy-done | bytes 7602200
  5.3 2.4 %prepare.4 = (bf16[128,3584]{1,0:T(8,128)(2,1)S(1)}, bf16[128,3584]{1,0:T(8,128)(2,1)}, bf16[256,256]{1,0:T(8,128)(2,1)S(1)}) custom-call(s32[1]{0:T(128)} %bitcast.me_ref, s32[1,256]{1,0:T(1,128)S(1)} %bitcast.19, bf16[116,256]{1,0:T(8,128)(2,1)S(1)} %bitcast.15, bf16[256,14848]{1,0:T(8,128)(2,1)S(1)} %bitcast.9), custom_call_target="tpu_custom_call" | custom-call | flops 1024 | bytes 1024 | tf_op jit(solution)/shard_map/prepare/pallas_call | solution.py:118
  8.2 2.4 %prepare.5 = (bf16[128,3584]{1,0:T(8,128)(2,1)S(1)}, bf16[128,3584]{1,0:T(8,128)(2,1)}, bf16[256,256]{1,0:T(8,128)(2,1)S(1)}) custom-call(s32[1]{0:T(128)} %bitcast.me_ref, s32[1,256]{1,0:T(1,128)S(1)} %bitcast.20, bf16[116,256]{1,0:T(8,128)(2,1)S(1)} %bitcast.16, bf16[256,14848]{1,0:T(8,128)(2,1)S(1)} %bitcast.10), custom_call_target="tpu_custom_call" | custom-call | flops 1024 | bytes 1024 | tf_op jit(solution)/shard_map/prepare/pallas_call | solution.py:118
  10.8 2.7 %prepare.6 = (bf16[128,4096]{1,0:T(8,128)(2,1)S(1)}, bf16[128,4096]{1,0:T(8,128)(2,1)}, bf16[256,256]{1,0:T(8,128)(2,1)S(1)}) custom-call(s32[1]{0:T(128)} %bitcast.me_ref, s32[1,256]{1,0:T(1,128)S(1)} %bitcast.21, bf16[116,256]{1,0:T(8,128)(2,1)S(1)} %bitcast.17, bf16[256,14848]{1,0:T(8,128)(2,1)S(1)} %bitcast.11), custom_call_target="tpu_custom_call" | custom-call | flops 1024 | bytes 1024 | tf_op jit(solution)/shard_map/prepare/pallas_call | solution.py:118
  14.1 2.6 %prepare.7 = (bf16[128,3584]{1,0:T(8,128)(2,1)S(1)}, bf16[128,3584]{1,0:T(8,128)(2,1)}, bf16[256,256]{1,0:T(8,128)(2,1)S(1)}) custom-call(s32[1]{0:T(128)} %bitcast.me_ref, s32[1,256]{1,0:T(1,128)S(1)} %bitcast.22, bf16[116,256]{1,0:T(8,128)(2,1)S(1)} %bitcast.18, bf16[256,14848]{1,0:T(8,128)(2,1)S(1)} %bitcast.12), custom_call_target="tpu_custom_call" | custom-call | flops 1024 | bytes 1024 | tf_op jit(solution)/shard_map/prepare/pallas_call | solution.py:118
  16.8 1.1 %add_convert_fusion.7 = bf16[64,3584]{1,0:T(8,128)(2,1)S(1)} fusion(bf16[128,3584]{1,0:T(8,128)(2,1)} %collective-permute-done.3, bf16[128,3584]{1,0:T(8,128)(2,1)S(1)} %get-tuple-element.163), kind=kLoop, calls=%fused_computation.11 | loop fusion | flops 917504 | bytes 1376256 | tf_op jit(solution)/shard_map/convert_element_type | solution.py:192
  17.9 3.0 %collective-permute-start.7 = (bf16[64,3584]{1,0:T(8,128)(2,1)S(1)}, bf16[64,3584]{1,0:T(8,128)(2,1)S(1)}, u32[]{:S(2)}, u32[]{:S(2)}) collective-permute-start(bf16[64,3584]{1,0:T(8,128)(2,1)S(1)} %add_convert_fusion.7), channel_id=1, source_target_pairs={{0,2},{1,17},{2,0},{3,19},{4,6},{5,21},{6,4},{7,23},{8,10},{9,25},... | collective-permute-start | bytes 1376264 | tf_op jit(solution)/shard_map/ppermute | solution.py:28
  21.0 1.3 %add_convert_fusion.6 = bf16[64,3584]{1,0:T(8,128)(2,1)S(1)} fusion(bf16[128,3584]{1,0:T(8,128)(2,1)} %collective-permute-done.2, bf16[128,3584]{1,0:T(8,128)(2,1)} %copy-done.3), kind=kLoop, calls=%fused_computation.10 | loop fusion | flops 917504 | bytes 1376256 | tf_op jit(solution)/shard_map/convert_element_type | solution.py:192
  22.2 1.6 %collective-permute-start.6 = (bf16[64,3584]{1,0:T(8,128)(2,1)S(1)}, bf16[64,3584]{1,0:T(8,128)(2,1)S(1)}, u32[]{:S(2)}, u32[]{:S(2)}) collective-permute-start(bf16[64,3584]{1,0:T(8,128)(2,1)S(1)} %add_convert_fusion.6), channel_id=1, source_target_pairs={{0,4},{1,3},{2,6},{3,1},{4,0},{5,7},{6,2},{7,5},{8,12},{9,11},{10,... | collective-permute-start | bytes 1376264 | tf_op jit(solution)/shard_map/ppermute | solution.py:28
  23.9 1.3 %add_convert_fusion.3 = bf16[64,3584]{1,0:T(8,128)(2,1)S(1)} fusion(bf16[128,3584]{1,0:T(8,128)(2,1)} %collective-permute-done.2, bf16[128,3584]{1,0:T(8,128)(2,1)} %copy-done.3), kind=kLoop, calls=%fused_computation.7 | loop fusion | flops 917504 | bytes 1376256 | tf_op jit(solution)/shard_map/convert_element_type | solution.py:192
  25.1 1.2 %add_convert_fusion.1 = bf16[64,4096]{1,0:T(8,128)(2,1)S(1)} fusion(bf16[128,4096]{1,0:T(8,128)(2,1)} %collective-permute-done.1, bf16[128,4096]{1,0:T(8,128)(2,1)S(1)} %get-tuple-element.159), kind=kLoop, calls=%fused_computation.3 | loop fusion | flops 1048576 | bytes 1572864 | tf_op jit(solution)/shard_map/convert_element_type | solution.py:192
  26.3 1.6 %collective-permute-start.5 = (bf16[64,4096]{1,0:T(8,128)(2,1)S(1)}, bf16[64,4096]{1,0:T(8,128)(2,1)S(1)}, u32[]{:S(2)}, u32[]{:S(2)}) collective-permute-start(bf16[64,4096]{1,0:T(8,128)(2,1)S(1)} %add_convert_fusion.1), channel_id=1, source_target_pairs={{0,16},{1,5},{2,18},{3,7},{4,20},{5,1},{6,22},{7,3},{8,24},{9,13},... | collective-permute-start | bytes 1572872 | tf_op jit(solution)/shard_map/ppermute | solution.py:28
  27.9 1.5 %add_convert_fusion.2 = (bf16[64,3584]{1,0:T(8,128)(2,1)S(1)}, bf16[64,3584]{1,0:T(8,128)(2,1)S(1)}) fusion(bf16[128,3584]{1,0:T(8,128)(2,1)} %collective-permute-done.3, bf16[128,3584]{1,0:T(8,128)(2,1)S(1)} %get-tuple-element.163, bf16[128,3584]{1,0:T(8,128)(2,1)} %collective-permute-done, bf16[128,3584]{1,0:T(8,128)(2,1)S(1)} %get-tuple-element.157), kind=kLoop, calls=%fused_computation.6 | loop fusion | flops 1835008 | bytes 2752512 | tf_op jit(solution)/shard_map/convert_element_type | solution.py:192
  30.0 1.2 %add_convert_fusion = bf16[64,4096]{1,0:T(8,128)(2,1)S(1)} fusion(bf16[128,4096]{1,0:T(8,128)(2,1)} %collective-permute-done.1, bf16[128,4096]{1,0:T(8,128)(2,1)S(1)} %get-tuple-element.159), kind=kLoop, calls=%fused_computation.2 | loop fusion | flops 1048576 | bytes 1572864 | tf_op jit(solution)/shard_map/convert_element_type | solution.py:192
  31.2 1.1 %add_convert_fusion.4 = bf16[64,3584]{1,0:T(8,128)(2,1)S(1)} fusion(bf16[128,3584]{1,0:T(8,128)(2,1)} %collective-permute-done, bf16[128,3584]{1,0:T(8,128)(2,1)S(1)} %get-tuple-element.157), kind=kLoop, calls=%fused_computation.8 | loop fusion | flops 917504 | bytes 1376256 | tf_op jit(solution)/shard_map/convert_element_type | solution.py:192
  32.4 1.8 %collective-permute-start.11 = (bf16[32,3584]{1,0:T(8,128)(2,1)S(1)}, bf16[32,3584]{1,0:T(8,128)(2,1)S(1)}, u32[]{:S(2)}, u32[]{:S(2)}) collective-permute-start(bf16[32,3584]{1,0:T(8,128)(2,1)S(1)} %add_convert_fusion.15), channel_id=1, source_target_pairs={{0,16},{1,5},{2,18},{3,7},{4,20},{5,1},{6,22},{7,3},{8,24},{9,13},... | collective-permute-start | bytes 688136 | tf_op jit(solution)/shard_map/ppermute | solution.py:28
  34.2 1.3 %collective-permute-start.10 = (bf16[32,3584]{1,0:T(8,128)(2,1)S(1)}, bf16[32,3584]{1,0:T(8,128)(2,1)S(1)}, u32[]{:S(2)}, u32[]{:S(2)}) collective-permute-start(bf16[32,3584]{1,0:T(8,128)(2,1)S(1)} %add_convert_fusion.14), channel_id=1, source_target_pairs={{0,2},{1,17},{2,0},{3,19},{4,6},{5,21},{6,4},{7,23},{8,10},{9,25},... | collective-permute-start | bytes 688136 | tf_op jit(solution)/shard_map/ppermute | solution.py:28
  35.7 4.2 %collective-permute-done.5 = bf16[64,4096]{1,0:T(8,128)(2,1)S(1)} collective-permute-done((bf16[64,4096]{1,0:T(8,128)(2,1)S(1)}, bf16[64,4096]{1,0:T(8,128)(2,1)S(1)}, u32[]{:S(2)}, u32[]{:S(2)}) %collective-permute-start.5) | collective-permute-done | bytes 524320 | tf_op jit(solution)/shard_map/ppermute | solution.py:28
  40.6 2.5 %collective-permute-start.8 = (bf16[32,3584]{1,0:T(8,128)(2,1)S(1)}, bf16[32,3584]{1,0:T(8,128)(2,1)S(1)}, u32[]{:S(2)}, u32[]{:S(2)}) collective-permute-start(bf16[32,3584]{1,0:T(8,128)(2,1)S(1)} %add_convert_fusion.13), channel_id=1, source_target_pairs={{0,16},{1,5},{2,18},{3,7},{4,20},{5,1},{6,22},{7,3},{8,24},{9,13},... | collective-permute-start | bytes 688136 | tf_op jit(solution)/shard_map/ppermute | solution.py:28
  43.2 1.5 %collective-permute-done.11 = bf16[32,3584]{1,0:T(8,128)(2,1)S(1)} collective-permute-done((bf16[32,3584]{1,0:T(8,128)(2,1)S(1)}, bf16[32,3584]{1,0:T(8,128)(2,1)S(1)}, u32[]{:S(2)}, u32[]{:S(2)}) %collective-permute-start.11) | collective-permute-done | bytes 229408 | tf_op jit(solution)/shard_map/ppermute | solution.py:28
  45.3 2.3 %collective-permute-start.14 = (bf16[16,3584]{1,0:T(8,128)(2,1)S(1)}, bf16[16,3584]{1,0:T(8,128)(2,1)S(1)}, u32[]{:S(2)}, u32[]{:S(2)}) collective-permute-start(bf16[16,3584]{1,0:T(8,128)(2,1)S(1)} %add_convert_fusion.22), channel_id=1, source_target_pairs={{0,16},{1,5},{2,18},{3,7},{4,20},{5,1},{6,22},{7,3},{8,24},{9,13},... | collective-permute-start | bytes 344072 | tf_op jit(solution)/shard_map/ppermute | solution.py:28
  47.6 1.2 %collective-permute-done.9 = bf16[32,4096]{1,0:T(8,128)(2,1)S(1)} collective-permute-done((bf16[32,4096]{1,0:T(8,128)(2,1)S(1)}, bf16[32,4096]{1,0:T(8,128)(2,1)S(1)}, u32[]{:S(2)}, u32[]{:S(2)}) %collective-permute-start.9) | collective-permute-done | bytes 262176 | tf_op jit(solution)/shard_map/ppermute | solution.py:28
  51.3 2.7 %collective-permute-start.19 = (bf16[8,3584]{1,0:T(8,128)(2,1)S(1)}, bf16[8,3584]{1,0:T(8,128)(2,1)S(1)}, u32[]{:S(2)}, u32[]{:S(2)}) collective-permute-start(bf16[8,3584]{1,0:T(8,128)(2,1)S(1)} %add_convert_fusion.35), channel_id=1, source_target_pairs={{0,8},{1,9},{2,10},{3,11},{4,12},{5,13},{6,14},{7,15},{8,0},{9,1},... | collective-permute-start | bytes 172040 | tf_op jit(solution)/shard_map/ppermute | solution.py:28
  54.5 2.7 %collective-permute-start.17 = (bf16[8,4096]{1,0:T(8,128)(2,1)S(1)}, bf16[8,4096]{1,0:T(8,128)(2,1)S(1)}, u32[]{:S(2)}, u32[]{:S(2)}) collective-permute-start(bf16[8,4096]{1,0:T(8,128)(2,1)S(1)} %add_convert_fusion.26), channel_id=1, source_target_pairs={{0,8},{1,9},{2,10},{3,11},{4,12},{5,13},{6,14},{7,15},{8,0},{9,1},... | collective-permute-start | bytes 196616 | tf_op jit(solution)/shard_map/ppermute | solution.py:28
  57.8 2.6 %collective-permute-start.23 = (bf16[8,3584]{1,0:T(8,128)(2,1)S(1)}, bf16[8,3584]{1,0:T(8,128)(2,1)S(1)}, u32[]{:S(2)}, u32[]{:S(2)}) collective-permute-start(bf16[8,3584]{1,0:T(8,128)(2,1)S(1)} %get-tuple-element.221), channel_id=1, source_target_pairs={{0,8},{1,9},{2,10},{3,11},{4,12},{5,13},{6,14},{7,15},{8,0},{9,1},... | collective-permute-start | bytes 172040 | tf_op jit(solution)/shard_map/ppermute | solution.py:28
  60.4 3.0 %collective-permute-done.18 = bf16[8,3584]{1,0:T(8,128)(2,1)S(1)} collective-permute-done((bf16[8,3584]{1,0:T(8,128)(2,1)S(1)}, bf16[8,3584]{1,0:T(8,128)(2,1)S(1)}, u32[]{:S(2)}, u32[]{:S(2)}) %collective-permute-start.18) | collective-permute-done | bytes 57376 | tf_op jit(solution)/shard_map/ppermute | solution.py:28
  63.7 1.2 %collective-permute-done.17 = bf16[8,4096]{1,0:T(8,128)(2,1)S(1)} collective-permute-done((bf16[8,4096]{1,0:T(8,128)(2,1)S(1)}, bf16[8,4096]{1,0:T(8,128)(2,1)S(1)}, u32[]{:S(2)}, u32[]{:S(2)}) %collective-permute-start.17) | collective-permute-done | bytes 65568 | tf_op jit(solution)/shard_map/ppermute | solution.py:28
  65.0 1.8 %collective-permute-start.21 = (bf16[8,4096]{1,0:T(8,128)(2,1)S(1)}, bf16[8,4096]{1,0:T(8,128)(2,1)S(1)}, u32[]{:S(2)}, u32[]{:S(2)}) collective-permute-start(bf16[8,4096]{1,0:T(8,128)(2,1)S(1)} %get-tuple-element.225), channel_id=1, source_target_pairs={{0,8},{1,9},{2,10},{3,11},{4,12},{5,13},{6,14},{7,15},{8,0},{9,1},... | collective-permute-start | bytes 196616 | tf_op jit(solution)/shard_map/ppermute | solution.py:28
  66.9 1.4 %collective-permute-start.32 = (bf16[8,14848]{1,0:T(8,128)(2,1)S(1)}, bf16[8,14848]{1,0:T(8,128)(2,1)S(1)}, u32[]{:S(2)}, u32[]{:S(2)}) collective-permute-start(bf16[8,14848]{1,0:T(8,128)(2,1)S(1)} %pad_maximum_fusion), channel_id=1, source_target_pairs={{0,16},{1,17},{2,18},{3,19},{4,20},{5,21},{6,22},{7,23},{8,24},{9,... | collective-permute-start | bytes 712712 | tf_op jit(solution)/shard_map/ppermute | solution.py:28
  68.3 1.9 %collective-permute-start.20 = (bf16[8,3584]{1,0:T(8,128)(2,1)S(1)}, bf16[8,3584]{1,0:T(8,128)(2,1)S(1)}, u32[]{:S(2)}, u32[]{:S(2)}) collective-permute-start(bf16[8,3584]{1,0:T(8,128)(2,1)S(1)} %get-tuple-element.227), channel_id=1, source_target_pairs={{0,8},{1,9},{2,10},{3,11},{4,12},{5,13},{6,14},{7,15},{8,0},{9,1},... | collective-permute-start | bytes 172040 | tf_op jit(solution)/shard_map/ppermute | solution.py:28
  70.2 1.5 %collective-permute-start.27 = (bf16[16,3584]{1,0:T(8,128)(2,1)S(1)}, bf16[16,3584]{1,0:T(8,128)(2,1)S(1)}, u32[]{:S(2)}, u32[]{:S(2)}) collective-permute-start(bf16[16,3584]{1,0:T(8,128)(2,1)S(1)} %constant_dynamic-update-slice_fusion), channel_id=1, source_target_pairs={{0,4},{1,3},{2,6},{3,1},{4,0},{5,7},{6,2},{7,5},{8,12},{9,11},{10,... | collective-permute-start | bytes 344072 | tf_op jit(solution)/shard_map/ppermute | solution.py:28
  71.8 2.0 %collective-permute-start.26 = (bf16[16,3584]{1,0:T(8,128)(2,1)S(1)}, bf16[16,3584]{1,0:T(8,128)(2,1)S(1)}, u32[]{:S(2)}, u32[]{:S(2)}) collective-permute-start(bf16[16,3584]{1,0:T(8,128)(2,1)S(1)} %constant_dynamic-update-slice_fusion.2), channel_id=1, source_target_pairs={{0,16},{1,5},{2,18},{3,7},{4,20},{5,1},{6,22},{7,3},{8,24},{9,13},... | collective-permute-start | bytes 344072 | tf_op jit(solution)/shard_map/ppermute | solution.py:28
  73.8 1.1 %collective-permute-start.25 = (bf16[16,4096]{1,0:T(8,128)(2,1)S(1)}, bf16[16,4096]{1,0:T(8,128)(2,1)S(1)}, u32[]{:S(2)}, u32[]{:S(2)}) collective-permute-start(bf16[16,4096]{1,0:T(8,128)(2,1)S(1)} %constant_dynamic-update-slice_fusion.4), channel_id=1, source_target_pairs={{0,2},{1,17},{2,0},{3,19},{4,6},{5,21},{6,4},{7,23},{8,10},{9,25},... | collective-permute-start | bytes 393224 | tf_op jit(solution)/shard_map/ppermute | solution.py:28
  75.5 1.8 %collective-permute-start.31 = (bf16[32,3584]{1,0:T(8,128)(2,1)S(1)}, bf16[32,3584]{1,0:T(8,128)(2,1)S(1)}, u32[]{:S(2)}, u32[]{:S(2)}) collective-permute-start(bf16[32,3584]{1,0:T(8,128)(2,1)S(1)} %constant_dynamic-update-slice_fusion.8), channel_id=1, source_target_pairs={{0,16},{1,5},{2,18},{3,7},{4,20},{5,1},{6,22},{7,3},{8,24},{9,13},... | collective-permute-start | bytes 688136 | tf_op jit(solution)/shard_map/ppermute | solution.py:28
  77.3 1.2 %collective-permute-start.30 = (bf16[32,3584]{1,0:T(8,128)(2,1)S(1)}, bf16[32,3584]{1,0:T(8,128)(2,1)S(1)}, u32[]{:S(2)}, u32[]{:S(2)}) collective-permute-start(bf16[32,3584]{1,0:T(8,128)(2,1)S(1)} %constant_dynamic-update-slice_fusion.10), channel_id=1, source_target_pairs={{0,2},{1,17},{2,0},{3,19},{4,6},{5,21},{6,4},{7,23},{8,10},{9,25},... | collective-permute-start | bytes 688136 | tf_op jit(solution)/shard_map/ppermute | solution.py:28
  78.5 1.2 %collective-permute-done.25 = bf16[16,4096]{1,0:T(8,128)(2,1)S(1)} collective-permute-done((bf16[16,4096]{1,0:T(8,128)(2,1)S(1)}, bf16[16,4096]{1,0:T(8,128)(2,1)S(1)}, u32[]{:S(2)}, u32[]{:S(2)}) %collective-permute-start.25) | collective-permute-done | bytes 131104 | tf_op jit(solution)/shard_map/ppermute | solution.py:28
  79.7 1.4 %collective-permute-start.29 = (bf16[32,4096]{1,0:T(8,128)(2,1)S(1)}, bf16[32,4096]{1,0:T(8,128)(2,1)S(1)}, u32[]{:S(2)}, u32[]{:S(2)}) collective-permute-start(bf16[32,4096]{1,0:T(8,128)(2,1)S(1)} %constant_dynamic-update-slice_fusion.12), channel_id=1, source_target_pairs={{0,4},{1,3},{2,6},{3,1},{4,0},{5,7},{6,2},{7,5},{8,12},{9,11},{10,... | collective-permute-start | bytes 786440 | tf_op jit(solution)/shard_map/ppermute | solution.py:28
  81.4 1.5 %fusion.1 = (f32[16,14848]{1,0:T(8,128)}, f32[16,14848]{1,0:T(8,128)}) fusion(bf16[16,14848]{1,0:T(8,128)(2,1)S(1)} %maximum_select_fusion, f32[16,14848]{1,0:T(8,128)S(1)} %copy-done.5, f32[16,14848]{1,0:T(8,128)S(1)} %copy-done.6), kind=kLoop, calls=%fused_computation.5 | loop fusion | flops 1900544 | bytes 4276224 | tf_op jit(solution)/shard_map/add | solution.py:197
  83.0 1.2 %collective-permute-start.36 = (bf16[64,3584]{1,0:T(8,128)(2,1)S(1)}, bf16[64,3584]{1,0:T(8,128)(2,1)S(1)}, u32[]{:S(2)}, u32[]{:S(2)}) collective-permute-start(bf16[64,3584]{1,0:T(8,128)(2,1)S(1)} %constant_dynamic-update-slice_fusion.16.refs_0_), channel_id=1, source_target_pairs={{0,2},{1,17},{2,0},{3,19},{4,6},{5,21},{6,4},{7,23},{8,10},{9,25},... | collective-permute-start | bytes 1376264 | tf_op jit(solution)/shard_map/ppermute | solution.py:28
  84.2 1.9 %collective-permute-start.35 = (bf16[64,3584]{1,0:T(8,128)(2,1)S(1)}, bf16[64,3584]{1,0:T(8,128)(2,1)S(1)}, u32[]{:S(2)}, u32[]{:S(2)}) collective-permute-start(bf16[64,3584]{1,0:T(8,128)(2,1)S(1)} %constant_dynamic-update-slice_fusion.18.refs_0_), channel_id=1, source_target_pairs={{0,4},{1,3},{2,6},{3,1},{4,0},{5,7},{6,2},{7,5},{8,12},{9,11},{10,... | collective-permute-start | bytes 1376264 | tf_op jit(solution)/shard_map/ppermute | solution.py:28
  86.2 2.5 %collective-permute-start.34 = (bf16[64,4096]{1,0:T(8,128)(2,1)S(1)}, bf16[64,4096]{1,0:T(8,128)(2,1)S(1)}, u32[]{:S(2)}, u32[]{:S(2)}) collective-permute-start(bf16[64,4096]{1,0:T(8,128)(2,1)S(1)} %constant_dynamic-update-slice_fusion.20.refs_0_), channel_id=1, source_target_pairs={{0,16},{1,5},{2,18},{3,7},{4,20},{5,1},{6,22},{7,3},{8,24},{9,13},... | collective-permute-start | bytes 1572872 | tf_op jit(solution)/shard_map/ppermute | solution.py:28
  90.7 5.0 %collective-permute-done.36.refs_1_ = bf16[64,3584]{1,0:T(8,128)(2,1)S(1)} collective-permute-done((bf16[64,3584]{1,0:T(8,128)(2,1)S(1)}, bf16[64,3584]{1,0:T(8,128)(2,1)S(1)}, u32[]{:S(2)}, u32[]{:S(2)}) %collective-permute-start.36) | collective-permute-done | bytes 458784 | tf_op jit(solution)/shard_map/ppermute | solution.py:28
  95.7 1.1 collective-permute-done.35.refs_1_
  97.2 3.5 %collective-permute-done.34.refs_1_ = bf16[64,4096]{1,0:T(8,128)(2,1)S(1)} collective-permute-done((bf16[64,4096]{1,0:T(8,128)(2,1)S(1)}, bf16[64,4096]{1,0:T(8,128)(2,1)S(1)}, u32[]{:S(2)}, u32[]{:S(2)}) %collective-permute-start.34) | collective-permute-done | bytes 524320 | tf_op jit(solution)/shard_map/ppermute | solution.py:28
  101.9 2.1 %apply_update.4.refs_4_ = bf16[256,14848]{1,0:T(8,128)(2,1)} custom-call(bf16[256,256]{1,0:T(8,128)(2,1)S(1)} %copy-done.1, bf16[256,256]{1,0:T(8,128)(2,1)S(1)} %get-tuple-element.252.placing_ref, bf16[256,14848]{1,0:T(8,128)(2,1)S(1)} %bitcast.14, bf16[64,3584]{1,0:T(8,128)(2,1)S(1)} %constant_dynamic-update-slice_fusion.16.refs_0_, ...), custom_call_target="tpu_custom_call" | custom-call | flops 1024 | bytes 1024 | tf_op jit(solution)/shard_map/apply_update/pallas_call | solution.py:171
  104.0 2.1 %apply_update.5.refs_4_ = bf16[256,14848]{1,0:T(8,128)(2,1)} custom-call(bf16[256,256]{1,0:T(8,128)(2,1)S(1)} %copy-done.1, bf16[256,256]{1,0:T(8,128)(2,1)S(1)} %get-tuple-element.251.placing_ref, bf16[256,14848]{1,0:T(8,128)(2,1)S(1)} %bitcast.14, ...), custom_call_target="tpu_custom_call", output_to_operand_aliasing={{}: (7, {})} | custom-call | flops 1024 | bytes 1024 | tf_op jit(solution)/shard_map/apply_update/pallas_call | solution.py:171
  106.1 2.4 %apply_update.6.refs_4_ = bf16[256,14848]{1,0:T(8,128)(2,1)} custom-call(bf16[256,256]{1,0:T(8,128)(2,1)S(1)} %copy-done.1, bf16[256,256]{1,0:T(8,128)(2,1)S(1)} %get-tuple-element.250.placing_ref, bf16[256,14848]{1,0:T(8,128)(2,1)S(1)} %bitcast.14, ...), custom_call_target="tpu_custom_call", output_to_operand_aliasing={{}: (7, {})} | custom-call | flops 1024 | bytes 1024 | tf_op jit(solution)/shard_map/apply_update/pallas_call | solution.py:171
  108.6 2.1 %apply_update.7 = bf16[256,14848]{1,0:T(8,128)(2,1)} custom-call(bf16[256,256]{1,0:T(8,128)(2,1)S(1)} %copy-done.1, bf16[256,256]{1,0:T(8,128)(2,1)S(1)} %get-tuple-element.143.placing_ref, bf16[256,14848]{1,0:T(8,128)(2,1)S(1)} %bitcast.14, bf16[64,3584]{1,0:T(8,128)(2,1)S(1)} %constant_dynamic-update-slice_fusion.22.refs_0_, ...), custom_call_target="tpu_custom_call", output_to_operand_aliasing={{}: (7, {})} | custom-call | flops 1024 | bytes 1024 | tf_op jit(solution)/shard_map/apply_update/pallas_call | solution.py:171
  (131 shorter events, 13.7 us)
Async XLA Ops:
  7.7 9.1 %collective-permute-start.3 = (bf16[128,3584]{1,0:T(8,128)(2,1)}, bf16[128,3584]{1,0:T(8,128)(2,1)}, u32[]{:S(2)}, u32[]{:S(2)}) collective-permute-start(bf16[128,3584]{1,0:T(8,128)(2,1)} %get-tuple-element.137), channel_id=1, source_target_pairs={{0,1},{1,0},{2,3},{3,2},{4,5},{5,4},{6,7},{7,6},{8,9},{9,8},{10,11... | collective-permute-start | bytes 2752520 | tf_op jit(solution)/shard_map/ppermute | solution.py:28
  10.7 10.3 %collective-permute-start.2 = (bf16[128,3584]{1,0:T(8,128)(2,1)}, bf16[128,3584]{1,0:T(8,128)(2,1)}, u32[]{:S(2)}, u32[]{:S(2)}) collective-permute-start(bf16[128,3584]{1,0:T(8,128)(2,1)} %get-tuple-element.139), channel_id=1, source_target_pairs={{0,1},{1,0},{2,3},{3,2},{4,5},{5,4},{6,7},{7,6},{8,9},{9,8},{10,11... | collective-permute-start | bytes 2752520 | tf_op jit(solution)/shard_map/ppermute | solution.py:28
  13.6 11.6 %collective-permute-start.1 = (bf16[128,4096]{1,0:T(8,128)(2,1)}, bf16[128,4096]{1,0:T(8,128)(2,1)}, u32[]{:S(2)}, u32[]{:S(2)}) collective-permute-start(bf16[128,4096]{1,0:T(8,128)(2,1)} %get-tuple-element.141), channel_id=1, source_target_pairs={{0,1},{1,0},{2,3},{3,2},{4,5},{5,4},{6,7},{7,6},{8,9},{9,8},{10,11... | collective-permute-start | bytes 3145736 | tf_op jit(solution)/shard_map/ppermute | solution.py:28
  16.7 11.2 %collective-permute-start = (bf16[128,3584]{1,0:T(8,128)(2,1)}, bf16[128,3584]{1,0:T(8,128)(2,1)}, u32[]{:S(2)}, u32[]{:S(2)}) collective-permute-start(bf16[128,3584]{1,0:T(8,128)(2,1)} %get-tuple-element.145), channel_id=1, source_target_pairs={{0,1},{1,0},{2,3},{3,2},{4,5},{5,4},{6,7},{7,6},{8,9},{9,8},{10,11... | collective-permute-start | bytes 2752520 | tf_op jit(solution)/shard_map/ppermute | solution.py:28
  17.9 14.4 %collective-permute-start.7 = (bf16[64,3584]{1,0:T(8,128)(2,1)S(1)}, bf16[64,3584]{1,0:T(8,128)(2,1)S(1)}, u32[]{:S(2)}, u32[]{:S(2)}) collective-permute-start(bf16[64,3584]{1,0:T(8,128)(2,1)S(1)} %add_convert_fusion.7), channel_id=1, source_target_pairs={{0,2},{1,17},{2,0},{3,19},{4,6},{5,21},{6,4},{7,23},{8,10},{9,25},... | collective-permute-start | bytes 1376264 | tf_op jit(solution)/shard_map/ppermute | solution.py:28
  22.2 11.9 %collective-permute-start.6 = (bf16[64,3584]{1,0:T(8,128)(2,1)S(1)}, bf16[64,3584]{1,0:T(8,128)(2,1)S(1)}, u32[]{:S(2)}, u32[]{:S(2)}) collective-permute-start(bf16[64,3584]{1,0:T(8,128)(2,1)S(1)} %add_convert_fusion.6), channel_id=1, source_target_pairs={{0,4},{1,3},{2,6},{3,1},{4,0},{5,7},{6,2},{7,5},{8,12},{9,11},{10,... | collective-permute-start | bytes 1376264 | tf_op jit(solution)/shard_map/ppermute | solution.py:28
  26.3 13.6 %collective-permute-start.5 = (bf16[64,4096]{1,0:T(8,128)(2,1)S(1)}, bf16[64,4096]{1,0:T(8,128)(2,1)S(1)}, u32[]{:S(2)}, u32[]{:S(2)}) collective-permute-start(bf16[64,4096]{1,0:T(8,128)(2,1)S(1)} %add_convert_fusion.1), channel_id=1, source_target_pairs={{0,16},{1,5},{2,18},{3,7},{4,20},{5,1},{6,22},{7,3},{8,24},{9,13},... | collective-permute-start | bytes 1572872 | tf_op jit(solution)/shard_map/ppermute | solution.py:28
  27.9 29.7 %copy-start.6 = (f32[16,14848]{1,0:T(8,128)S(1)}, f32[16,14848]{1,0:T(8,128)}, u32[]{:S(2)}) copy-start(f32[16,14848]{1,0:T(8,128)} %param.12) | copy-start | bytes 2850820
  29.4 11.1 %collective-permute-start.4 = (bf16[64,3584]{1,0:T(8,128)(2,1)S(1)}, bf16[64,3584]{1,0:T(8,128)(2,1)S(1)}, u32[]{:S(2)}, u32[]{:S(2)}) collective-permute-start(bf16[64,3584]{1,0:T(8,128)(2,1)S(1)} %get-tuple-element.280), channel_id=1, source_target_pairs={{0,2},{1,17},{2,0},{3,19},{4,6},{5,21},{6,4},{7,23},{8,10},{9,25},... | collective-permute-start | bytes 1376264 | tf_op jit(solution)/shard_map/ppermute | solution.py:28
  32.4 12.3 %collective-permute-start.11 = (bf16[32,3584]{1,0:T(8,128)(2,1)S(1)}, bf16[32,3584]{1,0:T(8,128)(2,1)S(1)}, u32[]{:S(2)}, u32[]{:S(2)}) collective-permute-start(bf16[32,3584]{1,0:T(8,128)(2,1)S(1)} %add_convert_fusion.15), channel_id=1, source_target_pairs={{0,16},{1,5},{2,18},{3,7},{4,20},{5,1},{6,22},{7,3},{8,24},{9,13},... | collective-permute-start | bytes 688136 | tf_op jit(solution)/shard_map/ppermute | solution.py:28
  34.2 11.0 %collective-permute-start.10 = (bf16[32,3584]{1,0:T(8,128)(2,1)S(1)}, bf16[32,3584]{1,0:T(8,128)(2,1)S(1)}, u32[]{:S(2)}, u32[]{:S(2)}) collective-permute-start(bf16[32,3584]{1,0:T(8,128)(2,1)S(1)} %add_convert_fusion.14), channel_id=1, source_target_pairs={{0,2},{1,17},{2,0},{3,19},{4,6},{5,21},{6,4},{7,23},{8,10},{9,25},... | collective-permute-start | bytes 688136 | tf_op jit(solution)/shard_map/ppermute | solution.py:28
  40.0 8.9 %collective-permute-start.9 = (bf16[32,4096]{1,0:T(8,128)(2,1)S(1)}, bf16[32,4096]{1,0:T(8,128)(2,1)S(1)}, u32[]{:S(2)}, u32[]{:S(2)}) collective-permute-start(bf16[32,4096]{1,0:T(8,128)(2,1)S(1)} %add_convert_fusion.9), channel_id=1, source_target_pairs={{0,4},{1,3},{2,6},{3,1},{4,0},{5,7},{6,2},{7,5},{8,12},{9,11},{10,... | collective-permute-start | bytes 786440 | tf_op jit(solution)/shard_map/ppermute | solution.py:28
  40.6 9.0 %collective-permute-start.8 = (bf16[32,3584]{1,0:T(8,128)(2,1)S(1)}, bf16[32,3584]{1,0:T(8,128)(2,1)S(1)}, u32[]{:S(2)}, u32[]{:S(2)}) collective-permute-start(bf16[32,3584]{1,0:T(8,128)(2,1)S(1)} %add_convert_fusion.13), channel_id=1, source_target_pairs={{0,16},{1,5},{2,18},{3,7},{4,20},{5,1},{6,22},{7,3},{8,24},{9,13},... | collective-permute-start | bytes 688136 | tf_op jit(solution)/shard_map/ppermute | solution.py:28
  44.7 6.5 %collective-permute-start.15 = (bf16[16,3584]{1,0:T(8,128)(2,1)S(1)}, bf16[16,3584]{1,0:T(8,128)(2,1)S(1)}, u32[]{:S(2)}, u32[]{:S(2)}) collective-permute-start(bf16[16,3584]{1,0:T(8,128)(2,1)S(1)} %add_convert_fusion.23), channel_id=1, source_target_pairs={{0,4},{1,3},{2,6},{3,1},{4,0},{5,7},{6,2},{7,5},{8,12},{9,11},{10,... | collective-permute-start | bytes 344072 | tf_op jit(solution)/shard_map/ppermute | solution.py:28
  45.3 8.6 %collective-permute-start.14 = (bf16[16,3584]{1,0:T(8,128)(2,1)S(1)}, bf16[16,3584]{1,0:T(8,128)(2,1)S(1)}, u32[]{:S(2)}, u32[]{:S(2)}) collective-permute-start(bf16[16,3584]{1,0:T(8,128)(2,1)S(1)} %add_convert_fusion.22), channel_id=1, source_target_pairs={{0,16},{1,5},{2,18},{3,7},{4,20},{5,1},{6,22},{7,3},{8,24},{9,13},... | collective-permute-start | bytes 344072 | tf_op jit(solution)/shard_map/ppermute | solution.py:28
  48.9 5.6 %collective-permute-start.13 = (bf16[16,4096]{1,0:T(8,128)(2,1)S(1)}, bf16[16,4096]{1,0:T(8,128)(2,1)S(1)}, u32[]{:S(2)}, u32[]{:S(2)}) collective-permute-start(bf16[16,4096]{1,0:T(8,128)(2,1)S(1)} %add_convert_fusion.17), channel_id=1, source_target_pairs={{0,2},{1,17},{2,0},{3,19},{4,6},{5,21},{6,4},{7,23},{8,10},{9,25},... | collective-permute-start | bytes 393224 | tf_op jit(solution)/shard_map/ppermute | solution.py:28
  49.6 7.6 %collective-permute-start.12 = (bf16[16,3584]{1,0:T(8,128)(2,1)S(1)}, bf16[16,3584]{1,0:T(8,128)(2,1)S(1)}, u32[]{:S(2)}, u32[]{:S(2)}) collective-permute-start(bf16[16,3584]{1,0:T(8,128)(2,1)S(1)} %add_convert_fusion.21), channel_id=1, source_target_pairs={{0,4},{1,3},{2,6},{3,1},{4,0},{5,7},{6,2},{7,5},{8,12},{9,11},{10,... | collective-permute-start | bytes 344072 | tf_op jit(solution)/shard_map/ppermute | solution.py:28
  51.3 6.4 %collective-permute-start.19 = (bf16[8,3584]{1,0:T(8,128)(2,1)S(1)}, bf16[8,3584]{1,0:T(8,128)(2,1)S(1)}, u32[]{:S(2)}, u32[]{:S(2)}) collective-permute-start(bf16[8,3584]{1,0:T(8,128)(2,1)S(1)} %add_convert_fusion.35), channel_id=1, source_target_pairs={{0,8},{1,9},{2,10},{3,11},{4,12},{5,13},{6,14},{7,15},{8,0},{9,1},... | collective-permute-start | bytes 172040 | tf_op jit(solution)/shard_map/ppermute | solution.py:28
  54.0 9.5 %collective-permute-start.18 = (bf16[8,3584]{1,0:T(8,128)(2,1)S(1)}, bf16[8,3584]{1,0:T(8,128)(2,1)S(1)}, u32[]{:S(2)}, u32[]{:S(2)}) collective-permute-start(bf16[8,3584]{1,0:T(8,128)(2,1)S(1)} %add_convert_fusion.34), channel_id=1, source_target_pairs={{0,8},{1,9},{2,10},{3,11},{4,12},{5,13},{6,14},{7,15},{8,0},{9,1},... | collective-permute-start | bytes 172040 | tf_op jit(solution)/shard_map/ppermute | solution.py:28
  54.5 47.5 %slice-start = ((s8[7602176]{0:T(1024)(128)(4,1)}), s8[4194304]{0:T(1024)(128)(4,1)S(1)}, s32[]{:S(2)}) async-start(s8[7602176]{0:T(1024)(128)(4,1)} %bitcast.13), calls=%async_computation | async-start | bytes 8388608
  54.5 47.5 %copy-start.1 = (bf16[256,256]{1,0:T(8,128)(2,1)S(1)}, bf16[256,256]{1,0:T(8,128)(2,1)}, u32[]{:S(2)}) copy-start(bf16[256,256]{1,0:T(8,128)(2,1)} %projector_ref.7) | copy-start | bytes 393220
  54.5 10.3 %collective-permute-start.17 = (bf16[8,4096]{1,0:T(8,128)(2,1)S(1)}, bf16[8,4096]{1,0:T(8,128)(2,1)S(1)}, u32[]{:S(2)}, u32[]{:S(2)}) collective-permute-start(bf16[8,4096]{1,0:T(8,128)(2,1)S(1)} %add_convert_fusion.26), channel_id=1, source_target_pairs={{0,8},{1,9},{2,10},{3,11},{4,12},{5,13},{6,14},{7,15},{8,0},{9,1},... | collective-permute-start | bytes 196616 | tf_op jit(solution)/shard_map/ppermute | solution.py:28
  57.2 9.5 %collective-permute-start.16 = (bf16[8,3584]{1,0:T(8,128)(2,1)S(1)}, bf16[8,3584]{1,0:T(8,128)(2,1)S(1)}, u32[]{:S(2)}, u32[]{:S(2)}) collective-permute-start(bf16[8,3584]{1,0:T(8,128)(2,1)S(1)} %add_convert_fusion.33), channel_id=1, source_target_pairs={{0,8},{1,9},{2,10},{3,11},{4,12},{5,13},{6,14},{7,15},{8,0},{9,1},... | collective-permute-start | bytes 172040 | tf_op jit(solution)/shard_map/ppermute | solution.py:28
  57.8 12.4 %collective-permute-start.23 = (bf16[8,3584]{1,0:T(8,128)(2,1)S(1)}, bf16[8,3584]{1,0:T(8,128)(2,1)S(1)}, u32[]{:S(2)}, u32[]{:S(2)}) collective-permute-start(bf16[8,3584]{1,0:T(8,128)(2,1)S(1)} %get-tuple-element.221), channel_id=1, source_target_pairs={{0,8},{1,9},{2,10},{3,11},{4,12},{5,13},{6,14},{7,15},{8,0},{9,1},... | collective-permute-start | bytes 172040 | tf_op jit(solution)/shard_map/ppermute | solution.py:28
  63.5 8.2 %collective-permute-start.22 = (bf16[8,3584]{1,0:T(8,128)(2,1)S(1)}, bf16[8,3584]{1,0:T(8,128)(2,1)S(1)}, u32[]{:S(2)}, u32[]{:S(2)}) collective-permute-start(bf16[8,3584]{1,0:T(8,128)(2,1)S(1)} %get-tuple-element.223), channel_id=1, source_target_pairs={{0,8},{1,9},{2,10},{3,11},{4,12},{5,13},{6,14},{7,15},{8,0},{9,1},... | collective-permute-start | bytes 172040 | tf_op jit(solution)/shard_map/ppermute | solution.py:28
  65.0 8.8 %collective-permute-start.21 = (bf16[8,4096]{1,0:T(8,128)(2,1)S(1)}, bf16[8,4096]{1,0:T(8,128)(2,1)S(1)}, u32[]{:S(2)}, u32[]{:S(2)}) collective-permute-start(bf16[8,4096]{1,0:T(8,128)(2,1)S(1)} %get-tuple-element.225), channel_id=1, source_target_pairs={{0,8},{1,9},{2,10},{3,11},{4,12},{5,13},{6,14},{7,15},{8,0},{9,1},... | collective-permute-start | bytes 196616 | tf_op jit(solution)/shard_map/ppermute | solution.py:28
  66.9 14.4 %collective-permute-start.32 = (bf16[8,14848]{1,0:T(8,128)(2,1)S(1)}, bf16[8,14848]{1,0:T(8,128)(2,1)S(1)}, u32[]{:S(2)}, u32[]{:S(2)}) collective-permute-start(bf16[8,14848]{1,0:T(8,128)(2,1)S(1)} %pad_maximum_fusion), channel_id=1, source_target_pairs={{0,16},{1,17},{2,18},{3,19},{4,20},{5,21},{6,22},{7,23},{8,24},{9,... | collective-permute-start | bytes 712712 | tf_op jit(solution)/shard_map/ppermute | solution.py:28
  68.3 6.7 %collective-permute-start.20 = (bf16[8,3584]{1,0:T(8,128)(2,1)S(1)}, bf16[8,3584]{1,0:T(8,128)(2,1)S(1)}, u32[]{:S(2)}, u32[]{:S(2)}) collective-permute-start(bf16[8,3584]{1,0:T(8,128)(2,1)S(1)} %get-tuple-element.227), channel_id=1, source_target_pairs={{0,8},{1,9},{2,10},{3,11},{4,12},{5,13},{6,14},{7,15},{8,0},{9,1},... | collective-permute-start | bytes 172040 | tf_op jit(solution)/shard_map/ppermute | solution.py:28
  70.2 5.3 %collective-permute-start.27 = (bf16[16,3584]{1,0:T(8,128)(2,1)S(1)}, bf16[16,3584]{1,0:T(8,128)(2,1)S(1)}, u32[]{:S(2)}, u32[]{:S(2)}) collective-permute-start(bf16[16,3584]{1,0:T(8,128)(2,1)S(1)} %constant_dynamic-update-slice_fusion), channel_id=1, source_target_pairs={{0,4},{1,3},{2,6},{3,1},{4,0},{5,7},{6,2},{7,5},{8,12},{9,11},{10,... | collective-permute-start | bytes 344072 | tf_op jit(solution)/shard_map/ppermute | solution.py:28
  71.8 5.5 %collective-permute-start.26 = (bf16[16,3584]{1,0:T(8,128)(2,1)S(1)}, bf16[16,3584]{1,0:T(8,128)(2,1)S(1)}, u32[]{:S(2)}, u32[]{:S(2)}) collective-permute-start(bf16[16,3584]{1,0:T(8,128)(2,1)S(1)} %constant_dynamic-update-slice_fusion.2), channel_id=1, source_target_pairs={{0,16},{1,5},{2,18},{3,7},{4,20},{5,1},{6,22},{7,3},{8,24},{9,13},... | collective-permute-start | bytes 344072 | tf_op jit(solution)/shard_map/ppermute | solution.py:28
  73.8 5.9 %collective-permute-start.25 = (bf16[16,4096]{1,0:T(8,128)(2,1)S(1)}, bf16[16,4096]{1,0:T(8,128)(2,1)S(1)}, u32[]{:S(2)}, u32[]{:S(2)}) collective-permute-start(bf16[16,4096]{1,0:T(8,128)(2,1)S(1)} %constant_dynamic-update-slice_fusion.4), channel_id=1, source_target_pairs={{0,2},{1,17},{2,0},{3,19},{4,6},{5,21},{6,4},{7,23},{8,10},{9,25},... | collective-permute-start | bytes 393224 | tf_op jit(solution)/shard_map/ppermute | solution.py:28
  75.0 6.2 %collective-permute-start.24 = (bf16[16,3584]{1,0:T(8,128)(2,1)S(1)}, bf16[16,3584]{1,0:T(8,128)(2,1)S(1)}, u32[]{:S(2)}, u32[]{:S(2)}) collective-permute-start(bf16[16,3584]{1,0:T(8,128)(2,1)S(1)} %constant_dynamic-update-slice_fusion.6), channel_id=1, source_target_pairs={{0,4},{1,3},{2,6},{3,1},{4,0},{5,7},{6,2},{7,5},{8,12},{9,11},{10,... | collective-permute-start | bytes 344072 | tf_op jit(solution)/shard_map/ppermute | solution.py:28
  75.5 7.4 %collective-permute-start.31 = (bf16[32,3584]{1,0:T(8,128)(2,1)S(1)}, bf16[32,3584]{1,0:T(8,128)(2,1)S(1)}, u32[]{:S(2)}, u32[]{:S(2)}) collective-permute-start(bf16[32,3584]{1,0:T(8,128)(2,1)S(1)} %constant_dynamic-update-slice_fusion.8), channel_id=1, source_target_pairs={{0,16},{1,5},{2,18},{3,7},{4,20},{5,1},{6,22},{7,3},{8,24},{9,13},... | collective-permute-start | bytes 688136 | tf_op jit(solution)/shard_map/ppermute | solution.py:28
  77.3 6.9 %collective-permute-start.30 = (bf16[32,3584]{1,0:T(8,128)(2,1)S(1)}, bf16[32,3584]{1,0:T(8,128)(2,1)S(1)}, u32[]{:S(2)}, u32[]{:S(2)}) collective-permute-start(bf16[32,3584]{1,0:T(8,128)(2,1)S(1)} %constant_dynamic-update-slice_fusion.10), channel_id=1, source_target_pairs={{0,2},{1,17},{2,0},{3,19},{4,6},{5,21},{6,4},{7,23},{8,10},{9,25},... | collective-permute-start | bytes 688136 | tf_op jit(solution)/shard_map/ppermute | solution.py:28
  79.7 6.4 %collective-permute-start.29 = (bf16[32,4096]{1,0:T(8,128)(2,1)S(1)}, bf16[32,4096]{1,0:T(8,128)(2,1)S(1)}, u32[]{:S(2)}, u32[]{:S(2)}) collective-permute-start(bf16[32,4096]{1,0:T(8,128)(2,1)S(1)} %constant_dynamic-update-slice_fusion.12), channel_id=1, source_target_pairs={{0,4},{1,3},{2,6},{3,1},{4,0},{5,7},{6,2},{7,5},{8,12},{9,11},{10,... | collective-permute-start | bytes 786440 | tf_op jit(solution)/shard_map/ppermute | solution.py:28
  81.2 8.5 %collective-permute-start.28 = (bf16[32,3584]{1,0:T(8,128)(2,1)S(1)}, bf16[32,3584]{1,0:T(8,128)(2,1)S(1)}, u32[]{:S(2)}, u32[]{:S(2)}) collective-permute-start(bf16[32,3584]{1,0:T(8,128)(2,1)S(1)} %constant_dynamic-update-slice_fusion.14), channel_id=1, source_target_pairs={{0,16},{1,5},{2,18},{3,7},{4,20},{5,1},{6,22},{7,3},{8,24},{9,13},... | collective-permute-start | bytes 688136 | tf_op jit(solution)/shard_map/ppermute | solution.py:28
  83.0 12.7 %collective-permute-start.36 = (bf16[64,3584]{1,0:T(8,128)(2,1)S(1)}, bf16[64,3584]{1,0:T(8,128)(2,1)S(1)}, u32[]{:S(2)}, u32[]{:S(2)}) collective-permute-start(bf16[64,3584]{1,0:T(8,128)(2,1)S(1)} %constant_dynamic-update-slice_fusion.16.refs_0_), channel_id=1, source_target_pairs={{0,2},{1,17},{2,0},{3,19},{4,6},{5,21},{6,4},{7,23},{8,10},{9,25},... | collective-permute-start | bytes 1376264 | tf_op jit(solution)/shard_map/ppermute | solution.py:28
  84.1 16.6 %collective-permute-start.43 = (bf16[64,3584]{1,0:T(8,128)(2,1)S(1)}, bf16[64,3584]{1,0:T(8,128)(2,1)S(1)}, u32[]{:S(2)}, u32[]{:S(2)}) collective-permute-start(bf16[64,3584]{1,0:T(8,128)(2,1)S(1)} %constant_dynamic-update-slice_fusion.16.refs_0_), channel_id=1, source_target_pairs={{0,1},{1,0},{2,3},{3,2},{4,5},{5,4},{6,7},{7,6},{8,9},{9,8},{10,11... | collective-permute-start | bytes 1376264 | tf_op jit(solution)/shard_map/ppermute | solution.py:28
  84.2 12.6 %collective-permute-start.35 = (bf16[64,3584]{1,0:T(8,128)(2,1)S(1)}, bf16[64,3584]{1,0:T(8,128)(2,1)S(1)}, u32[]{:S(2)}, u32[]{:S(2)}) collective-permute-start(bf16[64,3584]{1,0:T(8,128)(2,1)S(1)} %constant_dynamic-update-slice_fusion.18.refs_0_), channel_id=1, source_target_pairs={{0,4},{1,3},{2,6},{3,1},{4,0},{5,7},{6,2},{7,5},{8,12},{9,11},{10,... | collective-permute-start | bytes 1376264 | tf_op jit(solution)/shard_map/ppermute | solution.py:28
  86.2 14.5 %collective-permute-start.34 = (bf16[64,4096]{1,0:T(8,128)(2,1)S(1)}, bf16[64,4096]{1,0:T(8,128)(2,1)S(1)}, u32[]{:S(2)}, u32[]{:S(2)}) collective-permute-start(bf16[64,4096]{1,0:T(8,128)(2,1)S(1)} %constant_dynamic-update-slice_fusion.20.refs_0_), channel_id=1, source_target_pairs={{0,16},{1,5},{2,18},{3,7},{4,20},{5,1},{6,22},{7,3},{8,24},{9,13},... | collective-permute-start | bytes 1572872 | tf_op jit(solution)/shard_map/ppermute | solution.py:28
  89.7 11.6 %collective-permute-start.33 = (bf16[64,3584]{1,0:T(8,128)(2,1)S(1)}, bf16[64,3584]{1,0:T(8,128)(2,1)S(1)}, u32[]{:S(2)}, u32[]{:S(2)}) collective-permute-start(bf16[64,3584]{1,0:T(8,128)(2,1)S(1)} %constant_dynamic-update-slice_fusion.22.refs_0_), channel_id=1, source_target_pairs={{0,2},{1,17},{2,0},{3,19},{4,6},{5,21},{6,4},{7,23},{8,10},{9,25},... | collective-permute-start | bytes 1376264 | tf_op jit(solution)/shard_map/ppermute | solution.py:28
  95.7 5.6 %collective-permute-start.41 = (bf16[64,3584]{1,0:T(8,128)(2,1)S(1)}, bf16[64,3584]{1,0:T(8,128)(2,1)S(1)}, u32[]{:S(2)}, u32[]{:S(2)}) collective-permute-start(bf16[64,3584]{1,0:T(8,128)(2,1)S(1)} %constant_dynamic-update-slice_fusion.18.refs_0_), channel_id=1, source_target_pairs={{0,1},{1,0},{2,3},{3,2},{4,5},{5,4},{6,7},{7,6},{8,9},{9,8},{10,11... | collective-permute-start | bytes 1376264 | tf_op jit(solution)/shard_map/ppermute | solution.py:28
  96.8 5.1 %collective-permute-start.44 = (bf16[64,3584]{1,0:T(8,128)(2,1)S(1)}, bf16[64,3584]{1,0:T(8,128)(2,1)S(1)}, u32[]{:S(2)}, u32[]{:S(2)}) collective-permute-start(bf16[64,3584]{1,0:T(8,128)(2,1)S(1)} %collective-permute-done.36.refs_1_), channel_id=1, source_target_pairs={{0,1},{1,0},{2,3},{3,2},{4,5},{5,4},{6,7},{7,6},{8,9},{9,8},{10,11... | collective-permute-start | bytes 1376264 | tf_op jit(solution)/shard_map/ppermute | solution.py:28
  100.7 5.4 %collective-permute-start.39 = (bf16[64,4096]{1,0:T(8,128)(2,1)S(1)}, bf16[64,4096]{1,0:T(8,128)(2,1)S(1)}, u32[]{:S(2)}, u32[]{:S(2)}) collective-permute-start(bf16[64,4096]{1,0:T(8,128)(2,1)S(1)} %constant_dynamic-update-slice_fusion.20.refs_0_), channel_id=1, source_target_pairs={{0,1},{1,0},{2,3},{3,2},{4,5},{5,4},{6,7},{7,6},{8,9},{9,8},{10,11... | collective-permute-start | bytes 1572872 | tf_op jit(solution)/shard_map/ppermute | solution.py:28
  100.7 5.4 %collective-permute-start.40 = (bf16[64,4096]{1,0:T(8,128)(2,1)S(1)}, bf16[64,4096]{1,0:T(8,128)(2,1)S(1)}, u32[]{:S(2)}, u32[]{:S(2)}) collective-permute-start(bf16[64,4096]{1,0:T(8,128)(2,1)S(1)} %collective-permute-done.34.refs_1_), channel_id=1, source_target_pairs={{0,1},{1,0},{2,3},{3,2},{4,5},{5,4},{6,7},{7,6},{8,9},{9,8},{10,11... | collective-permute-start | bytes 1572872 | tf_op jit(solution)/shard_map/ppermute | solution.py:28
  101.3 2.7 %collective-permute-start.42 = (bf16[64,3584]{1,0:T(8,128)(2,1)S(1)}, bf16[64,3584]{1,0:T(8,128)(2,1)S(1)}, u32[]{:S(2)}, u32[]{:S(2)}) collective-permute-start(bf16[64,3584]{1,0:T(8,128)(2,1)S(1)} %collective-permute-done.35.refs_1_), channel_id=1, source_target_pairs={{0,1},{1,0},{2,3},{3,2},{4,5},{5,4},{6,7},{7,6},{8,9},{9,8},{10,11... | collective-permute-start | bytes 1376264 | tf_op jit(solution)/shard_map/ppermute | solution.py:28
  101.3 7.2 %collective-permute-start.37 = (bf16[64,3584]{1,0:T(8,128)(2,1)S(1)}, bf16[64,3584]{1,0:T(8,128)(2,1)S(1)}, u32[]{:S(2)}, u32[]{:S(2)}) collective-permute-start(bf16[64,3584]{1,0:T(8,128)(2,1)S(1)} %constant_dynamic-update-slice_fusion.22.refs_0_), channel_id=1, source_target_pairs={{0,1},{1,0},{2,3},{3,2},{4,5},{5,4},{6,7},{7,6},{8,9},{9,8},{10,11... | collective-permute-start | bytes 1376264 | tf_op jit(solution)/shard_map/ppermute | solution.py:28
  101.8 6.7 %collective-permute-start.38 = (bf16[64,3584]{1,0:T(8,128)(2,1)S(1)}, bf16[64,3584]{1,0:T(8,128)(2,1)S(1)}, u32[]{:S(2)}, u32[]{:S(2)}) collective-permute-start(bf16[64,3584]{1,0:T(8,128)(2,1)S(1)} %collective-permute-done.33.refs_1_), channel_id=1, source_target_pairs={{0,1},{1,0},{2,3},{3,2},{4,5},{5,4},{6,7},{7,6},{8,9},{9,8},{10,11... | collective-permute-start | bytes 1376264 | tf_op jit(solution)/shard_map/ppermute | solution.py:28
  (6 other events, 61.0 us)

commit v3 on v0

v3 whole, which is shorter than its diff:
```python
import functools

import jax
import jax.numpy as jnp
from jax import lax
from jax.experimental import pallas as pl
from jax.experimental.pallas import tpu as pltpu
from jax.sharding import PartitionSpec as P

first_decay = 0.9
second_decay = 0.999
step_count = 100.0
update_scale = 0.25
both = ("outer", "shard")
chains = ((1, 0, 1), (1, 2, 0), (1, 1, 2), (1, 0, 1))


runs_per_chain = 2
slots = 3
lags = (0, 0, 0, 0)


def bits_of(count):
    return list(range(count.bit_length() - 1))


def swap(array, bits):
    size = lax.axis_size("outer") * lax.axis_size("shard")
    return lax.ppermute(array, both, [(i, i ^ (1 << bits[i % 2])) for i in range(size)])


def axis_orders():
    shard_bits = bits_of(lax.axis_size("shard"))
    outer_bits = [len(shard_bits) + bit for bit in bits_of(lax.axis_size("outer"))]
    turning = shard_bits[1:2] + outer_bits + shard_bits[2:-1]
    return [turning[t:] + turning[:t] + shard_bits[-1:] for t in range(3)]


def pieces_of(start, count):
    ends = [start + count * (run + 1) // runs_per_chain for run in range(runs_per_chain)]
    return [(at, end - at) for at, end in zip([start] + ends, ends) if end > at]


def prepare_kernel(spans, block_width, orders, shards, leaf_rows, me_ref, *refs):
    chain_count = len(spans)
    owner_hbm, scales_hbm, values_hbm = refs[:3]
    keep_refs, send_refs = refs[3 : 3 + chain_count], refs[3 + chain_count : 3 + 2 * chain_count]
    position_ref, owner_ref, scales_ref, wide_scales_ref, in_ref, keep_ref, send_ref = refs[
        3 + 2 * chain_count : -3
    ]
    small_sems, in_sems, out_sems = refs[-3:]
    rows = in_ref.shape[1]
    half = rows // 2
    runs = [
        (chain, at, size)
        for chain, (start, count) in enumerate(spans)
        for at, size in pieces_of(start, count)
    ]

    def incoming(index):
        _, at, size = runs[index]
        slot = index % slots
        return pltpu.make_async_copy(
            values_hbm.at[:, pl.ds(at * block_width, size * block_width)],
            in_ref.at[slot, :, pl.ds(0, size * block_width)],
            in_sems.at[slot],
        )

    def outgoing(index):
        chain, at, size = runs[index]
        slot = index % slots
        columns = pl.ds(0, size * block_width)
        target = pl.ds((at - spans[chain][0]) * block_width, size * block_width)
        return [
            pltpu.make_async_copy(
                buffer.at[slot, :, columns], outs[chain].at[:, target], out_sems.at[slot, which]
            )
            for which, (buffer, outs) in enumerate(((keep_ref, keep_refs), (send_ref, send_refs)))
        ]

    owner_copy = pltpu.make_async_copy(owner_hbm, owner_ref, small_sems.at[0])
    scales_copy = pltpu.make_async_copy(scales_hbm, scales_ref, small_sems.at[1])
    owner_copy.start()
    scales_copy.start()
    for index in range(min(slots - 1, len(runs))):
        incoming(index).start()
    owner_copy.wait()
    down = lax.broadcasted_iota(jnp.int32, (rows, rows), 0)
    across = lax.broadcasted_iota(jnp.int32, (rows, rows), 1)
    owner = owner_ref[...]
    owner_across = jnp.broadcast_to(owner, (rows, rows))
    earlier = (owner_across == owner_across.T) & (down < across)
    rank = jnp.sum(earlier.astype(jnp.int32), axis=0, keepdims=True)
    away = ((rank // leaf_rows) * shards + owner) ^ me_ref[0]
    for chain in range(chain_count):
        position = away & 1
        for bits in zip(*orders[chain]):
            bit = jnp.where(owner % 2 == 0, bits[0], bits[1])
            position = 2 * position + ((away >> bit) & 1)
        position_ref[chain] = position * leaf_rows + rank % leaf_rows
    scales_copy.wait()
    wide_scales_ref[...] = scales_ref[...].astype(jnp.float32)

    for index, (chain, at, size) in enumerate(runs):
        slot = index % slots
        if index + slots - 1 < len(runs):
            incoming(index + slots - 1).start()
        incoming(index).wait()
        if index >= slots:
            for copy in outgoing(index - slots):
                copy.wait()
        placing = (down == position_ref[chain]).astype(jnp.bfloat16)
        for block in range(size):
            columns = slice(block * block_width, (block + 1) * block_width)
            scale = wide_scales_ref[at + block : at + block + 1, :].astype(jnp.bfloat16)
            placed = jnp.dot(
                placing * scale, in_ref[slot, :, columns], preferred_element_type=jnp.float32
            ).astype(jnp.bfloat16)
            keep_ref[slot, :, columns] = placed[:half]
            send_ref[slot, :, columns] = placed[half:]
        for copy in outgoing(index):
            copy.start()
    for index in range(max(0, len(runs) - slots), len(runs)):
        for copy in outgoing(index):
            copy.wait()


def prepare(me, owner, values, scales, orders, spans, shards, leaf_rows):
    rows = values.shape[0]
    block_width = values.shape[1] // scales.shape[0]
    longest = max(size for span in spans for _, size in pieces_of(*span)) * block_width
    halves = [
        jax.ShapeDtypeStruct((rows // 2, count * block_width), jnp.bfloat16) for _, count in spans
    ]
    anywhere = pl.BlockSpec(memory_space=pl.ANY)
    *parts, position = pl.pallas_call(
        functools.partial(prepare_kernel, spans, block_width, orders, shards, leaf_rows),
        in_specs=[pl.BlockSpec(memory_space=pltpu.SMEM)] + [anywhere] * 3,
        out_specs=[anywhere] * (2 * len(spans)) + [pl.BlockSpec(memory_space=pltpu.VMEM)],
        out_shape=halves * 2 + [jax.ShapeDtypeStruct((len(spans), 1, rows), jnp.int32)],
        scratch_shapes=[
            pltpu.VMEM(owner.shape, jnp.int32),
            pltpu.VMEM(scales.shape, scales.dtype),
            pltpu.VMEM(scales.shape, jnp.float32),
            pltpu.VMEM((slots, rows, longest), jnp.bfloat16),
            pltpu.VMEM((slots, rows // 2, longest), jnp.bfloat16),
            pltpu.VMEM((slots, rows // 2, longest), jnp.bfloat16),
            pltpu.SemaphoreType.DMA((2,)),
            pltpu.SemaphoreType.DMA((slots,)),
            pltpu.SemaphoreType.DMA((slots, 2)),
        ],
        compiler_params=pltpu.CompilerParams(vmem_limit_bytes=56 * 1024 * 1024),
        cost_estimate=pl.CostEstimate(flops=1024, bytes_accessed=1024, transcendentals=0),
        name="prepare",
    )(me, owner, scales, values)
    return parts[: len(spans)], parts[len(spans) :], position


def apply_kernel(chosen, spans, block_width, projector_ref, position_ref, weights_hbm, *refs):
    chain_count = len(spans)
    pieces = refs[: 4 * chain_count]
    out_hbm, reordered_ref, weights_ref, direction_ref, out_ref, in_sems, out_sems = refs[-7:]
    rank = projector_ref.shape[1]
    quarter = rank // 4
    runs = [
        (chain, at, size)
        for chain, (start, count) in enumerate(spans)
        for at, size in pieces_of(start, count)
    ]

    def incoming(index):
        chain, at, size = runs[index]
        slot = index % slots
        columns = pl.ds(0, size * block_width)
        source = pl.ds((at - spans[chain][0]) * block_width, size * block_width)
        return [
            pltpu.make_async_copy(
                weights_hbm.at[:, pl.ds(at * block_width, size * block_width)],
                weights_ref.at[slot, :, columns],
                in_sems.at[slot, 4],
            )
        ] + [
            pltpu.make_async_copy(
                pieces[4 * chain + part].at[:, source],
                direction_ref.at[slot, pl.ds(part * quarter, quarter), columns],
                in_sems.at[slot, part],
            )
            for part in range(4)
        ]

    def outgoing(index):
        _, at, size = runs[index]
        slot = index % slots
        return pltpu.make_async_copy(
            out_ref.at[slot, :, pl.ds(0, size * block_width)],
            out_hbm.at[:, pl.ds(at * block_width, size * block_width)],
            out_sems.at[slot],
        )

    for index in range(min(slots - 1, len(runs))):
        for copy in incoming(index):
            copy.start()
    down = lax.broadcasted_iota(jnp.int32, (rank, rank), 0)
    for chain in range(chain_count):
        placing = (down == position_ref[chosen[chain]]).astype(jnp.bfloat16)
        reordered_ref[chain] = lax.dot_general(
            projector_ref[...],
            placing,
            (((1,), (1,)), ((), ())),
            preferred_element_type=jnp.float32,
        ).astype(jnp.bfloat16)
    for index, (chain, at, size) in enumerate(runs):
        slot = index % slots
        if index + slots - 1 < len(runs):
            for copy in incoming(index + slots - 1):
                copy.start()
        for copy in incoming(index):
            copy.wait()
        if index >= slots:
            outgoing(index - slots).wait()
        for block in range(0, size, 2):
            columns = slice(block * block_width, min(block + 2, size) * block_width)
            change = jnp.dot(
                reordered_ref[chain],
                direction_ref[slot, :, columns],
                preferred_element_type=jnp.float32,
            )
            out_ref[slot, :, columns] = (
                weights_ref[slot, :, columns].astype(jnp.float32) - update_scale * change
            ).astype(out_ref.dtype)
        outgoing(index).start()
    for index in range(max(0, len(runs) - slots), len(runs)):
        outgoing(index).wait()


def apply_update(projector, position, weights, pieces, so_far, chosen, spans, block_width):
    rows, rank = projector.shape
    longest = max(size for span in spans for _, size in pieces_of(*span)) * block_width
    whole = pl.BlockSpec(memory_space=pltpu.VMEM)
    anywhere = pl.BlockSpec(memory_space=pl.ANY)
    aliased = [] if so_far is None else [so_far]
    return pl.pallas_call(
        functools.partial(apply_kernel, chosen, spans, block_width),
        in_specs=[whole, whole] + [anywhere] * (1 + len(pieces) + len(aliased)),
        out_specs=anywhere,
        input_output_aliases={3 + len(pieces): 0} if aliased else {},
        out_shape=jax.ShapeDtypeStruct(weights.shape, weights.dtype),
        scratch_shapes=[
            pltpu.VMEM((len(spans), rows, rank), jnp.bfloat16),
            pltpu.VMEM((slots, rows, longest), jnp.bfloat16),
            pltpu.VMEM((slots, rank, longest), jnp.bfloat16),
            pltpu.VMEM((slots, rows, longest), jnp.bfloat16),
            pltpu.SemaphoreType.DMA((slots, 5)),
            pltpu.SemaphoreType.DMA((slots,)),
        ],
        compiler_params=pltpu.CompilerParams(vmem_limit_bytes=20 * 1024 * 1024),
        cost_estimate=pl.CostEstimate(flops=1024, bytes_accessed=1024, transcendentals=0),
        name="apply_update",
    )(projector, position, weights, *pieces, *aliased)


def added(terms):
    return sum(term.astype(jnp.float32) for term in terms).astype(jnp.bfloat16)


def normalized(owned, first, second):
    new_first = first_decay * first + (1.0 - first_decay) * owned
    new_second = second_decay * second + (1.0 - second_decay) * owned * owned
    return new_first, new_second


def per_device(
    grad_values, grad_scales, block_owner, projector, weights, first_moment, second_moment
):
    shards, outers = lax.axis_size("shard"), lax.axis_size("outer")
    outer = lax.axis_index("outer")
    rank_rows = block_owner.shape[0]
    leaf_rows = rank_rows // shards // outers
    values = grad_values[0, 0]
    scales = grad_scales[0, 0].T
    col_blocks = scales.shape[0]
    block_width = values.shape[1] // col_blocks
    me = lax.axis_index(both).astype(jnp.int32)[None]

    turns = axis_orders()
    stages = len(turns[0])
    total = sum(share for share, _, _ in chains)
    ends = [
        round(col_blocks * sum(share for share, _, _ in chains[: i + 1]) / total)
        for i in range(len(chains))
    ]
    starts = [0] + ends[:-1]
    counts = [end - start for start, end in zip(starts, ends)]
    spans = list(zip(starts, counts))
    orders = [(turns[left], turns[right]) for _, left, right in chains]
    every = range(len(chains))

    last = [me]

    def turn_of(*arrays):
        return lax.optimization_barrier((*arrays, last[0]))[:-1]

    bits = [list(zip(*order)) for order in orders]
    partial, gathered, owned_parts = {}, {}, {}

    def reduce_stage(i, stage):
        mine, came = turn_of(*partial[i])
        half = mine.shape[0] // 2
        send = added([mine[half:], came[half:]])
        sent = swap(send, bits[i][stage])
        mine, came, last[0] = lax.optimization_barrier((mine, came, send))
        partial[i] = (added([mine[:half], came[:half]]), sent)

    def update_stage(i):
        owned_parts[i] = added(turn_of(*partial[i]))
        own = (outer * leaf_rows, starts[i] * block_width)
        shape = (leaf_rows, counts[i] * block_width)
        new_first, new_second = normalized(
            owned_parts[i].astype(jnp.float32),
            lax.dynamic_slice(first_moment, own, shape),
            lax.dynamic_slice(second_moment, own, shape),
        )
        corrected = new_first / (1.0 - first_decay**step_count)
        spread = jnp.sqrt(new_second / (1.0 - second_decay**step_count)) + 1e-08
        update = (corrected / spread).astype(jnp.bfloat16)
        gathered[i] = (update, swap(update, bits[i][-1]))
        last[0] = update

    def gather_stage(i, stage):
        mine = jnp.concatenate(turn_of(*gathered[i]), axis=0)
        gathered[i] = (mine, swap(mine, bits[i][stage]))
        last[0] = mine

    def owned_by_shard():
        owned = jnp.concatenate([owned_parts[i] for i in every], axis=1)
        for bit in bits_of(outers):
            other = swap(owned, (len(bits_of(shards)) + bit,) * 2)
            low = ((outer >> bit) & 1) == 0
            owned = jnp.where(
                low,
                jnp.concatenate([owned, other], axis=0),
                jnp.concatenate([other, owned], axis=0),
            )
        return owned

    def moments(owned):
        (owned,) = turn_of(owned)
        moved = normalized(owned.astype(jnp.float32), first_moment, second_moment)
        last[0] = moved[0]
        return moved

    keeps, sends, position = prepare(
        me, block_owner[None, :], values, scales, orders, spans, shards, leaf_rows
    )
    for i in every:
        partial[i] = [keeps[i], swap(sends[i], (0, 0))]
    owned = new_first = new_second = None
    work = [(stage + lags[i], i, stage) for i in every for stage in range(2 * stages)]
    for _, i, stage in sorted(work):
        if stage < stages:
            reduce_stage(i, stage)
        elif stage == stages:
            update_stage(i)
            if len(owned_parts) == len(chains):
                owned = owned_by_shard()
        else:
            if stage == 2 * stages - 1 and new_first is None:
                new_first, new_second = moments(owned)
            gather_stage(i, 2 * stages - 1 - stage)
    forwarded = {}
    for i in every:
        mine, came = gathered[i]
        beside = swap(mine, (0, 0))
        (came,) = turn_of(came)
        forwarded[i] = (mine, came, beside, swap(came, (0, 0)))
        last[0] = came
    new_weights = None
    for chosen in ((0, 1), (2, 3)):
        new_weights = last[0] = apply_update(
            projector,
            position,
            weights,
            turn_of(*[piece for i in chosen for piece in forwarded[i]]),
            new_weights,
            chosen,
            [spans[i] for i in chosen],
            block_width,
        )
    return (new_weights, new_first, new_second)


def solution(mesh):
    placed = (
        P("outer", "shard", None, None),
        P("outer", "shard", None, None),
        P(),
        P(("outer", "shard"), None),
        P(("outer", "shard"), None),
        P("shard", None),
        P("shard", None),
    )
    return jax.shard_map(
        per_device,
        mesh=mesh,
        in_specs=placed,
        out_specs=(P(("outer", "shard"), None), P("shard", None), P("shard", None)),
        check_vma=False,
    )
```

time: 258 us -> 109 us (0.42)
  waiting for transfers between devices: 168 us -> 31.1 us
  starting transfers between devices: 0.08 us -> 46.8 us
  local copies, waits for them, and re-layouts: 27.6 us -> 0.39 us
  matrix products: 19.9 us -> 0 us
  Pallas kernels: 0 us -> 16.2 us
  blocking collectives: 13 us -> 0 us
  between operations: 14.1 us -> 1.32 us
    reduce_scatter x1 -> x0, waiting for transfers between devices: 98.2 us -> none  [per_device(): lax.psum_scatter(partial_terms.astype(jnp.bfloat16), 'shard', scatter_dim...]
    all_gather x1 -> x0, waiting for transfers between devices: 70.2 us -> none  [per_device(): gathered = lax.all_gather(update, 'shard', axis=0, tiled=True)]
    ppermute x0 -> x45, starting transfers between devices: none -> 46.8 us  [swap(): lax.ppermute(array, both, [(i, i ^ 1 << bits[i % 2]) for i in range(size)])]
    ppermute x0 -> x45, waiting for transfers between devices: none -> 31.1 us  [swap(): lax.ppermute(array, both, [(i, i ^ 1 << bits[i % 2]) for i in range(size)])]
    convert_element_type x3 -> x0, local copies, waits for them, and re-layouts: 27.6 us -> none  [the longest x1 15.6 us: per_device(): sent_values.reshape(rank_rows, col_blocks, block_width).astype(jnp.float32)]
    dot_general x3 -> x0, matrix products: 19.9 us -> none  [the longest x1 10.7 us: per_device(): jnp.dot(placing, values, preferred_element_type=jnp.float32)]
    pallas_call x0 -> x3, Pallas kernels: none -> 16.2 us  [the longest x2 8.13 us: apply_update(): pl.pallas_call(functools.partial(apply_kernel, chosen, spans, block_width...]
    all_gather x1 -> x0, blocking collectives: 13 us -> none  [per_device(): all_rows = lax.all_gather(pod_low[None], 'outer', axis=0, tiled=True)]
  transfers between devices with their start and end apart: 2 -> 45, of which waited for: 2 -> 10; matrix products, arithmetic and copies ran while one was open for 0% -> 12% of each run, Pallas kernels for 0% -> 4%
where the time goes in v3:
time: 109 us; the launch traced here: 108 us
  starting transfers between devices  46.8 us (43%)
  waiting for transfers between devices  31.1 us (29%)
  Pallas kernels  16.2 us (15%)
  other arithmetic  12.6 us (12%)
  between operations  1.32 us (1%)
    ppermute x45, starting transfers between devices, swap(): lax.ppermute(array, both, [(i, i ^ 1 << bits[i % 2]) for i in range(size)])  46.8 us
    ppermute x45, waiting for transfers between devices, swap(): lax.ppermute(array, both, [(i, i ^ 1 << bits[i % 2]) for i in range(size)])  31.1 us
    convert_element_type x31, other arithmetic, added(): sum((term.astype(jnp.float32) for term in terms)).astype(jnp.bfloat16)  10.5 us
    pallas_call x2, Pallas kernels, apply_update(): pl.pallas_call(functools.partial(apply_kernel, chosen, spans, block_width...  8.13 us
    pallas_call x1, Pallas kernels, prepare(): pl.pallas_call(functools.partial(prepare_kernel, spans, block_width, orde...  8.08 us
  transfers between devices with their start and end apart: 45, of which 10 were waited for; matrix products, arithmetic and copies ran while one was open for 12% of the time, Pallas kernels for 4%

profile of v3, /device:TPU:0, one launch (start us, length us, event | category | flops | bytes accessed | tf_op | source)
XLA Modules:
  0.0 108.4 jit_solution(10006517042841831283)
XLA Ops:
  0.6 8.1 %prepare.1 = (bf16[128,3712]{1,0:T(8,128)(2,1)}, bf16[128,3712]{1,0:T(8,128)(2,1)}, bf16[128,3712]{1,0:T(8,128)(2,1)}, bf16[128,3712]{1,0:T(8,128)(2,1)}, bf16[1...) custom-call(s32[1]{0:T(128)} %bitcast.me_ref, ...), custom_call_target="tpu_custom_call" | custom-call | flops 1024 | bytes 1024 | tf_op jit(solution)/shard_map/prepare/pallas_call | solution.py:136
  8.7 0.5 collective-permute-start
  9.8 2.3 %collective-permute-done = bf16[128,3712]{1,0:T(8,128)(2,1)S(1)} collective-permute-done((bf16[128,3712]{1,0:T(8,128)(2,1)}, bf16[128,3712]{1,0:T(8,128)(2,1)S(1)}, u32[]{:S(2)}, u32[]{:S(2)}) %collective-permute-start) | collective-permute-done | bytes 950304 | tf_op jit(solution)/shard_map/ppermute | solution.py:29
  12.2 1.1 %add_convert_fusion.7 = bf16[64,3712]{1,0:T(8,128)(2,1)S(1)} fusion(bf16[128,3712]{1,0:T(8,128)(2,1)S(1)} %collective-permute-done, bf16[128,3712]{1,0:T(8,128)(2,1)} %get-tuple-element.134), kind=kLoop, calls=%fused_computation.11 | loop fusion | flops 950272 | bytes 1425408 | tf_op jit(solution)/shard_map/convert_element_type | solution.py:263
  13.3 3.0 %collective-permute-start.1 = (bf16[64,3712]{1,0:T(8,128)(2,1)S(1)}, bf16[64,3712]{1,0:T(8,128)(2,1)S(1)}, u32[]{:S(2)}, u32[]{:S(2)}) collective-permute-start(bf16[64,3712]{1,0:T(8,128)(2,1)S(1)} %add_convert_fusion.7), channel_id=1, source_target_pairs={{0,16},{1,5},{2,18},{3,7},{4,20},{5,1},{6,22},{7,3},{8,24},{9,13},... | collective-permute-start | bytes 1425416 | tf_op jit(solution)/shard_map/ppermute | solution.py:29
  16.3 1.3 %add_convert_fusion.5 = bf16[64,3712]{1,0:T(8,128)(2,1)S(1)} fusion(bf16[128,3712]{1,0:T(8,128)(2,1)} %collective-permute-done.5, bf16[128,3712]{1,0:T(8,128)(2,1)} %get-tuple-element.152), kind=kLoop, calls=%fused_computation.9 | loop fusion | flops 950272 | bytes 1425408 | tf_op jit(solution)/shard_map/convert_element_type | solution.py:263
  17.6 1.6 %collective-permute-start.6 = (bf16[64,3712]{1,0:T(8,128)(2,1)S(1)}, bf16[64,3712]{1,0:T(8,128)(2,1)S(1)}, u32[]{:S(2)}, u32[]{:S(2)}) collective-permute-start(bf16[64,3712]{1,0:T(8,128)(2,1)S(1)} %add_convert_fusion.5), channel_id=1, source_target_pairs={{0,4},{1,3},{2,6},{3,1},{4,0},{5,7},{6,2},{7,5},{8,12},{9,11},{10,... | collective-permute-start | bytes 1425416 | tf_op jit(solution)/shard_map/ppermute | solution.py:29
  19.2 1.3 %add_convert_fusion.3 = bf16[64,3712]{1,0:T(8,128)(2,1)S(1)} fusion(bf16[128,3712]{1,0:T(8,128)(2,1)} %collective-permute-done.10, bf16[128,3712]{1,0:T(8,128)(2,1)} %get-tuple-element.170), kind=kLoop, calls=%fused_computation.7 | loop fusion | flops 950272 | bytes 1425408 | tf_op jit(solution)/shard_map/convert_element_type | solution.py:263
  20.5 1.6 %collective-permute-start.11 = (bf16[64,3712]{1,0:T(8,128)(2,1)S(1)}, bf16[64,3712]{1,0:T(8,128)(2,1)S(1)}, u32[]{:S(2)}, u32[]{:S(2)}) collective-permute-start(bf16[64,3712]{1,0:T(8,128)(2,1)S(1)} %add_convert_fusion.3), channel_id=1, source_target_pairs={{0,2},{1,17},{2,0},{3,19},{4,6},{5,21},{6,4},{7,23},{8,10},{9,25},... | collective-permute-start | bytes 1425416 | tf_op jit(solution)/shard_map/ppermute | solution.py:29
  22.1 1.3 %add_convert_fusion.1 = bf16[64,3712]{1,0:T(8,128)(2,1)S(1)} fusion(bf16[128,3712]{1,0:T(8,128)(2,1)} %collective-permute-done.18, bf16[128,3712]{1,0:T(8,128)(2,1)} %get-tuple-element.194), kind=kLoop, calls=%fused_computation.5 | loop fusion | flops 950272 | bytes 1425408 | tf_op jit(solution)/shard_map/convert_element_type | solution.py:263
  23.4 0.6 collective-permute-start.19
  24.0 1.1 %add_convert_fusion.6 = bf16[64,3712]{1,0:T(8,128)(2,1)S(1)} fusion(bf16[128,3712]{1,0:T(8,128)(2,1)S(1)} %collective-permute-done, bf16[128,3712]{1,0:T(8,128)(2,1)} %get-tuple-element.134), kind=kLoop, calls=%fused_computation.10 | loop fusion | flops 950272 | bytes 1425408 | tf_op jit(solution)/shard_map/convert_element_type | solution.py:263
  25.1 1.3 %add_convert_fusion.4 = bf16[64,3712]{1,0:T(8,128)(2,1)S(1)} fusion(bf16[128,3712]{1,0:T(8,128)(2,1)} %collective-permute-done.5, bf16[128,3712]{1,0:T(8,128)(2,1)} %get-tuple-element.152), kind=kLoop, calls=%fused_computation.8 | loop fusion | flops 950272 | bytes 1425408 | tf_op jit(solution)/shard_map/convert_element_type | solution.py:263
  26.4 1.1 %add_convert_fusion.2 = bf16[64,3712]{1,0:T(8,128)(2,1)S(1)} fusion(bf16[128,3712]{1,0:T(8,128)(2,1)} %collective-permute-done.10, bf16[128,3712]{1,0:T(8,128)(2,1)S(1)} %copy-done.5), kind=kLoop, calls=%fused_computation.6 | loop fusion | flops 950272 | bytes 1425408 | tf_op jit(solution)/shard_map/convert_element_type | solution.py:263
  27.5 1.1 %add_convert_fusion = bf16[64,3712]{1,0:T(8,128)(2,1)S(1)} fusion(bf16[128,3712]{1,0:T(8,128)(2,1)} %collective-permute-done.18, bf16[128,3712]{1,0:T(8,128)(2,1)S(1)} %copy-done.4), kind=kLoop, calls=%fused_computation.4 | loop fusion | flops 950272 | bytes 1425408 | tf_op jit(solution)/shard_map/convert_element_type | solution.py:263
  29.3 1.6 %collective-permute-start.7 = (bf16[32,3712]{1,0:T(8,128)(2,1)S(1)}, bf16[32,3712]{1,0:T(8,128)(2,1)S(1)}, u32[]{:S(2)}, u32[]{:S(2)}) collective-permute-start(bf16[32,3712]{1,0:T(8,128)(2,1)S(1)} %add_convert_fusion.13), channel_id=1, source_target_pairs={{0,2},{1,17},{2,0},{3,19},{4,6},{5,21},{6,4},{7,23},{8,10},{9,25},... | collective-permute-start | bytes 712712 | tf_op jit(solution)/shard_map/ppermute | solution.py:29
  31.0 1.0 collective-permute-start.12
  32.0 6.0 %collective-permute-done.19 = bf16[64,3712]{1,0:T(8,128)(2,1)S(1)} collective-permute-done((bf16[64,3712]{1,0:T(8,128)(2,1)S(1)}, bf16[64,3712]{1,0:T(8,128)(2,1)S(1)}, u32[]{:S(2)}, u32[]{:S(2)}) %collective-permute-start.19) | collective-permute-done | bytes 475168 | tf_op jit(solution)/shard_map/ppermute | solution.py:29
  38.0 1.6 %collective-permute-start.20 = (bf16[32,3712]{1,0:T(8,128)(2,1)S(1)}, bf16[32,3712]{1,0:T(8,128)(2,1)S(1)}, u32[]{:S(2)}, u32[]{:S(2)}) collective-permute-start(bf16[32,3712]{1,0:T(8,128)(2,1)S(1)} %add_convert_fusion.9), channel_id=1, source_target_pairs={{0,16},{1,5},{2,18},{3,7},{4,20},{5,1},{6,22},{7,3},{8,24},{9,13},... | collective-permute-start | bytes 712712 | tf_op jit(solution)/shard_map/ppermute | solution.py:29
  39.9 1.6 %collective-permute-start.3 = (bf16[16,3712]{1,0:T(8,128)(2,1)S(1)}, bf16[16,3712]{1,0:T(8,128)(2,1)S(1)}, u32[]{:S(2)}, u32[]{:S(2)}) collective-permute-start(bf16[16,3712]{1,0:T(8,128)(2,1)S(1)} %add_convert_fusion.23), channel_id=1, source_target_pairs={{0,2},{1,17},{2,0},{3,19},{4,6},{5,21},{6,4},{7,23},{8,10},{9,25},... | collective-permute-start | bytes 356360 | tf_op jit(solution)/shard_map/ppermute | solution.py:29
  41.5 0.6 collective-permute-start.8
  42.7 1.5 %collective-permute-done.20 = bf16[32,3712]{1,0:T(8,128)(2,1)S(1)} collective-permute-done((bf16[32,3712]{1,0:T(8,128)(2,1)S(1)}, bf16[32,3712]{1,0:T(8,128)(2,1)S(1)}, u32[]{:S(2)}, u32[]{:S(2)}) %collective-permute-start.20) | collective-permute-done | bytes 237600 | tf_op jit(solution)/shard_map/ppermute | solution.py:29
  44.8 1.2 %collective-permute-done.3 = bf16[16,3712]{1,0:T(8,128)(2,1)S(1)} collective-permute-done((bf16[16,3712]{1,0:T(8,128)(2,1)S(1)}, bf16[16,3712]{1,0:T(8,128)(2,1)S(1)}, u32[]{:S(2)}, u32[]{:S(2)}) %collective-permute-start.3) | collective-permute-done | bytes 118816 | tf_op jit(solution)/shard_map/ppermute | solution.py:29
  46.0 2.7 %collective-permute-start.4 = (bf16[8,3712]{1,0:T(8,128)(2,1)S(1)}, bf16[8,3712]{1,0:T(8,128)(2,1)S(1)}, u32[]{:S(2)}, u32[]{:S(2)}) collective-permute-start(bf16[8,3712]{1,0:T(8,128)(2,1)S(1)} %add_convert_fusion.35), channel_id=1, source_target_pairs={{0,8},{1,9},{2,10},{3,11},{4,12},{5,13},{6,14},{7,15},{8,0},{9,1},... | collective-permute-start | bytes 178184 | tf_op jit(solution)/shard_map/ppermute | solution.py:29
  48.8 1.4 %collective-permute-start.14 = (bf16[8,3712]{1,0:T(8,128)(2,1)S(1)}, bf16[8,3712]{1,0:T(8,128)(2,1)S(1)}, u32[]{:S(2)}, u32[]{:S(2)}) collective-permute-start(bf16[8,3712]{1,0:T(8,128)(2,1)S(1)} %add_convert_fusion.31), channel_id=1, source_target_pairs={{0,8},{1,9},{2,10},{3,11},{4,12},{5,13},{6,14},{7,15},{8,0},{9,1},... | collective-permute-start | bytes 178184 | tf_op jit(solution)/shard_map/ppermute | solution.py:29
  50.2 2.2 %collective-permute-start.22 = (bf16[8,3712]{1,0:T(8,128)(2,1)S(1)}, bf16[8,3712]{1,0:T(8,128)(2,1)S(1)}, u32[]{:S(2)}, u32[]{:S(2)}) collective-permute-start(bf16[8,3712]{1,0:T(8,128)(2,1)S(1)} %add_convert_fusion.26), channel_id=1, source_target_pairs={{0,8},{1,9},{2,10},{3,11},{4,12},{5,13},{6,14},{7,15},{8,0},{9,1},... | collective-permute-start | bytes 178184 | tf_op jit(solution)/shard_map/ppermute | solution.py:29
  52.4 0.8 collective-permute-start.9
  53.3 3.1 %collective-permute-done.14 = bf16[8,3712]{1,0:T(8,128)(2,1)S(1)} collective-permute-done((bf16[8,3712]{1,0:T(8,128)(2,1)S(1)}, bf16[8,3712]{1,0:T(8,128)(2,1)S(1)}, u32[]{:S(2)}, u32[]{:S(2)}) %collective-permute-start.14) | collective-permute-done | bytes 59424 | tf_op jit(solution)/shard_map/ppermute | solution.py:29
  56.6 3.0 %collective-permute-done.9 = bf16[8,3712]{1,0:T(8,128)(2,1)S(1)} collective-permute-done((bf16[8,3712]{1,0:T(8,128)(2,1)S(1)}, bf16[8,3712]{1,0:T(8,128)(2,1)S(1)}, u32[]{:S(2)}, u32[]{:S(2)}) %collective-permute-start.9) | collective-permute-done | bytes 59424 | tf_op jit(solution)/shard_map/ppermute | solution.py:29
  59.9 3.0 %collective-permute-start.15 = (bf16[8,3712]{1,0:T(8,128)(2,1)S(1)}, bf16[8,3712]{1,0:T(8,128)(2,1)S(1)}, u32[]{:S(2)}, u32[]{:S(2)}) collective-permute-start(bf16[8,3712]{1,0:T(8,128)(2,1)S(1)} %get-tuple-element.214), channel_id=1, source_target_pairs={{0,8},{1,9},{2,10},{3,11},{4,12},{5,13},{6,14},{7,15},{8,0},{9,1},... | collective-permute-start | bytes 178184 | tf_op jit(solution)/shard_map/ppermute | solution.py:29
  63.0 1.5 %collective-permute-start.30 = (bf16[8,14848]{1,0:T(8,128)(2,1)S(1)}, bf16[8,14848]{1,0:T(8,128)(2,1)S(1)}, u32[]{:S(2)}, u32[]{:S(2)}) collective-permute-start(bf16[8,14848]{1,0:T(8,128)(2,1)S(1)} %pad_maximum_fusion), channel_id=1, source_target_pairs={{0,16},{1,17},{2,18},{3,19},{4,20},{5,21},{6,22},{7,23},{8,24},{9,... | collective-permute-start | bytes 712712 | tf_op jit(solution)/shard_map/ppermute | solution.py:29
  64.5 3.0 %collective-permute-start.25 = (bf16[16,3712]{1,0:T(8,128)(2,1)S(1)}, bf16[16,3712]{1,0:T(8,128)(2,1)S(1)}, u32[]{:S(2)}, u32[]{:S(2)}) collective-permute-start(bf16[16,3712]{1,0:T(8,128)(2,1)S(1)} %constant_dynamic-update-slice_fusion), channel_id=1, source_target_pairs={{0,4},{1,3},{2,6},{3,1},{4,0},{5,7},{6,2},{7,5},{8,12},{9,11},{10,... | collective-permute-start | bytes 356360 | tf_op jit(solution)/shard_map/ppermute | solution.py:29
  67.5 1.6 %collective-permute-start.24 = (bf16[16,3712]{1,0:T(8,128)(2,1)S(1)}, bf16[16,3712]{1,0:T(8,128)(2,1)S(1)}, u32[]{:S(2)}, u32[]{:S(2)}) collective-permute-start(bf16[16,3712]{1,0:T(8,128)(2,1)S(1)} %constant_dynamic-update-slice_fusion.2), channel_id=1, source_target_pairs={{0,16},{1,5},{2,18},{3,7},{4,20},{5,1},{6,22},{7,3},{8,24},{9,13},... | collective-permute-start | bytes 356360 | tf_op jit(solution)/shard_map/ppermute | solution.py:29
  69.2 1.1 collective-permute-start.23
  70.4 2.4 %collective-permute-start.29 = (bf16[32,3712]{1,0:T(8,128)(2,1)S(1)}, bf16[32,3712]{1,0:T(8,128)(2,1)S(1)}, u32[]{:S(2)}, u32[]{:S(2)}) collective-permute-start(bf16[32,3712]{1,0:T(8,128)(2,1)S(1)} %constant_dynamic-update-slice_fusion.8), channel_id=1, source_target_pairs={{0,16},{1,5},{2,18},{3,7},{4,20},{5,1},{6,22},{7,3},{8,24},{9,13},... | collective-permute-start | bytes 712712 | tf_op jit(solution)/shard_map/ppermute | solution.py:29
  72.8 1.6 %collective-permute-start.28 = (bf16[32,3712]{1,0:T(8,128)(2,1)S(1)}, bf16[32,3712]{1,0:T(8,128)(2,1)S(1)}, u32[]{:S(2)}, u32[]{:S(2)}) collective-permute-start(bf16[32,3712]{1,0:T(8,128)(2,1)S(1)} %constant_dynamic-update-slice_fusion.10), channel_id=1, source_target_pairs={{0,2},{1,17},{2,0},{3,19},{4,6},{5,21},{6,4},{7,23},{8,10},{9,25},... | collective-permute-start | bytes 712712 | tf_op jit(solution)/shard_map/ppermute | solution.py:29
  74.4 1.0 collective-permute-start.27
  75.8 3.0 %collective-permute-start.35 = (bf16[32,3712]{1,0:T(8,128)(2,1)S(1)}, bf16[32,3712]{1,0:T(8,128)(2,1)S(1)}, u32[]{:S(2)}, u32[]{:S(2)}) collective-permute-start(bf16[32,3712]{1,0:T(8,128)(2,1)S(1)} %constant_dynamic-update-slice_fusion.14), channel_id=1, source_target_pairs={{0,16},{1,5},{2,18},{3,7},{4,20},{5,1},{6,22},{7,3},{8,24},{9,13},... | collective-permute-start | bytes 712712 | tf_op jit(solution)/shard_map/ppermute | solution.py:29
  78.9 1.5 %fusion.1 = (f32[16,14848]{1,0:T(8,128)}, f32[16,14848]{1,0:T(8,128)}) fusion(bf16[16,14848]{1,0:T(8,128)(2,1)S(1)} %maximum_select_fusion, f32[16,14848]{1,0:T(8,128)S(1)} %copy-done.2, f32[16,14848]{1,0:T(8,128)S(1)} %copy-done.3), kind=kLoop, calls=%fused_computation.3 | loop fusion | flops 1900544 | bytes 4276224 | tf_op jit(solution)/shard_map/add | solution.py:268
  80.6 1.1 collective-permute-start.33
  81.7 0.9 collective-permute-start.34
  82.6 1.1 %collective-permute-start.32 = (bf16[64,3712]{1,0:T(8,128)(2,1)S(1)}, bf16[64,3712]{1,0:T(8,128)(2,1)S(1)}, u32[]{:S(2)}, u32[]{:S(2)}) collective-permute-start(bf16[64,3712]{1,0:T(8,128)(2,1)S(1)} %constant_dynamic-update-slice_fusion.20.refs_0_), channel_id=1, source_target_pairs={{0,16},{1,5},{2,18},{3,7},{4,20},{5,1},{6,22},{7,3},{8,24},{9,13},... | collective-permute-start | bytes 1425416 | tf_op jit(solution)/shard_map/ppermute | solution.py:29
  83.8 1.1 %collective-permute-start.38 = (bf16[64,3712]{1,0:T(8,128)(2,1)S(1)}, bf16[64,3712]{1,0:T(8,128)(2,1)S(1)}, u32[]{:S(2)}, u32[]{:S(2)}) collective-permute-start(bf16[64,3712]{1,0:T(8,128)(2,1)S(1)} %constant_dynamic-update-slice_fusion.22.refs_4_), channel_id=1, source_target_pairs={{0,2},{1,17},{2,0},{3,19},{4,6},{5,21},{6,4},{7,23},{8,10},{9,25},... | collective-permute-start | bytes 1425416 | tf_op jit(solution)/shard_map/ppermute | solution.py:29
  84.9 9.0 %collective-permute-done.34.refs_1_ = bf16[64,3712]{1,0:T(8,128)(2,1)S(1)} collective-permute-done((bf16[64,3712]{1,0:T(8,128)(2,1)S(1)}, bf16[64,3712]{1,0:T(8,128)(2,1)S(1)}, u32[]{:S(2)}, u32[]{:S(2)}) %collective-permute-start.34) | collective-permute-done | bytes 475168 | tf_op jit(solution)/shard_map/ppermute | solution.py:29
  94.4 2.1 %collective-permute-done.32.refs_1_ = bf16[64,3712]{1,0:T(8,128)(2,1)S(1)} collective-permute-done((bf16[64,3712]{1,0:T(8,128)(2,1)S(1)}, bf16[64,3712]{1,0:T(8,128)(2,1)S(1)}, u32[]{:S(2)}, u32[]{:S(2)}) %collective-permute-start.32) | collective-permute-done | bytes 475168 | tf_op jit(solution)/shard_map/ppermute | solution.py:29
  96.5 2.5 %collective-permute-done.38.refs_5_ = bf16[64,3712]{1,0:T(8,128)(2,1)S(1)} collective-permute-done((bf16[64,3712]{1,0:T(8,128)(2,1)S(1)}, bf16[64,3712]{1,0:T(8,128)(2,1)S(1)}, u32[]{:S(2)}, u32[]{:S(2)}) %collective-permute-start.38) | collective-permute-done | bytes 475168 | tf_op jit(solution)/shard_map/ppermute | solution.py:29
  100.1 4.1 %apply_update.2.refs_8_ = bf16[256,14848]{1,0:T(8,128)(2,1)} custom-call(bf16[256,256]{1,0:T(8,128)(2,1)S(1)} %copy-done, s32[4,1,256]{2,1,0:T(1,128)S(1)} %copy-done.1, bf16[256,14848]{1,0:T(8,128)(2,1)S(1)} %bitcast.7, bf16[64,3712]{1,0:T(8,128)(2,1)S(1)} %constant_dynamic-update-slice_fusion.16.refs_0_, ...), custom_call_target="tpu_custom_call" | custom-call | flops 1024 | bytes 1024 | tf_op jit(solution)/shard_map/apply_update/pallas_call | solution.py:242
  104.2 4.1 %apply_update.3 = bf16[256,14848]{1,0:T(8,128)(2,1)} custom-call(bf16[256,256]{1,0:T(8,128)(2,1)S(1)} %copy-done, s32[4,1,256]{2,1,0:T(1,128)S(1)} %copy-done.1, bf16[256,14848]{1,0:T(8,128)(2,1)S(1)} %bitcast.7, bf16[64,3712]{1,0:T(8,128)(2,1)S(1)} %constant_dynamic-update-slice_fusion.20.refs_0_, ...), custom_call_target="tpu_custom_call", output_to_operand_aliasing={{}: (11, {})} | custom-call | flops 1024 | bytes 1024 | tf_op jit(solution)/shard_map/apply_update/pallas_call | solution.py:242
  (124 shorter events, 6.2 us)
Async XLA Ops:
  8.7 3.4 %collective-permute-start = (bf16[128,3712]{1,0:T(8,128)(2,1)}, bf16[128,3712]{1,0:T(8,128)(2,1)S(1)}, u32[]{:S(2)}, u32[]{:S(2)}) collective-permute-start(bf16[128,3712]{1,0:T(8,128)(2,1)} %get-tuple-element.131), channel_id=1, source_target_pairs={{0,1},{1,0},{2,3},{3,2},{4,5},{5,4},{6,7},{7,6},{8,9},{9,8},{10,11... | collective-permute-start | bytes 2850824 | tf_op jit(solution)/shard_map/ppermute | solution.py:29
  9.3 7.0 %collective-permute-start.5 = (bf16[128,3712]{1,0:T(8,128)(2,1)}, bf16[128,3712]{1,0:T(8,128)(2,1)}, u32[]{:S(2)}, u32[]{:S(2)}) collective-permute-start(bf16[128,3712]{1,0:T(8,128)(2,1)} %get-tuple-element.149), channel_id=1, source_target_pairs={{0,1},{1,0},{2,3},{3,2},{4,5},{5,4},{6,7},{7,6},{8,9},{9,8},{10,11... | collective-permute-start | bytes 2850824 | tf_op jit(solution)/shard_map/ppermute | solution.py:29
  9.3 9.9 %collective-permute-start.10 = (bf16[128,3712]{1,0:T(8,128)(2,1)}, bf16[128,3712]{1,0:T(8,128)(2,1)}, u32[]{:S(2)}, u32[]{:S(2)}) collective-permute-start(bf16[128,3712]{1,0:T(8,128)(2,1)} %get-tuple-element.167), channel_id=1, source_target_pairs={{0,1},{1,0},{2,3},{3,2},{4,5},{5,4},{6,7},{7,6},{8,9},{9,8},{10,11... | collective-permute-start | bytes 2850824 | tf_op jit(solution)/shard_map/ppermute | solution.py:29
  9.8 12.3 %collective-permute-start.18 = (bf16[128,3712]{1,0:T(8,128)(2,1)}, bf16[128,3712]{1,0:T(8,128)(2,1)}, u32[]{:S(2)}, u32[]{:S(2)}) collective-permute-start(bf16[128,3712]{1,0:T(8,128)(2,1)} %get-tuple-element.191), channel_id=1, source_target_pairs={{0,1},{1,0},{2,3},{3,2},{4,5},{5,4},{6,7},{7,6},{8,9},{9,8},{10,11... | collective-permute-start | bytes 2850824 | tf_op jit(solution)/shard_map/ppermute | solution.py:29
  13.3 15.4 %collective-permute-start.1 = (bf16[64,3712]{1,0:T(8,128)(2,1)S(1)}, bf16[64,3712]{1,0:T(8,128)(2,1)S(1)}, u32[]{:S(2)}, u32[]{:S(2)}) collective-permute-start(bf16[64,3712]{1,0:T(8,128)(2,1)S(1)} %add_convert_fusion.7), channel_id=1, source_target_pairs={{0,16},{1,5},{2,18},{3,7},{4,20},{5,1},{6,22},{7,3},{8,24},{9,13},... | collective-permute-start | bytes 1425416 | tf_op jit(solution)/shard_map/ppermute | solution.py:29
  17.6 11.7 %collective-permute-start.6 = (bf16[64,3712]{1,0:T(8,128)(2,1)S(1)}, bf16[64,3712]{1,0:T(8,128)(2,1)S(1)}, u32[]{:S(2)}, u32[]{:S(2)}) collective-permute-start(bf16[64,3712]{1,0:T(8,128)(2,1)S(1)} %add_convert_fusion.5), channel_id=1, source_target_pairs={{0,4},{1,3},{2,6},{3,1},{4,0},{5,7},{6,2},{7,5},{8,12},{9,11},{10,... | collective-permute-start | bytes 1425416 | tf_op jit(solution)/shard_map/ppermute | solution.py:29
  20.5 10.4 %collective-permute-start.11 = (bf16[64,3712]{1,0:T(8,128)(2,1)S(1)}, bf16[64,3712]{1,0:T(8,128)(2,1)S(1)}, u32[]{:S(2)}, u32[]{:S(2)}) collective-permute-start(bf16[64,3712]{1,0:T(8,128)(2,1)S(1)} %add_convert_fusion.3), channel_id=1, source_target_pairs={{0,2},{1,17},{2,0},{3,19},{4,6},{5,21},{6,4},{7,23},{8,10},{9,25},... | collective-permute-start | bytes 1425416 | tf_op jit(solution)/shard_map/ppermute | solution.py:29
  23.4 14.6 %collective-permute-start.19 = (bf16[64,3712]{1,0:T(8,128)(2,1)S(1)}, bf16[64,3712]{1,0:T(8,128)(2,1)S(1)}, u32[]{:S(2)}, u32[]{:S(2)}) collective-permute-start(bf16[64,3712]{1,0:T(8,128)(2,1)S(1)} %add_convert_fusion.1), channel_id=1, source_target_pairs={{0,2},{1,17},{2,0},{3,19},{4,6},{5,21},{6,4},{7,23},{8,10},{9,25},... | collective-permute-start | bytes 1425416 | tf_op jit(solution)/shard_map/ppermute | solution.py:29
  28.8 11.1 %collective-permute-start.2 = (bf16[32,3712]{1,0:T(8,128)(2,1)S(1)}, bf16[32,3712]{1,0:T(8,128)(2,1)S(1)}, u32[]{:S(2)}, u32[]{:S(2)}) collective-permute-start(bf16[32,3712]{1,0:T(8,128)(2,1)S(1)} %add_convert_fusion.15), channel_id=1, source_target_pairs={{0,4},{1,3},{2,6},{3,1},{4,0},{5,7},{6,2},{7,5},{8,12},{9,11},{10,... | collective-permute-start | bytes 712712 | tf_op jit(solution)/shard_map/ppermute | solution.py:29
  29.3 12.1 %collective-permute-start.7 = (bf16[32,3712]{1,0:T(8,128)(2,1)S(1)}, bf16[32,3712]{1,0:T(8,128)(2,1)S(1)}, u32[]{:S(2)}, u32[]{:S(2)}) collective-permute-start(bf16[32,3712]{1,0:T(8,128)(2,1)S(1)} %add_convert_fusion.13), channel_id=1, source_target_pairs={{0,2},{1,17},{2,0},{3,19},{4,6},{5,21},{6,4},{7,23},{8,10},{9,25},... | collective-permute-start | bytes 712712 | tf_op jit(solution)/shard_map/ppermute | solution.py:29
  31.0 11.2 %collective-permute-start.12 = (bf16[32,3712]{1,0:T(8,128)(2,1)S(1)}, bf16[32,3712]{1,0:T(8,128)(2,1)S(1)}, u32[]{:S(2)}, u32[]{:S(2)}) collective-permute-start(bf16[32,3712]{1,0:T(8,128)(2,1)S(1)} %add_convert_fusion.11), channel_id=1, source_target_pairs={{0,16},{1,5},{2,18},{3,7},{4,20},{5,1},{6,22},{7,3},{8,24},{9,13},... | collective-permute-start | bytes 712712 | tf_op jit(solution)/shard_map/ppermute | solution.py:29
  38.0 6.2 %collective-permute-start.20 = (bf16[32,3712]{1,0:T(8,128)(2,1)S(1)}, bf16[32,3712]{1,0:T(8,128)(2,1)S(1)}, u32[]{:S(2)}, u32[]{:S(2)}) collective-permute-start(bf16[32,3712]{1,0:T(8,128)(2,1)S(1)} %add_convert_fusion.9), channel_id=1, source_target_pairs={{0,16},{1,5},{2,18},{3,7},{4,20},{5,1},{6,22},{7,3},{8,24},{9,13},... | collective-permute-start | bytes 712712 | tf_op jit(solution)/shard_map/ppermute | solution.py:29
  39.9 6.1 %collective-permute-start.3 = (bf16[16,3712]{1,0:T(8,128)(2,1)S(1)}, bf16[16,3712]{1,0:T(8,128)(2,1)S(1)}, u32[]{:S(2)}, u32[]{:S(2)}) collective-permute-start(bf16[16,3712]{1,0:T(8,128)(2,1)S(1)} %add_convert_fusion.23), channel_id=1, source_target_pairs={{0,2},{1,17},{2,0},{3,19},{4,6},{5,21},{6,4},{7,23},{8,10},{9,25},... | collective-permute-start | bytes 356360 | tf_op jit(solution)/shard_map/ppermute | solution.py:29
  41.5 10.9 %collective-permute-start.8 = (bf16[16,3712]{1,0:T(8,128)(2,1)S(1)}, bf16[16,3712]{1,0:T(8,128)(2,1)S(1)}, u32[]{:S(2)}, u32[]{:S(2)}) collective-permute-start(bf16[16,3712]{1,0:T(8,128)(2,1)S(1)} %add_convert_fusion.21), channel_id=1, source_target_pairs={{0,16},{1,5},{2,18},{3,7},{4,20},{5,1},{6,22},{7,3},{8,24},{9,13},... | collective-permute-start | bytes 356360 | tf_op jit(solution)/shard_map/ppermute | solution.py:29
  42.2 6.6 %collective-permute-start.13 = (bf16[16,3712]{1,0:T(8,128)(2,1)S(1)}, bf16[16,3712]{1,0:T(8,128)(2,1)S(1)}, u32[]{:S(2)}, u32[]{:S(2)}) collective-permute-start(bf16[16,3712]{1,0:T(8,128)(2,1)S(1)} %add_convert_fusion.19), channel_id=1, source_target_pairs={{0,4},{1,3},{2,6},{3,1},{4,0},{5,7},{6,2},{7,5},{8,12},{9,11},{10,... | collective-permute-start | bytes 356360 | tf_op jit(solution)/shard_map/ppermute | solution.py:29
  44.2 5.9 %collective-permute-start.21 = (bf16[16,3712]{1,0:T(8,128)(2,1)S(1)}, bf16[16,3712]{1,0:T(8,128)(2,1)S(1)}, u32[]{:S(2)}, u32[]{:S(2)}) collective-permute-start(bf16[16,3712]{1,0:T(8,128)(2,1)S(1)} %add_convert_fusion.17), channel_id=1, source_target_pairs={{0,4},{1,3},{2,6},{3,1},{4,0},{5,7},{6,2},{7,5},{8,12},{9,11},{10,... | collective-permute-start | bytes 356360 | tf_op jit(solution)/shard_map/ppermute | solution.py:29
  46.0 13.7 %collective-permute-start.4 = (bf16[8,3712]{1,0:T(8,128)(2,1)S(1)}, bf16[8,3712]{1,0:T(8,128)(2,1)S(1)}, u32[]{:S(2)}, u32[]{:S(2)}) collective-permute-start(bf16[8,3712]{1,0:T(8,128)(2,1)S(1)} %add_convert_fusion.35), channel_id=1, source_target_pairs={{0,8},{1,9},{2,10},{3,11},{4,12},{5,13},{6,14},{7,15},{8,0},{9,1},... | collective-permute-start | bytes 178184 | tf_op jit(solution)/shard_map/ppermute | solution.py:29
  48.8 7.6 %collective-permute-start.14 = (bf16[8,3712]{1,0:T(8,128)(2,1)S(1)}, bf16[8,3712]{1,0:T(8,128)(2,1)S(1)}, u32[]{:S(2)}, u32[]{:S(2)}) collective-permute-start(bf16[8,3712]{1,0:T(8,128)(2,1)S(1)} %add_convert_fusion.31), channel_id=1, source_target_pairs={{0,8},{1,9},{2,10},{3,11},{4,12},{5,13},{6,14},{7,15},{8,0},{9,1},... | collective-permute-start | bytes 178184 | tf_op jit(solution)/shard_map/ppermute | solution.py:29
  50.2 49.9 %slice-start = ((s8[7602176]{0:T(1024)(128)(4,1)}), s8[4194304]{0:T(1024)(128)(4,1)S(1)}, s32[]{:S(2)}) async-start(s8[7602176]{0:T(1024)(128)(4,1)} %bitcast.6), calls=%async_computation | async-start | bytes 8388608
  50.2 49.8 %copy-start = (bf16[256,256]{1,0:T(8,128)(2,1)S(1)}, bf16[256,256]{1,0:T(8,128)(2,1)}, u32[]{:S(2)}) copy-start(bf16[256,256]{1,0:T(8,128)(2,1)} %projector_ref.3) | copy-start | bytes 393220
  50.2 49.8 %copy-start.1 = (s32[4,1,256]{2,1,0:T(1,128)S(1)}, s32[4,1,256]{2,1,0:T(1,128)}, u32[]{:S(2)}) copy-start(s32[4,1,256]{2,1,0:T(1,128)} %get-tuple-element.129.position_ref) | copy-start | bytes 12292
  50.2 12.6 %collective-permute-start.22 = (bf16[8,3712]{1,0:T(8,128)(2,1)S(1)}, bf16[8,3712]{1,0:T(8,128)(2,1)S(1)}, u32[]{:S(2)}, u32[]{:S(2)}) collective-permute-start(bf16[8,3712]{1,0:T(8,128)(2,1)S(1)} %add_convert_fusion.26), channel_id=1, source_target_pairs={{0,8},{1,9},{2,10},{3,11},{4,12},{5,13},{6,14},{7,15},{8,0},{9,1},... | collective-permute-start | bytes 178184 | tf_op jit(solution)/shard_map/ppermute | solution.py:29
  52.4 7.1 %collective-permute-start.9 = (bf16[8,3712]{1,0:T(8,128)(2,1)S(1)}, bf16[8,3712]{1,0:T(8,128)(2,1)S(1)}, u32[]{:S(2)}, u32[]{:S(2)}) collective-permute-start(bf16[8,3712]{1,0:T(8,128)(2,1)S(1)} %add_convert_fusion.33), channel_id=1, source_target_pairs={{0,8},{1,9},{2,10},{3,11},{4,12},{5,13},{6,14},{7,15},{8,0},{9,1},... | collective-permute-start | bytes 178184 | tf_op jit(solution)/shard_map/ppermute | solution.py:29
  56.5 8.0 %collective-permute-start.17 = (bf16[8,3712]{1,0:T(8,128)(2,1)S(1)}, bf16[8,3712]{1,0:T(8,128)(2,1)S(1)}, u32[]{:S(2)}, u32[]{:S(2)}) collective-permute-start(bf16[8,3712]{1,0:T(8,128)(2,1)S(1)} %get-tuple-element.210), channel_id=1, source_target_pairs={{0,8},{1,9},{2,10},{3,11},{4,12},{5,13},{6,14},{7,15},{8,0},{9,1},... | collective-permute-start | bytes 178184 | tf_op jit(solution)/shard_map/ppermute | solution.py:29
  59.7 7.8 %collective-permute-start.16 = (bf16[8,3712]{1,0:T(8,128)(2,1)S(1)}, bf16[8,3712]{1,0:T(8,128)(2,1)S(1)}, u32[]{:S(2)}, u32[]{:S(2)}) collective-permute-start(bf16[8,3712]{1,0:T(8,128)(2,1)S(1)} %get-tuple-element.212), channel_id=1, source_target_pairs={{0,8},{1,9},{2,10},{3,11},{4,12},{5,13},{6,14},{7,15},{8,0},{9,1},... | collective-permute-start | bytes 178184 | tf_op jit(solution)/shard_map/ppermute | solution.py:29
  59.9 9.3 %collective-permute-start.15 = (bf16[8,3712]{1,0:T(8,128)(2,1)S(1)}, bf16[8,3712]{1,0:T(8,128)(2,1)S(1)}, u32[]{:S(2)}, u32[]{:S(2)}) collective-permute-start(bf16[8,3712]{1,0:T(8,128)(2,1)S(1)} %get-tuple-element.214), channel_id=1, source_target_pairs={{0,8},{1,9},{2,10},{3,11},{4,12},{5,13},{6,14},{7,15},{8,0},{9,1},... | collective-permute-start | bytes 178184 | tf_op jit(solution)/shard_map/ppermute | solution.py:29
  62.9 7.3 %collective-permute-start.26 = (bf16[8,3712]{1,0:T(8,128)(2,1)S(1)}, bf16[8,3712]{1,0:T(8,128)(2,1)S(1)}, u32[]{:S(2)}, u32[]{:S(2)}) collective-permute-start(bf16[8,3712]{1,0:T(8,128)(2,1)S(1)} %get-tuple-element.216), channel_id=1, source_target_pairs={{0,8},{1,9},{2,10},{3,11},{4,12},{5,13},{6,14},{7,15},{8,0},{9,1},... | collective-permute-start | bytes 178184 | tf_op jit(solution)/shard_map/ppermute | solution.py:29
  63.0 15.7 %collective-permute-start.30 = (bf16[8,14848]{1,0:T(8,128)(2,1)S(1)}, bf16[8,14848]{1,0:T(8,128)(2,1)S(1)}, u32[]{:S(2)}, u32[]{:S(2)}) collective-permute-start(bf16[8,14848]{1,0:T(8,128)(2,1)S(1)} %pad_maximum_fusion), channel_id=1, source_target_pairs={{0,16},{1,17},{2,18},{3,19},{4,20},{5,21},{6,22},{7,23},{8,24},{9,... | collective-permute-start | bytes 712712 | tf_op jit(solution)/shard_map/ppermute | solution.py:29
  64.5 5.8 %collective-permute-start.25 = (bf16[16,3712]{1,0:T(8,128)(2,1)S(1)}, bf16[16,3712]{1,0:T(8,128)(2,1)S(1)}, u32[]{:S(2)}, u32[]{:S(2)}) collective-permute-start(bf16[16,3712]{1,0:T(8,128)(2,1)S(1)} %constant_dynamic-update-slice_fusion), channel_id=1, source_target_pairs={{0,4},{1,3},{2,6},{3,1},{4,0},{5,7},{6,2},{7,5},{8,12},{9,11},{10,... | collective-permute-start | bytes 356360 | tf_op jit(solution)/shard_map/ppermute | solution.py:29
  67.5 5.2 %collective-permute-start.24 = (bf16[16,3712]{1,0:T(8,128)(2,1)S(1)}, bf16[16,3712]{1,0:T(8,128)(2,1)S(1)}, u32[]{:S(2)}, u32[]{:S(2)}) collective-permute-start(bf16[16,3712]{1,0:T(8,128)(2,1)S(1)} %constant_dynamic-update-slice_fusion.2), channel_id=1, source_target_pairs={{0,16},{1,5},{2,18},{3,7},{4,20},{5,1},{6,22},{7,3},{8,24},{9,13},... | collective-permute-start | bytes 356360 | tf_op jit(solution)/shard_map/ppermute | solution.py:29
  69.2 5.2 %collective-permute-start.23 = (bf16[16,3712]{1,0:T(8,128)(2,1)S(1)}, bf16[16,3712]{1,0:T(8,128)(2,1)S(1)}, u32[]{:S(2)}, u32[]{:S(2)}) collective-permute-start(bf16[16,3712]{1,0:T(8,128)(2,1)S(1)} %constant_dynamic-update-slice_fusion.4), channel_id=1, source_target_pairs={{0,2},{1,17},{2,0},{3,19},{4,6},{5,21},{6,4},{7,23},{8,10},{9,25},... | collective-permute-start | bytes 356360 | tf_op jit(solution)/shard_map/ppermute | solution.py:29
  70.3 5.5 %collective-permute-start.31 = (bf16[16,3712]{1,0:T(8,128)(2,1)S(1)}, bf16[16,3712]{1,0:T(8,128)(2,1)S(1)}, u32[]{:S(2)}, u32[]{:S(2)}) collective-permute-start(bf16[16,3712]{1,0:T(8,128)(2,1)S(1)} %constant_dynamic-update-slice_fusion.6), channel_id=1, source_target_pairs={{0,4},{1,3},{2,6},{3,1},{4,0},{5,7},{6,2},{7,5},{8,12},{9,11},{10,... | collective-permute-start | bytes 356360 | tf_op jit(solution)/shard_map/ppermute | solution.py:29
  70.4 10.0 %collective-permute-start.29 = (bf16[32,3712]{1,0:T(8,128)(2,1)S(1)}, bf16[32,3712]{1,0:T(8,128)(2,1)S(1)}, u32[]{:S(2)}, u32[]{:S(2)}) collective-permute-start(bf16[32,3712]{1,0:T(8,128)(2,1)S(1)} %constant_dynamic-update-slice_fusion.8), channel_id=1, source_target_pairs={{0,16},{1,5},{2,18},{3,7},{4,20},{5,1},{6,22},{7,3},{8,24},{9,13},... | collective-permute-start | bytes 712712 | tf_op jit(solution)/shard_map/ppermute | solution.py:29
  72.8 7.7 %collective-permute-start.28 = (bf16[32,3712]{1,0:T(8,128)(2,1)S(1)}, bf16[32,3712]{1,0:T(8,128)(2,1)S(1)}, u32[]{:S(2)}, u32[]{:S(2)}) collective-permute-start(bf16[32,3712]{1,0:T(8,128)(2,1)S(1)} %constant_dynamic-update-slice_fusion.10), channel_id=1, source_target_pairs={{0,2},{1,17},{2,0},{3,19},{4,6},{5,21},{6,4},{7,23},{8,10},{9,25},... | collective-permute-start | bytes 712712 | tf_op jit(solution)/shard_map/ppermute | solution.py:29
  74.4 8.2 %collective-permute-start.27 = (bf16[32,3712]{1,0:T(8,128)(2,1)S(1)}, bf16[32,3712]{1,0:T(8,128)(2,1)S(1)}, u32[]{:S(2)}, u32[]{:S(2)}) collective-permute-start(bf16[32,3712]{1,0:T(8,128)(2,1)S(1)} %constant_dynamic-update-slice_fusion.12), channel_id=1, source_target_pairs={{0,4},{1,3},{2,6},{3,1},{4,0},{5,7},{6,2},{7,5},{8,12},{9,11},{10,... | collective-permute-start | bytes 712712 | tf_op jit(solution)/shard_map/ppermute | solution.py:29
  75.8 7.9 %collective-permute-start.35 = (bf16[32,3712]{1,0:T(8,128)(2,1)S(1)}, bf16[32,3712]{1,0:T(8,128)(2,1)S(1)}, u32[]{:S(2)}, u32[]{:S(2)}) collective-permute-start(bf16[32,3712]{1,0:T(8,128)(2,1)S(1)} %constant_dynamic-update-slice_fusion.14), channel_id=1, source_target_pairs={{0,16},{1,5},{2,18},{3,7},{4,20},{5,1},{6,22},{7,3},{8,24},{9,13},... | collective-permute-start | bytes 712712 | tf_op jit(solution)/shard_map/ppermute | solution.py:29
  80.5 18.7 %collective-permute-start.43 = (bf16[64,3712]{1,0:T(8,128)(2,1)S(1)}, bf16[64,3712]{1,0:T(8,128)(2,1)S(1)}, u32[]{:S(2)}, u32[]{:S(2)}) collective-permute-start(bf16[64,3712]{1,0:T(8,128)(2,1)S(1)} %constant_dynamic-update-slice_fusion.18.refs_4_), channel_id=1, source_target_pairs={{0,1},{1,0},{2,3},{3,2},{4,5},{5,4},{6,7},{7,6},{8,9},{9,8},{10,11... | collective-permute-start | bytes 1425416 | tf_op jit(solution)/shard_map/ppermute | solution.py:29
  80.6 13.3 %collective-permute-start.33 = (bf16[64,3712]{1,0:T(8,128)(2,1)S(1)}, bf16[64,3712]{1,0:T(8,128)(2,1)S(1)}, u32[]{:S(2)}, u32[]{:S(2)}) collective-permute-start(bf16[64,3712]{1,0:T(8,128)(2,1)S(1)} %constant_dynamic-update-slice_fusion.18.refs_4_), channel_id=1, source_target_pairs={{0,4},{1,3},{2,6},{3,1},{4,0},{5,7},{6,2},{7,5},{8,12},{9,11},{10,... | collective-permute-start | bytes 1425416 | tf_op jit(solution)/shard_map/ppermute | solution.py:29
  81.7 12.2 %collective-permute-start.34 = (bf16[64,3712]{1,0:T(8,128)(2,1)S(1)}, bf16[64,3712]{1,0:T(8,128)(2,1)S(1)}, u32[]{:S(2)}, u32[]{:S(2)}) collective-permute-start(bf16[64,3712]{1,0:T(8,128)(2,1)S(1)} %constant_dynamic-update-slice_fusion.16.refs_0_), channel_id=1, source_target_pairs={{0,2},{1,17},{2,0},{3,19},{4,6},{5,21},{6,4},{7,23},{8,10},{9,25},... | collective-permute-start | bytes 1425416 | tf_op jit(solution)/shard_map/ppermute | solution.py:29
  82.6 13.9 %collective-permute-start.32 = (bf16[64,3712]{1,0:T(8,128)(2,1)S(1)}, bf16[64,3712]{1,0:T(8,128)(2,1)S(1)}, u32[]{:S(2)}, u32[]{:S(2)}) collective-permute-start(bf16[64,3712]{1,0:T(8,128)(2,1)S(1)} %constant_dynamic-update-slice_fusion.20.refs_0_), channel_id=1, source_target_pairs={{0,16},{1,5},{2,18},{3,7},{4,20},{5,1},{6,22},{7,3},{8,24},{9,13},... | collective-permute-start | bytes 1425416 | tf_op jit(solution)/shard_map/ppermute | solution.py:29
  83.8 15.2 %collective-permute-start.38 = (bf16[64,3712]{1,0:T(8,128)(2,1)S(1)}, bf16[64,3712]{1,0:T(8,128)(2,1)S(1)}, u32[]{:S(2)}, u32[]{:S(2)}) collective-permute-start(bf16[64,3712]{1,0:T(8,128)(2,1)S(1)} %constant_dynamic-update-slice_fusion.22.refs_4_), channel_id=1, source_target_pairs={{0,2},{1,17},{2,0},{3,19},{4,6},{5,21},{6,4},{7,23},{8,10},{9,25},... | collective-permute-start | bytes 1425416 | tf_op jit(solution)/shard_map/ppermute | solution.py:29
  93.9 5.6 %collective-permute-start.41 = (bf16[64,3712]{1,0:T(8,128)(2,1)S(1)}, bf16[64,3712]{1,0:T(8,128)(2,1)S(1)}, u32[]{:S(2)}, u32[]{:S(2)}) collective-permute-start(bf16[64,3712]{1,0:T(8,128)(2,1)S(1)} %constant_dynamic-update-slice_fusion.16.refs_0_), channel_id=1, source_target_pairs={{0,1},{1,0},{2,3},{3,2},{4,5},{5,4},{6,7},{7,6},{8,9},{9,8},{10,11... | collective-permute-start | bytes 1425416 | tf_op jit(solution)/shard_map/ppermute | solution.py:29
  93.9 5.9 %collective-permute-start.44 = (bf16[64,3712]{1,0:T(8,128)(2,1)S(1)}, bf16[64,3712]{1,0:T(8,128)(2,1)S(1)}, u32[]{:S(2)}, u32[]{:S(2)}) collective-permute-start(bf16[64,3712]{1,0:T(8,128)(2,1)S(1)} %collective-permute-done.33.refs_5_), channel_id=1, source_target_pairs={{0,1},{1,0},{2,3},{3,2},{4,5},{5,4},{6,7},{7,6},{8,9},{9,8},{10,11... | collective-permute-start | bytes 1425416 | tf_op jit(solution)/shard_map/ppermute | solution.py:29
  96.5 3.5 %collective-permute-start.42 = (bf16[64,3712]{1,0:T(8,128)(2,1)S(1)}, bf16[64,3712]{1,0:T(8,128)(2,1)S(1)}, u32[]{:S(2)}, u32[]{:S(2)}) collective-permute-start(bf16[64,3712]{1,0:T(8,128)(2,1)S(1)} %collective-permute-done.34.refs_1_), channel_id=1, source_target_pairs={{0,1},{1,0},{2,3},{3,2},{4,5},{5,4},{6,7},{7,6},{8,9},{9,8},{10,11... | collective-permute-start | bytes 1425416 | tf_op jit(solution)/shard_map/ppermute | solution.py:29
  99.0 5.2 %collective-permute-start.39 = (bf16[64,3712]{1,0:T(8,128)(2,1)S(1)}, bf16[64,3712]{1,0:T(8,128)(2,1)S(1)}, u32[]{:S(2)}, u32[]{:S(2)}) collective-permute-start(bf16[64,3712]{1,0:T(8,128)(2,1)S(1)} %constant_dynamic-update-slice_fusion.22.refs_4_), channel_id=1, source_target_pairs={{0,1},{1,0},{2,3},{3,2},{4,5},{5,4},{6,7},{7,6},{8,9},{9,8},{10,11... | collective-permute-start | bytes 1425416 | tf_op jit(solution)/shard_map/ppermute | solution.py:29
  99.2 4.9 %collective-permute-start.36 = (bf16[64,3712]{1,0:T(8,128)(2,1)S(1)}, bf16[64,3712]{1,0:T(8,128)(2,1)S(1)}, u32[]{:S(2)}, u32[]{:S(2)}) collective-permute-start(bf16[64,3712]{1,0:T(8,128)(2,1)S(1)} %constant_dynamic-update-slice_fusion.20.refs_0_), channel_id=1, source_target_pairs={{0,1},{1,0},{2,3},{3,2},{4,5},{5,4},{6,7},{7,6},{8,9},{9,8},{10,11... | collective-permute-start | bytes 1425416 | tf_op jit(solution)/shard_map/ppermute | solution.py:29
  99.5 4.7 %collective-permute-start.40 = (bf16[64,3712]{1,0:T(8,128)(2,1)S(1)}, bf16[64,3712]{1,0:T(8,128)(2,1)S(1)}, u32[]{:S(2)}, u32[]{:S(2)}) collective-permute-start(bf16[64,3712]{1,0:T(8,128)(2,1)S(1)} %collective-permute-done.38.refs_5_), channel_id=1, source_target_pairs={{0,1},{1,0},{2,3},{3,2},{4,5},{5,4},{6,7},{7,6},{8,9},{9,8},{10,11... | collective-permute-start | bytes 1425416 | tf_op jit(solution)/shard_map/ppermute | solution.py:29
  99.8 4.4 %collective-permute-start.37 = (bf16[64,3712]{1,0:T(8,128)(2,1)S(1)}, bf16[64,3712]{1,0:T(8,128)(2,1)S(1)}, u32[]{:S(2)}, u32[]{:S(2)}) collective-permute-start(bf16[64,3712]{1,0:T(8,128)(2,1)S(1)} %collective-permute-done.32.refs_1_), channel_id=1, source_target_pairs={{0,1},{1,0},{2,3},{3,2},{4,5},{5,4},{6,7},{7,6},{8,9},{9,8},{10,11... | collective-permute-start | bytes 1425416 | tf_op jit(solution)/shard_map/ppermute | solution.py:29
  (5 other events, 123.8 us)

commit v4 on v3

--- a/solution.py
+++ b/solution.py
@@ -156,37 +156,16 @@
     return parts[: len(spans)], parts[len(spans) :], position
 
 
-def apply_kernel(chosen, spans, block_width, projector_ref, position_ref, weights_hbm, *refs):
+def apply_kernel(chosen, spans, block_width, projector_ref, position_ref, weights_ref, *refs):
     chain_count = len(spans)
     pieces = refs[: 4 * chain_count]
-    out_hbm, reordered_ref, weights_ref, direction_ref, out_ref, in_sems, out_sems = refs[-7:]
+    out_hbm, reordered_ref, out_ref, out_sems = refs[-4:]
     rank = projector_ref.shape[1]
-    quarter = rank // 4
     runs = [
         (chain, at, size)
         for chain, (start, count) in enumerate(spans)
         for at, size in pieces_of(start, count)
     ]
-
-    def incoming(index):
-        chain, at, size = runs[index]
-        slot = index % slots
-        columns = pl.ds(0, size * block_width)
-        source = pl.ds((at - spans[chain][0]) * block_width, size * block_width)
-        return [
-            pltpu.make_async_copy(
-                weights_hbm.at[:, pl.ds(at * block_width, size * block_width)],
-                weights_ref.at[slot, :, columns],
-                in_sems.at[slot, 4],
-            )
-        ] + [
-            pltpu.make_async_copy(
-                pieces[4 * chain + part].at[:, source],
-                direction_ref.at[slot, pl.ds(part * quarter, quarter), columns],
-                in_sems.at[slot, part],
-            )
-            for part in range(4)
-        ]
 
     def outgoing(index):
         _, at, size = runs[index]
@@ -197,9 +176,6 @@
             out_sems.at[slot],
         )
 
-    for index in range(min(slots - 1, len(runs))):
-        for copy in incoming(index):
-            copy.start()
     down = lax.broadcasted_iota(jnp.int32, (rank, rank), 0)
     for chain in range(chain_count):
         placing = (down == position_ref[chosen[chain]]).astype(jnp.bfloat16)
@@ -211,22 +187,18 @@
         ).astype(jnp.bfloat16)
     for index, (chain, at, size) in enumerate(runs):
         slot = index % slots
-        if index + slots - 1 < len(runs):
-            for copy in incoming(index + slots - 1):
-                copy.start()
-        for copy in incoming(index):
-            copy.wait()
         if index >= slots:
             outgoing(index - slots).wait()
         for block in range(0, size, 2):
             columns = slice(block * block_width, min(block + 2, size) * block_width)
-            change = jnp.dot(
-                reordered_ref[chain],
-                direction_ref[slot, :, columns],
-                preferred_element_type=jnp.float32,
+            here = slice(columns.start + at * block_width, columns.stop + at * block_width)
+            source = pl.ds(here.start - spans[chain][0] * block_width, here.stop - here.start)
+            direction = jnp.concatenate(
+                [piece[:, source] for piece in pieces[4 * chain : 4 * chain + 4]], axis=0
             )
+            change = jnp.dot(reordered_ref[chain], direction, preferred_element_type=jnp.float32)
             out_ref[slot, :, columns] = (
-                weights_ref[slot, :, columns].astype(jnp.float32) - update_scale * change
+                weights_ref[:, here].astype(jnp.float32) - update_scale * change
             ).astype(out_ref.dtype)
         outgoing(index).start()
     for index in range(max(0, len(runs) - slots), len(runs)):
@@ -241,16 +213,13 @@
     aliased = [] if so_far is None else [so_far]
     return pl.pallas_call(
         functools.partial(apply_kernel, chosen, spans, block_width),
-        in_specs=[whole, whole] + [anywhere] * (1 + len(pieces) + len(aliased)),
+        in_specs=[whole] * (3 + len(pieces)) + [anywhere] * len(aliased),
         out_specs=anywhere,
         input_output_aliases={3 + len(pieces): 0} if aliased else {},
         out_shape=jax.ShapeDtypeStruct(weights.shape, weights.dtype),
         scratch_shapes=[
             pltpu.VMEM((len(spans), rows, rank), jnp.bfloat16),
             pltpu.VMEM((slots, rows, longest), jnp.bfloat16),
-            pltpu.VMEM((slots, rank, longest), jnp.bfloat16),
-            pltpu.VMEM((slots, rows, longest), jnp.bfloat16),
-            pltpu.SemaphoreType.DMA((slots, 5)),
             pltpu.SemaphoreType.DMA((slots,)),
         ],
         compiler_params=pltpu.CompilerParams(vmem_limit_bytes=20 * 1024 * 1024),
@@ -375,7 +344,7 @@
         forwarded[i] = (mine, came, beside, swap(came, (0, 0)))
         last[0] = came
     new_weights = None
-    for chosen in ((0, 1), (2, 3)):
+    for chosen in ((0, 1, 2), (3,)):
         new_weights = last[0] = apply_update(
             projector,
             position,

time: 109 us -> 105 us (0.963)
  waiting for transfers between devices: 31.1 us -> 24.9 us
  starting transfers between devices: 46.8 us -> 51.8 us
  Pallas kernels: 16.2 us -> 13.8 us
    ppermute x45, waiting for transfers between devices: 31.1 us -> 24.9 us  [swap(): lax.ppermute(array, both, [(i, i ^ 1 << bits[i % 2]) for i in range(size)])]
    ppermute x45, starting transfers between devices: 46.8 us -> 51.8 us  [swap(): lax.ppermute(array, both, [(i, i ^ 1 << bits[i % 2]) for i in range(size)])]
    pallas_call x2, Pallas kernels: 8.13 us -> 5.73 us  [apply_update(): pl.pallas_call(functools.partial(apply_kernel, chosen, spans, block_width...]
  transfers between devices with their start and end apart: 45 -> 45, of which waited for: 10 -> 15; matrix products, arithmetic and copies ran while one was open for 12% -> 12% of each run, Pallas kernels for 4% -> 4%
where the time goes in v4:
time: 105 us
  starting transfers between devices  51.8 us (49%)
  waiting for transfers between devices  24.9 us (24%)
  Pallas kernels  13.8 us (13%)
  other arithmetic  12.6 us (12%)
  between operations  1.25 us (1%)
    ppermute x45, starting transfers between devices, swap(): lax.ppermute(array, both, [(i, i ^ 1 << bits[i % 2]) for i in range(size)])  51.8 us
    ppermute x45, waiting for transfers between devices, swap(): lax.ppermute(array, both, [(i, i ^ 1 << bits[i % 2]) for i in range(size)])  24.9 us
    convert_element_type x31, other arithmetic, added(): sum((term.astype(jnp.float32) for term in terms)).astype(jnp.bfloat16)  10.5 us
    pallas_call x1, Pallas kernels, prepare(): pl.pallas_call(functools.partial(prepare_kernel, spans, block_width, orde...  8.08 us
    pallas_call x2, Pallas kernels, apply_update(): pl.pallas_call(functools.partial(apply_kernel, chosen, spans, block_width...  5.73 us
  transfers between devices with their start and end apart: 45, of which 15 were waited for; matrix products, arithmetic and copies ran while one was open for 12% of the time, Pallas kernels for 4%

profile of v4, /device:TPU:0, one launch (start us, length us, event | category | flops | bytes accessed | tf_op | source)
XLA Modules:
  0.0 104.7 jit_solution(10256272452622901956)
XLA Ops:
  0.6 8.1 %prepare.1 = (bf16[128,3712]{1,0:T(8,128)(2,1)}, bf16[128,3712]{1,0:T(8,128)(2,1)}, bf16[128,3712]{1,0:T(8,128)(2,1)}, bf16[128,3712]{1,0:T(8,128)(2,1)}, bf16[1...) custom-call(s32[1]{0:T(128)} %bitcast.me_ref, ...), custom_call_target="tpu_custom_call" | custom-call | flops 1024 | bytes 1024 | tf_op jit(solution)/shard_map/prepare/pallas_call | solution.py:136
  9.9 2.3 %collective-permute-done = bf16[128,3712]{1,0:T(8,128)(2,1)S(1)} collective-permute-done((bf16[128,3712]{1,0:T(8,128)(2,1)}, bf16[128,3712]{1,0:T(8,128)(2,1)S(1)}, u32[]{:S(2)}, u32[]{:S(2)}) %collective-permute-start) | collective-permute-done | bytes 950304 | tf_op jit(solution)/shard_map/ppermute | solution.py:29
  12.2 1.1 %add_convert_fusion.7 = bf16[64,3712]{1,0:T(8,128)(2,1)S(1)} fusion(bf16[128,3712]{1,0:T(8,128)(2,1)S(1)} %collective-permute-done, bf16[128,3712]{1,0:T(8,128)(2,1)} %get-tuple-element.134), kind=kLoop, calls=%fused_computation.11 | loop fusion | flops 950272 | bytes 1425408 | tf_op jit(solution)/shard_map/convert_element_type | solution.py:232
  13.3 2.9 %collective-permute-start.1 = (bf16[64,3712]{1,0:T(8,128)(2,1)S(1)}, bf16[64,3712]{1,0:T(8,128)(2,1)S(1)}, u32[]{:S(2)}, u32[]{:S(2)}) collective-permute-start(bf16[64,3712]{1,0:T(8,128)(2,1)S(1)} %add_convert_fusion.7), channel_id=1, source_target_pairs={{0,2},{1,17},{2,0},{3,19},{4,6},{5,21},{6,4},{7,23},{8,10},{9,25},... | collective-permute-start | bytes 1425416 | tf_op jit(solution)/shard_map/ppermute | solution.py:29
  16.3 1.3 %add_convert_fusion.5 = bf16[64,3712]{1,0:T(8,128)(2,1)S(1)} fusion(bf16[128,3712]{1,0:T(8,128)(2,1)} %collective-permute-done.5, bf16[128,3712]{1,0:T(8,128)(2,1)} %get-tuple-element.152), kind=kLoop, calls=%fused_computation.9 | loop fusion | flops 950272 | bytes 1425408 | tf_op jit(solution)/shard_map/convert_element_type | solution.py:232
  17.5 1.6 %collective-permute-start.6 = (bf16[64,3712]{1,0:T(8,128)(2,1)S(1)}, bf16[64,3712]{1,0:T(8,128)(2,1)S(1)}, u32[]{:S(2)}, u32[]{:S(2)}) collective-permute-start(bf16[64,3712]{1,0:T(8,128)(2,1)S(1)} %add_convert_fusion.5), channel_id=1, source_target_pairs={{0,16},{1,5},{2,18},{3,7},{4,20},{5,1},{6,22},{7,3},{8,24},{9,13},... | collective-permute-start | bytes 1425416 | tf_op jit(solution)/shard_map/ppermute | solution.py:29
  19.1 1.3 %add_convert_fusion.3 = bf16[64,3712]{1,0:T(8,128)(2,1)S(1)} fusion(bf16[128,3712]{1,0:T(8,128)(2,1)} %collective-permute-done.10, bf16[128,3712]{1,0:T(8,128)(2,1)} %get-tuple-element.170), kind=kLoop, calls=%fused_computation.7 | loop fusion | flops 950272 | bytes 1425408 | tf_op jit(solution)/shard_map/convert_element_type | solution.py:232
  20.4 1.6 %collective-permute-start.11 = (bf16[64,3712]{1,0:T(8,128)(2,1)S(1)}, bf16[64,3712]{1,0:T(8,128)(2,1)S(1)}, u32[]{:S(2)}, u32[]{:S(2)}) collective-permute-start(bf16[64,3712]{1,0:T(8,128)(2,1)S(1)} %add_convert_fusion.3), channel_id=1, source_target_pairs={{0,4},{1,3},{2,6},{3,1},{4,0},{5,7},{6,2},{7,5},{8,12},{9,11},{10,... | collective-permute-start | bytes 1425416 | tf_op jit(solution)/shard_map/ppermute | solution.py:29
  22.1 1.3 %add_convert_fusion.1 = bf16[64,3712]{1,0:T(8,128)(2,1)S(1)} fusion(bf16[128,3712]{1,0:T(8,128)(2,1)} %collective-permute-done.15, bf16[128,3712]{1,0:T(8,128)(2,1)} %get-tuple-element.188), kind=kLoop, calls=%fused_computation.5 | loop fusion | flops 950272 | bytes 1425408 | tf_op jit(solution)/shard_map/convert_element_type | solution.py:232
  23.4 0.6 collective-permute-start.16
  24.0 1.1 %add_convert_fusion.6 = bf16[64,3712]{1,0:T(8,128)(2,1)S(1)} fusion(bf16[128,3712]{1,0:T(8,128)(2,1)S(1)} %collective-permute-done, bf16[128,3712]{1,0:T(8,128)(2,1)} %get-tuple-element.134), kind=kLoop, calls=%fused_computation.10 | loop fusion | flops 950272 | bytes 1425408 | tf_op jit(solution)/shard_map/convert_element_type | solution.py:232
  25.1 1.3 %add_convert_fusion.4 = bf16[64,3712]{1,0:T(8,128)(2,1)S(1)} fusion(bf16[128,3712]{1,0:T(8,128)(2,1)} %collective-permute-done.5, bf16[128,3712]{1,0:T(8,128)(2,1)} %get-tuple-element.152), kind=kLoop, calls=%fused_computation.8 | loop fusion | flops 950272 | bytes 1425408 | tf_op jit(solution)/shard_map/convert_element_type | solution.py:232
  26.4 1.1 %add_convert_fusion.2 = bf16[64,3712]{1,0:T(8,128)(2,1)S(1)} fusion(bf16[128,3712]{1,0:T(8,128)(2,1)} %collective-permute-done.10, bf16[128,3712]{1,0:T(8,128)(2,1)S(1)} %copy-done.5), kind=kLoop, calls=%fused_computation.6 | loop fusion | flops 950272 | bytes 1425408 | tf_op jit(solution)/shard_map/convert_element_type | solution.py:232
  27.5 1.1 %add_convert_fusion = bf16[64,3712]{1,0:T(8,128)(2,1)S(1)} fusion(bf16[128,3712]{1,0:T(8,128)(2,1)} %collective-permute-done.15, bf16[128,3712]{1,0:T(8,128)(2,1)S(1)} %copy-done.4), kind=kLoop, calls=%fused_computation.4 | loop fusion | flops 950272 | bytes 1425408 | tf_op jit(solution)/shard_map/convert_element_type | solution.py:232
  29.3 0.7 collective-permute-done.6
  30.1 2.7 %collective-permute-start.7 = (bf16[32,3712]{1,0:T(8,128)(2,1)S(1)}, bf16[32,3712]{1,0:T(8,128)(2,1)S(1)}, u32[]{:S(2)}, u32[]{:S(2)}) collective-permute-start(bf16[32,3712]{1,0:T(8,128)(2,1)S(1)} %add_convert_fusion.13), channel_id=1, source_target_pairs={{0,4},{1,3},{2,6},{3,1},{4,0},{5,7},{6,2},{7,5},{8,12},{9,11},{10,... | collective-permute-start | bytes 712712 | tf_op jit(solution)/shard_map/ppermute | solution.py:29
  32.9 0.9 collective-permute-start.12
  33.8 1.4 %collective-permute-done.16 = bf16[64,3712]{1,0:T(8,128)(2,1)S(1)} collective-permute-done((bf16[64,3712]{1,0:T(8,128)(2,1)S(1)}, bf16[64,3712]{1,0:T(8,128)(2,1)S(1)}, u32[]{:S(2)}, u32[]{:S(2)}) %collective-permute-start.16) | collective-permute-done | bytes 475168 | tf_op jit(solution)/shard_map/ppermute | solution.py:29
  35.3 2.5 %collective-permute-start.17 = (bf16[32,3712]{1,0:T(8,128)(2,1)S(1)}, bf16[32,3712]{1,0:T(8,128)(2,1)S(1)}, u32[]{:S(2)}, u32[]{:S(2)}) collective-permute-start(bf16[32,3712]{1,0:T(8,128)(2,1)S(1)} %add_convert_fusion.9), channel_id=1, source_target_pairs={{0,16},{1,5},{2,18},{3,7},{4,20},{5,1},{6,22},{7,3},{8,24},{9,13},... | collective-permute-start | bytes 712712 | tf_op jit(solution)/shard_map/ppermute | solution.py:29
  38.1 1.6 %collective-permute-start.3 = (bf16[16,3712]{1,0:T(8,128)(2,1)S(1)}, bf16[16,3712]{1,0:T(8,128)(2,1)S(1)}, u32[]{:S(2)}, u32[]{:S(2)}) collective-permute-start(bf16[16,3712]{1,0:T(8,128)(2,1)S(1)} %add_convert_fusion.23), channel_id=1, source_target_pairs={{0,4},{1,3},{2,6},{3,1},{4,0},{5,7},{6,2},{7,5},{8,12},{9,11},{10,... | collective-permute-start | bytes 356360 | tf_op jit(solution)/shard_map/ppermute | solution.py:29
  39.8 1.6 %collective-permute-start.8 = (bf16[16,3712]{1,0:T(8,128)(2,1)S(1)}, bf16[16,3712]{1,0:T(8,128)(2,1)S(1)}, u32[]{:S(2)}, u32[]{:S(2)}) collective-permute-start(bf16[16,3712]{1,0:T(8,128)(2,1)S(1)} %add_convert_fusion.21), channel_id=1, source_target_pairs={{0,2},{1,17},{2,0},{3,19},{4,6},{5,21},{6,4},{7,23},{8,10},{9,25},... | collective-permute-start | bytes 356360 | tf_op jit(solution)/shard_map/ppermute | solution.py:29
  41.5 1.6 %collective-permute-done.17 = bf16[32,3712]{1,0:T(8,128)(2,1)S(1)} collective-permute-done((bf16[32,3712]{1,0:T(8,128)(2,1)S(1)}, bf16[32,3712]{1,0:T(8,128)(2,1)S(1)}, u32[]{:S(2)}, u32[]{:S(2)}) %collective-permute-start.17) | collective-permute-done | bytes 237600 | tf_op jit(solution)/shard_map/ppermute | solution.py:29
  43.1 1.8 %collective-permute-start.18 = (bf16[16,3712]{1,0:T(8,128)(2,1)S(1)}, bf16[16,3712]{1,0:T(8,128)(2,1)S(1)}, u32[]{:S(2)}, u32[]{:S(2)}) collective-permute-start(bf16[16,3712]{1,0:T(8,128)(2,1)S(1)} %add_convert_fusion.17), channel_id=1, source_target_pairs={{0,4},{1,3},{2,6},{3,1},{4,0},{5,7},{6,2},{7,5},{8,12},{9,11},{10,... | collective-permute-start | bytes 356360 | tf_op jit(solution)/shard_map/ppermute | solution.py:29
  45.1 2.7 %collective-permute-start.4 = (bf16[8,3712]{1,0:T(8,128)(2,1)S(1)}, bf16[8,3712]{1,0:T(8,128)(2,1)S(1)}, u32[]{:S(2)}, u32[]{:S(2)}) collective-permute-start(bf16[8,3712]{1,0:T(8,128)(2,1)S(1)} %add_convert_fusion.35), channel_id=1, source_target_pairs={{0,8},{1,9},{2,10},{3,11},{4,12},{5,13},{6,14},{7,15},{8,0},{9,1},... | collective-permute-start | bytes 178184 | tf_op jit(solution)/shard_map/ppermute | solution.py:29
  48.7 3.3 %collective-permute-start.19 = (bf16[8,3712]{1,0:T(8,128)(2,1)S(1)}, bf16[8,3712]{1,0:T(8,128)(2,1)S(1)}, u32[]{:S(2)}, u32[]{:S(2)}) collective-permute-start(bf16[8,3712]{1,0:T(8,128)(2,1)S(1)} %add_convert_fusion.29), channel_id=1, source_target_pairs={{0,8},{1,9},{2,10},{3,11},{4,12},{5,13},{6,14},{7,15},{8,0},{9,1},... | collective-permute-start | bytes 178184 | tf_op jit(solution)/shard_map/ppermute | solution.py:29
  52.1 3.8 %collective-permute-done.19 = bf16[8,3712]{1,0:T(8,128)(2,1)S(1)} collective-permute-done((bf16[8,3712]{1,0:T(8,128)(2,1)S(1)}, bf16[8,3712]{1,0:T(8,128)(2,1)S(1)}, u32[]{:S(2)}, u32[]{:S(2)}) %collective-permute-start.19) | collective-permute-done | bytes 59424 | tf_op jit(solution)/shard_map/ppermute | solution.py:29
  56.0 1.2 %collective-permute-start.23 = (bf16[8,3712]{1,0:T(8,128)(2,1)S(1)}, bf16[8,3712]{1,0:T(8,128)(2,1)S(1)}, u32[]{:S(2)}, u32[]{:S(2)}) collective-permute-start(bf16[8,3712]{1,0:T(8,128)(2,1)S(1)} %get-tuple-element.210), channel_id=1, source_target_pairs={{0,8},{1,9},{2,10},{3,11},{4,12},{5,13},{6,14},{7,15},{8,0},{9,1},... | collective-permute-start | bytes 178184 | tf_op jit(solution)/shard_map/ppermute | solution.py:29
  57.2 1.5 %collective-permute-done.14 = bf16[8,3712]{1,0:T(8,128)(2,1)S(1)} collective-permute-done((bf16[8,3712]{1,0:T(8,128)(2,1)S(1)}, bf16[8,3712]{1,0:T(8,128)(2,1)S(1)}, u32[]{:S(2)}, u32[]{:S(2)}) %collective-permute-start.14) | collective-permute-done | bytes 59424 | tf_op jit(solution)/shard_map/ppermute | solution.py:29
  59.3 2.7 %collective-permute-start.21 = (bf16[8,3712]{1,0:T(8,128)(2,1)S(1)}, bf16[8,3712]{1,0:T(8,128)(2,1)S(1)}, u32[]{:S(2)}, u32[]{:S(2)}) collective-permute-start(bf16[8,3712]{1,0:T(8,128)(2,1)S(1)} %get-tuple-element.214), channel_id=1, source_target_pairs={{0,8},{1,9},{2,10},{3,11},{4,12},{5,13},{6,14},{7,15},{8,0},{9,1},... | collective-permute-start | bytes 178184 | tf_op jit(solution)/shard_map/ppermute | solution.py:29
  62.5 3.9 %collective-permute-start.32 = (bf16[8,14848]{1,0:T(8,128)(2,1)S(1)}, bf16[8,14848]{1,0:T(8,128)(2,1)S(1)}, u32[]{:S(2)}, u32[]{:S(2)}) collective-permute-start(bf16[8,14848]{1,0:T(8,128)(2,1)S(1)} %pad_maximum_fusion), channel_id=1, source_target_pairs={{0,16},{1,17},{2,18},{3,19},{4,20},{5,21},{6,22},{7,23},{8,24},{9,... | collective-permute-start | bytes 712712 | tf_op jit(solution)/shard_map/ppermute | solution.py:29
  66.4 1.1 %collective-permute-start.27 = (bf16[16,3712]{1,0:T(8,128)(2,1)S(1)}, bf16[16,3712]{1,0:T(8,128)(2,1)S(1)}, u32[]{:S(2)}, u32[]{:S(2)}) collective-permute-start(bf16[16,3712]{1,0:T(8,128)(2,1)S(1)} %constant_dynamic-update-slice_fusion), channel_id=1, source_target_pairs={{0,4},{1,3},{2,6},{3,1},{4,0},{5,7},{6,2},{7,5},{8,12},{9,11},{10,... | collective-permute-start | bytes 356360 | tf_op jit(solution)/shard_map/ppermute | solution.py:29
  67.8 2.6 %collective-permute-start.25 = (bf16[16,3712]{1,0:T(8,128)(2,1)S(1)}, bf16[16,3712]{1,0:T(8,128)(2,1)S(1)}, u32[]{:S(2)}, u32[]{:S(2)}) collective-permute-start(bf16[16,3712]{1,0:T(8,128)(2,1)S(1)} %constant_dynamic-update-slice_fusion.4), channel_id=1, source_target_pairs={{0,2},{1,17},{2,0},{3,19},{4,6},{5,21},{6,4},{7,23},{8,10},{9,25},... | collective-permute-start | bytes 356360 | tf_op jit(solution)/shard_map/ppermute | solution.py:29
  70.5 1.9 %collective-permute-done.27 = bf16[16,3712]{1,0:T(8,128)(2,1)S(1)} collective-permute-done((bf16[16,3712]{1,0:T(8,128)(2,1)S(1)}, bf16[16,3712]{1,0:T(8,128)(2,1)S(1)}, u32[]{:S(2)}, u32[]{:S(2)}) %collective-permute-start.27) | collective-permute-done | bytes 118816 | tf_op jit(solution)/shard_map/ppermute | solution.py:29
  72.7 2.0 %collective-permute-done.26 = bf16[16,3712]{1,0:T(8,128)(2,1)S(1)} collective-permute-done((bf16[16,3712]{1,0:T(8,128)(2,1)S(1)}, bf16[16,3712]{1,0:T(8,128)(2,1)S(1)}, u32[]{:S(2)}, u32[]{:S(2)}) %collective-permute-start.26) | collective-permute-done | bytes 118816 | tf_op jit(solution)/shard_map/ppermute | solution.py:29
  74.7 1.0 collective-permute-start.30
  75.8 2.4 %collective-permute-start.29 = (bf16[32,3712]{1,0:T(8,128)(2,1)S(1)}, bf16[32,3712]{1,0:T(8,128)(2,1)S(1)}, u32[]{:S(2)}, u32[]{:S(2)}) collective-permute-start(bf16[32,3712]{1,0:T(8,128)(2,1)S(1)} %constant_dynamic-update-slice_fusion.12), channel_id=1, source_target_pairs={{0,4},{1,3},{2,6},{3,1},{4,0},{5,7},{6,2},{7,5},{8,12},{9,11},{10,... | collective-permute-start | bytes 712712 | tf_op jit(solution)/shard_map/ppermute | solution.py:29
  78.2 2.2 %collective-permute-start.28 = (bf16[32,3712]{1,0:T(8,128)(2,1)S(1)}, bf16[32,3712]{1,0:T(8,128)(2,1)S(1)}, u32[]{:S(2)}, u32[]{:S(2)}) collective-permute-start(bf16[32,3712]{1,0:T(8,128)(2,1)S(1)} %constant_dynamic-update-slice_fusion.14), channel_id=1, source_target_pairs={{0,16},{1,5},{2,18},{3,7},{4,20},{5,1},{6,22},{7,3},{8,24},{9,13},... | collective-permute-start | bytes 712712 | tf_op jit(solution)/shard_map/ppermute | solution.py:29
  80.5 1.5 %fusion.1 = (f32[16,14848]{1,0:T(8,128)}, f32[16,14848]{1,0:T(8,128)}) fusion(bf16[16,14848]{1,0:T(8,128)(2,1)S(1)} %maximum_select_fusion, f32[16,14848]{1,0:T(8,128)S(1)} %copy-done.2, f32[16,14848]{1,0:T(8,128)S(1)} %copy-done.3), kind=kLoop, calls=%fused_computation.3 | loop fusion | flops 1900544 | bytes 4276224 | tf_op jit(solution)/shard_map/add | solution.py:237
  82.1 0.9 collective-permute-start.36
  83.4 2.0 %collective-permute-start.35 = (bf16[64,3712]{1,0:T(8,128)(2,1)S(1)}, bf16[64,3712]{1,0:T(8,128)(2,1)S(1)}, u32[]{:S(2)}, u32[]{:S(2)}) collective-permute-start(bf16[64,3712]{1,0:T(8,128)(2,1)S(1)} %constant_dynamic-update-slice_fusion.18.refs_4_), channel_id=1, source_target_pairs={{0,4},{1,3},{2,6},{3,1},{4,0},{5,7},{6,2},{7,5},{8,12},{9,11},{10,... | collective-permute-start | bytes 1425416 | tf_op jit(solution)/shard_map/ppermute | solution.py:29
  85.4 1.7 %collective-permute-start.34 = (bf16[64,3712]{1,0:T(8,128)(2,1)S(1)}, bf16[64,3712]{1,0:T(8,128)(2,1)S(1)}, u32[]{:S(2)}, u32[]{:S(2)}) collective-permute-start(bf16[64,3712]{1,0:T(8,128)(2,1)S(1)} %constant_dynamic-update-slice_fusion.20.refs_8_), channel_id=1, source_target_pairs={{0,16},{1,5},{2,18},{3,7},{4,20},{5,1},{6,22},{7,3},{8,24},{9,13},... | collective-permute-start | bytes 1425416 | tf_op jit(solution)/shard_map/ppermute | solution.py:29
  87.2 1.3 %collective-permute-start.33 = (bf16[64,3712]{1,0:T(8,128)(2,1)S(1)}, bf16[64,3712]{1,0:T(8,128)(2,1)S(1)}, u32[]{:S(2)}, u32[]{:S(2)}) collective-permute-start(bf16[64,3712]{1,0:T(8,128)(2,1)S(1)} %constant_dynamic-update-slice_fusion.22.refs_0_), channel_id=1, source_target_pairs={{0,2},{1,17},{2,0},{3,19},{4,6},{5,21},{6,4},{7,23},{8,10},{9,25},... | collective-permute-start | bytes 1425416 | tf_op jit(solution)/shard_map/ppermute | solution.py:29
  88.5 3.6 %collective-permute-done.35.refs_5_ = bf16[64,3712]{1,0:T(8,128)(2,1)S(1)} collective-permute-done((bf16[64,3712]{1,0:T(8,128)(2,1)S(1)}, bf16[64,3712]{1,0:T(8,128)(2,1)S(1)}, u32[]{:S(2)}, u32[]{:S(2)}) %collective-permute-start.35) | collective-permute-done | bytes 475168 | tf_op jit(solution)/shard_map/ppermute | solution.py:29
  92.6 2.9 %collective-permute-done.34.refs_9_ = bf16[64,3712]{1,0:T(8,128)(2,1)S(1)} collective-permute-done((bf16[64,3712]{1,0:T(8,128)(2,1)S(1)}, bf16[64,3712]{1,0:T(8,128)(2,1)S(1)}, u32[]{:S(2)}, u32[]{:S(2)}) %collective-permute-start.34) | collective-permute-done | bytes 475168 | tf_op jit(solution)/shard_map/ppermute | solution.py:29
  96.9 1.1 %collective-permute-done.44.refs_11_ = bf16[64,3712]{1,0:T(8,128)(2,1)S(1)} collective-permute-done((bf16[64,3712]{1,0:T(8,128)(2,1)S(1)}, bf16[64,3712]{1,0:T(8,128)(2,1)S(1)}, u32[]{:S(2)}, u32[]{:S(2)}) %collective-permute-start.44) | collective-permute-done | bytes 475168 | tf_op jit(solution)/shard_map/ppermute | solution.py:29
  98.1 0.7 collective-permute-done.40.refs_3_
  98.8 3.8 %apply_update.2.refs_4_ = bf16[256,14848]{1,0:T(8,128)(2,1)} custom-call(bf16[256,256]{1,0:T(8,128)(2,1)S(1)} %copy-done, s32[4,1,256]{2,1,0:T(1,128)S(1)} %copy-done.1, bf16[256,14848]{1,0:T(8,128)(2,1)S(1)} %bitcast.7, bf16[64,3712]{1,0:T(8,128)(2,1)S(1)} %constant_dynamic-update-slice_fusion.16.refs_0_, ...), custom_call_target="tpu_custom_call" | custom-call | flops 1024 | bytes 1024 | tf_op jit(solution)/shard_map/apply_update/pallas_call | solution.py:214
  102.6 1.9 %apply_update.3 = bf16[256,14848]{1,0:T(8,128)(2,1)} custom-call(bf16[256,256]{1,0:T(8,128)(2,1)S(1)} %copy-done, s32[4,1,256]{2,1,0:T(1,128)S(1)} %copy-done.1, bf16[256,14848]{1,0:T(8,128)(2,1)S(1)} %bitcast.7, bf16[64,3712]{1,0:T(8,128)(2,1)S(1)} %constant_dynamic-update-slice_fusion.22.refs_0_, ...), custom_call_target="tpu_custom_call", output_to_operand_aliasing={{}: (7, {})} | custom-call | flops 1024 | bytes 1024 | tf_op jit(solution)/shard_map/apply_update/pallas_call | solution.py:214
  (124 shorter events, 8.1 us)
Async XLA Ops:
  8.7 3.4 %collective-permute-start = (bf16[128,3712]{1,0:T(8,128)(2,1)}, bf16[128,3712]{1,0:T(8,128)(2,1)S(1)}, u32[]{:S(2)}, u32[]{:S(2)}) collective-permute-start(bf16[128,3712]{1,0:T(8,128)(2,1)} %get-tuple-element.131), channel_id=1, source_target_pairs={{0,1},{1,0},{2,3},{3,2},{4,5},{5,4},{6,7},{7,6},{8,9},{9,8},{10,11... | collective-permute-start | bytes 2850824 | tf_op jit(solution)/shard_map/ppermute | solution.py:29
  9.3 7.0 %collective-permute-start.5 = (bf16[128,3712]{1,0:T(8,128)(2,1)}, bf16[128,3712]{1,0:T(8,128)(2,1)}, u32[]{:S(2)}, u32[]{:S(2)}) collective-permute-start(bf16[128,3712]{1,0:T(8,128)(2,1)} %get-tuple-element.149), channel_id=1, source_target_pairs={{0,1},{1,0},{2,3},{3,2},{4,5},{5,4},{6,7},{7,6},{8,9},{9,8},{10,11... | collective-permute-start | bytes 2850824 | tf_op jit(solution)/shard_map/ppermute | solution.py:29
  9.3 9.8 %collective-permute-start.10 = (bf16[128,3712]{1,0:T(8,128)(2,1)}, bf16[128,3712]{1,0:T(8,128)(2,1)}, u32[]{:S(2)}, u32[]{:S(2)}) collective-permute-start(bf16[128,3712]{1,0:T(8,128)(2,1)} %get-tuple-element.167), channel_id=1, source_target_pairs={{0,1},{1,0},{2,3},{3,2},{4,5},{5,4},{6,7},{7,6},{8,9},{9,8},{10,11... | collective-permute-start | bytes 2850824 | tf_op jit(solution)/shard_map/ppermute | solution.py:29
  9.8 12.3 %collective-permute-start.15 = (bf16[128,3712]{1,0:T(8,128)(2,1)}, bf16[128,3712]{1,0:T(8,128)(2,1)}, u32[]{:S(2)}, u32[]{:S(2)}) collective-permute-start(bf16[128,3712]{1,0:T(8,128)(2,1)} %get-tuple-element.185), channel_id=1, source_target_pairs={{0,1},{1,0},{2,3},{3,2},{4,5},{5,4},{6,7},{7,6},{8,9},{9,8},{10,11... | collective-permute-start | bytes 2850824 | tf_op jit(solution)/shard_map/ppermute | solution.py:29
  13.3 15.4 %collective-permute-start.1 = (bf16[64,3712]{1,0:T(8,128)(2,1)S(1)}, bf16[64,3712]{1,0:T(8,128)(2,1)S(1)}, u32[]{:S(2)}, u32[]{:S(2)}) collective-permute-start(bf16[64,3712]{1,0:T(8,128)(2,1)S(1)} %add_convert_fusion.7), channel_id=1, source_target_pairs={{0,2},{1,17},{2,0},{3,19},{4,6},{5,21},{6,4},{7,23},{8,10},{9,25},... | collective-permute-start | bytes 1425416 | tf_op jit(solution)/shard_map/ppermute | solution.py:29
  17.5 12.5 %collective-permute-start.6 = (bf16[64,3712]{1,0:T(8,128)(2,1)S(1)}, bf16[64,3712]{1,0:T(8,128)(2,1)S(1)}, u32[]{:S(2)}, u32[]{:S(2)}) collective-permute-start(bf16[64,3712]{1,0:T(8,128)(2,1)S(1)} %add_convert_fusion.5), channel_id=1, source_target_pairs={{0,16},{1,5},{2,18},{3,7},{4,20},{5,1},{6,22},{7,3},{8,24},{9,13},... | collective-permute-start | bytes 1425416 | tf_op jit(solution)/shard_map/ppermute | solution.py:29
  20.4 12.4 %collective-permute-start.11 = (bf16[64,3712]{1,0:T(8,128)(2,1)S(1)}, bf16[64,3712]{1,0:T(8,128)(2,1)S(1)}, u32[]{:S(2)}, u32[]{:S(2)}) collective-permute-start(bf16[64,3712]{1,0:T(8,128)(2,1)S(1)} %add_convert_fusion.3), channel_id=1, source_target_pairs={{0,4},{1,3},{2,6},{3,1},{4,0},{5,7},{6,2},{7,5},{8,12},{9,11},{10,... | collective-permute-start | bytes 1425416 | tf_op jit(solution)/shard_map/ppermute | solution.py:29
  23.4 11.8 %collective-permute-start.16 = (bf16[64,3712]{1,0:T(8,128)(2,1)S(1)}, bf16[64,3712]{1,0:T(8,128)(2,1)S(1)}, u32[]{:S(2)}, u32[]{:S(2)}) collective-permute-start(bf16[64,3712]{1,0:T(8,128)(2,1)S(1)} %add_convert_fusion.1), channel_id=1, source_target_pairs={{0,2},{1,17},{2,0},{3,19},{4,6},{5,21},{6,4},{7,23},{8,10},{9,25},... | collective-permute-start | bytes 1425416 | tf_op jit(solution)/shard_map/ppermute | solution.py:29
  28.8 9.3 %collective-permute-start.2 = (bf16[32,3712]{1,0:T(8,128)(2,1)S(1)}, bf16[32,3712]{1,0:T(8,128)(2,1)S(1)}, u32[]{:S(2)}, u32[]{:S(2)}) collective-permute-start(bf16[32,3712]{1,0:T(8,128)(2,1)S(1)} %add_convert_fusion.15), channel_id=1, source_target_pairs={{0,16},{1,5},{2,18},{3,7},{4,20},{5,1},{6,22},{7,3},{8,24},{9,13},... | collective-permute-start | bytes 712712 | tf_op jit(solution)/shard_map/ppermute | solution.py:29
  30.1 9.7 %collective-permute-start.7 = (bf16[32,3712]{1,0:T(8,128)(2,1)S(1)}, bf16[32,3712]{1,0:T(8,128)(2,1)S(1)}, u32[]{:S(2)}, u32[]{:S(2)}) collective-permute-start(bf16[32,3712]{1,0:T(8,128)(2,1)S(1)} %add_convert_fusion.13), channel_id=1, source_target_pairs={{0,4},{1,3},{2,6},{3,1},{4,0},{5,7},{6,2},{7,5},{8,12},{9,11},{10,... | collective-permute-start | bytes 712712 | tf_op jit(solution)/shard_map/ppermute | solution.py:29
  32.9 8.5 %collective-permute-start.12 = (bf16[32,3712]{1,0:T(8,128)(2,1)S(1)}, bf16[32,3712]{1,0:T(8,128)(2,1)S(1)}, u32[]{:S(2)}, u32[]{:S(2)}) collective-permute-start(bf16[32,3712]{1,0:T(8,128)(2,1)S(1)} %add_convert_fusion.11), channel_id=1, source_target_pairs={{0,2},{1,17},{2,0},{3,19},{4,6},{5,21},{6,4},{7,23},{8,10},{9,25},... | collective-permute-start | bytes 712712 | tf_op jit(solution)/shard_map/ppermute | solution.py:29
  35.3 7.8 %collective-permute-start.17 = (bf16[32,3712]{1,0:T(8,128)(2,1)S(1)}, bf16[32,3712]{1,0:T(8,128)(2,1)S(1)}, u32[]{:S(2)}, u32[]{:S(2)}) collective-permute-start(bf16[32,3712]{1,0:T(8,128)(2,1)S(1)} %add_convert_fusion.9), channel_id=1, source_target_pairs={{0,16},{1,5},{2,18},{3,7},{4,20},{5,1},{6,22},{7,3},{8,24},{9,13},... | collective-permute-start | bytes 712712 | tf_op jit(solution)/shard_map/ppermute | solution.py:29
  38.1 6.9 %collective-permute-start.3 = (bf16[16,3712]{1,0:T(8,128)(2,1)S(1)}, bf16[16,3712]{1,0:T(8,128)(2,1)S(1)}, u32[]{:S(2)}, u32[]{:S(2)}) collective-permute-start(bf16[16,3712]{1,0:T(8,128)(2,1)S(1)} %add_convert_fusion.23), channel_id=1, source_target_pairs={{0,4},{1,3},{2,6},{3,1},{4,0},{5,7},{6,2},{7,5},{8,12},{9,11},{10,... | collective-permute-start | bytes 356360 | tf_op jit(solution)/shard_map/ppermute | solution.py:29
  39.8 8.0 %collective-permute-start.8 = (bf16[16,3712]{1,0:T(8,128)(2,1)S(1)}, bf16[16,3712]{1,0:T(8,128)(2,1)S(1)}, u32[]{:S(2)}, u32[]{:S(2)}) collective-permute-start(bf16[16,3712]{1,0:T(8,128)(2,1)S(1)} %add_convert_fusion.21), channel_id=1, source_target_pairs={{0,2},{1,17},{2,0},{3,19},{4,6},{5,21},{6,4},{7,23},{8,10},{9,25},... | collective-permute-start | bytes 356360 | tf_op jit(solution)/shard_map/ppermute | solution.py:29
  41.4 10.6 %collective-permute-start.13 = (bf16[16,3712]{1,0:T(8,128)(2,1)S(1)}, bf16[16,3712]{1,0:T(8,128)(2,1)S(1)}, u32[]{:S(2)}, u32[]{:S(2)}) collective-permute-start(bf16[16,3712]{1,0:T(8,128)(2,1)S(1)} %add_convert_fusion.19), channel_id=1, source_target_pairs={{0,16},{1,5},{2,18},{3,7},{4,20},{5,1},{6,22},{7,3},{8,24},{9,13},... | collective-permute-start | bytes 356360 | tf_op jit(solution)/shard_map/ppermute | solution.py:29
  43.1 5.5 %collective-permute-start.18 = (bf16[16,3712]{1,0:T(8,128)(2,1)S(1)}, bf16[16,3712]{1,0:T(8,128)(2,1)S(1)}, u32[]{:S(2)}, u32[]{:S(2)}) collective-permute-start(bf16[16,3712]{1,0:T(8,128)(2,1)S(1)} %add_convert_fusion.17), channel_id=1, source_target_pairs={{0,4},{1,3},{2,6},{3,1},{4,0},{5,7},{6,2},{7,5},{8,12},{9,11},{10,... | collective-permute-start | bytes 356360 | tf_op jit(solution)/shard_map/ppermute | solution.py:29
  45.1 16.9 %collective-permute-start.4 = (bf16[8,3712]{1,0:T(8,128)(2,1)S(1)}, bf16[8,3712]{1,0:T(8,128)(2,1)S(1)}, u32[]{:S(2)}, u32[]{:S(2)}) collective-permute-start(bf16[8,3712]{1,0:T(8,128)(2,1)S(1)} %add_convert_fusion.35), channel_id=1, source_target_pairs={{0,8},{1,9},{2,10},{3,11},{4,12},{5,13},{6,14},{7,15},{8,0},{9,1},... | collective-permute-start | bytes 178184 | tf_op jit(solution)/shard_map/ppermute | solution.py:29
  47.8 11.4 %collective-permute-start.9 = (bf16[8,3712]{1,0:T(8,128)(2,1)S(1)}, bf16[8,3712]{1,0:T(8,128)(2,1)S(1)}, u32[]{:S(2)}, u32[]{:S(2)}) collective-permute-start(bf16[8,3712]{1,0:T(8,128)(2,1)S(1)} %add_convert_fusion.33), channel_id=1, source_target_pairs={{0,8},{1,9},{2,10},{3,11},{4,12},{5,13},{6,14},{7,15},{8,0},{9,1},... | collective-permute-start | bytes 178184 | tf_op jit(solution)/shard_map/ppermute | solution.py:29
  48.6 50.1 %slice-start = ((s8[7602176]{0:T(1024)(128)(4,1)}), s8[4194304]{0:T(1024)(128)(4,1)S(1)}, s32[]{:S(2)}) async-start(s8[7602176]{0:T(1024)(128)(4,1)} %bitcast.6), calls=%async_computation | async-start | bytes 8388608
  48.7 50.1 %copy-start = (bf16[256,256]{1,0:T(8,128)(2,1)S(1)}, bf16[256,256]{1,0:T(8,128)(2,1)}, u32[]{:S(2)}) copy-start(bf16[256,256]{1,0:T(8,128)(2,1)} %projector_ref.3) | copy-start | bytes 393220
  48.7 50.1 %copy-start.1 = (s32[4,1,256]{2,1,0:T(1,128)S(1)}, s32[4,1,256]{2,1,0:T(1,128)}, u32[]{:S(2)}) copy-start(s32[4,1,256]{2,1,0:T(1,128)} %get-tuple-element.129.position_ref) | copy-start | bytes 12292
  48.7 7.2 %collective-permute-start.19 = (bf16[8,3712]{1,0:T(8,128)(2,1)S(1)}, bf16[8,3712]{1,0:T(8,128)(2,1)S(1)}, u32[]{:S(2)}, u32[]{:S(2)}) collective-permute-start(bf16[8,3712]{1,0:T(8,128)(2,1)S(1)} %add_convert_fusion.29), channel_id=1, source_target_pairs={{0,8},{1,9},{2,10},{3,11},{4,12},{5,13},{6,14},{7,15},{8,0},{9,1},... | collective-permute-start | bytes 178184 | tf_op jit(solution)/shard_map/ppermute | solution.py:29
  52.0 6.8 %collective-permute-start.14 = (bf16[8,3712]{1,0:T(8,128)(2,1)S(1)}, bf16[8,3712]{1,0:T(8,128)(2,1)S(1)}, u32[]{:S(2)}, u32[]{:S(2)}) collective-permute-start(bf16[8,3712]{1,0:T(8,128)(2,1)S(1)} %add_convert_fusion.31), channel_id=1, source_target_pairs={{0,8},{1,9},{2,10},{3,11},{4,12},{5,13},{6,14},{7,15},{8,0},{9,1},... | collective-permute-start | bytes 178184 | tf_op jit(solution)/shard_map/ppermute | solution.py:29
  56.0 10.4 %collective-permute-start.23 = (bf16[8,3712]{1,0:T(8,128)(2,1)S(1)}, bf16[8,3712]{1,0:T(8,128)(2,1)S(1)}, u32[]{:S(2)}, u32[]{:S(2)}) collective-permute-start(bf16[8,3712]{1,0:T(8,128)(2,1)S(1)} %get-tuple-element.210), channel_id=1, source_target_pairs={{0,8},{1,9},{2,10},{3,11},{4,12},{5,13},{6,14},{7,15},{8,0},{9,1},... | collective-permute-start | bytes 178184 | tf_op jit(solution)/shard_map/ppermute | solution.py:29
  58.9 8.6 %collective-permute-start.22 = (bf16[8,3712]{1,0:T(8,128)(2,1)S(1)}, bf16[8,3712]{1,0:T(8,128)(2,1)S(1)}, u32[]{:S(2)}, u32[]{:S(2)}) collective-permute-start(bf16[8,3712]{1,0:T(8,128)(2,1)S(1)} %get-tuple-element.212), channel_id=1, source_target_pairs={{0,8},{1,9},{2,10},{3,11},{4,12},{5,13},{6,14},{7,15},{8,0},{9,1},... | collective-permute-start | bytes 178184 | tf_op jit(solution)/shard_map/ppermute | solution.py:29
  59.3 8.5 %collective-permute-start.21 = (bf16[8,3712]{1,0:T(8,128)(2,1)S(1)}, bf16[8,3712]{1,0:T(8,128)(2,1)S(1)}, u32[]{:S(2)}, u32[]{:S(2)}) collective-permute-start(bf16[8,3712]{1,0:T(8,128)(2,1)S(1)} %get-tuple-element.214), channel_id=1, source_target_pairs={{0,8},{1,9},{2,10},{3,11},{4,12},{5,13},{6,14},{7,15},{8,0},{9,1},... | collective-permute-start | bytes 178184 | tf_op jit(solution)/shard_map/ppermute | solution.py:29
  62.1 8.2 %collective-permute-start.20 = (bf16[8,3712]{1,0:T(8,128)(2,1)S(1)}, bf16[8,3712]{1,0:T(8,128)(2,1)S(1)}, u32[]{:S(2)}, u32[]{:S(2)}) collective-permute-start(bf16[8,3712]{1,0:T(8,128)(2,1)S(1)} %get-tuple-element.216), channel_id=1, source_target_pairs={{0,8},{1,9},{2,10},{3,11},{4,12},{5,13},{6,14},{7,15},{8,0},{9,1},... | collective-permute-start | bytes 178184 | tf_op jit(solution)/shard_map/ppermute | solution.py:29
  62.5 17.9 %collective-permute-start.32 = (bf16[8,14848]{1,0:T(8,128)(2,1)S(1)}, bf16[8,14848]{1,0:T(8,128)(2,1)S(1)}, u32[]{:S(2)}, u32[]{:S(2)}) collective-permute-start(bf16[8,14848]{1,0:T(8,128)(2,1)S(1)} %pad_maximum_fusion), channel_id=1, source_target_pairs={{0,16},{1,17},{2,18},{3,19},{4,20},{5,21},{6,22},{7,23},{8,24},{9,... | collective-permute-start | bytes 712712 | tf_op jit(solution)/shard_map/ppermute | solution.py:29
  66.4 5.9 %collective-permute-start.27 = (bf16[16,3712]{1,0:T(8,128)(2,1)S(1)}, bf16[16,3712]{1,0:T(8,128)(2,1)S(1)}, u32[]{:S(2)}, u32[]{:S(2)}) collective-permute-start(bf16[16,3712]{1,0:T(8,128)(2,1)S(1)} %constant_dynamic-update-slice_fusion), channel_id=1, source_target_pairs={{0,4},{1,3},{2,6},{3,1},{4,0},{5,7},{6,2},{7,5},{8,12},{9,11},{10,... | collective-permute-start | bytes 356360 | tf_op jit(solution)/shard_map/ppermute | solution.py:29
  67.5 7.2 %collective-permute-start.26 = (bf16[16,3712]{1,0:T(8,128)(2,1)S(1)}, bf16[16,3712]{1,0:T(8,128)(2,1)S(1)}, u32[]{:S(2)}, u32[]{:S(2)}) collective-permute-start(bf16[16,3712]{1,0:T(8,128)(2,1)S(1)} %constant_dynamic-update-slice_fusion.2), channel_id=1, source_target_pairs={{0,16},{1,5},{2,18},{3,7},{4,20},{5,1},{6,22},{7,3},{8,24},{9,13},... | collective-permute-start | bytes 356360 | tf_op jit(solution)/shard_map/ppermute | solution.py:29
  67.8 8.0 %collective-permute-start.25 = (bf16[16,3712]{1,0:T(8,128)(2,1)S(1)}, bf16[16,3712]{1,0:T(8,128)(2,1)S(1)}, u32[]{:S(2)}, u32[]{:S(2)}) collective-permute-start(bf16[16,3712]{1,0:T(8,128)(2,1)S(1)} %constant_dynamic-update-slice_fusion.4), channel_id=1, source_target_pairs={{0,2},{1,17},{2,0},{3,19},{4,6},{5,21},{6,4},{7,23},{8,10},{9,25},... | collective-permute-start | bytes 356360 | tf_op jit(solution)/shard_map/ppermute | solution.py:29
  70.4 7.8 %collective-permute-start.24 = (bf16[16,3712]{1,0:T(8,128)(2,1)S(1)}, bf16[16,3712]{1,0:T(8,128)(2,1)S(1)}, u32[]{:S(2)}, u32[]{:S(2)}) collective-permute-start(bf16[16,3712]{1,0:T(8,128)(2,1)S(1)} %constant_dynamic-update-slice_fusion.6), channel_id=1, source_target_pairs={{0,4},{1,3},{2,6},{3,1},{4,0},{5,7},{6,2},{7,5},{8,12},{9,11},{10,... | collective-permute-start | bytes 356360 | tf_op jit(solution)/shard_map/ppermute | solution.py:29
  72.4 9.6 %collective-permute-start.31 = (bf16[32,3712]{1,0:T(8,128)(2,1)S(1)}, bf16[32,3712]{1,0:T(8,128)(2,1)S(1)}, u32[]{:S(2)}, u32[]{:S(2)}) collective-permute-start(bf16[32,3712]{1,0:T(8,128)(2,1)S(1)} %constant_dynamic-update-slice_fusion.8), channel_id=1, source_target_pairs={{0,16},{1,5},{2,18},{3,7},{4,20},{5,1},{6,22},{7,3},{8,24},{9,13},... | collective-permute-start | bytes 712712 | tf_op jit(solution)/shard_map/ppermute | solution.py:29
  74.7 8.6 %collective-permute-start.30 = (bf16[32,3712]{1,0:T(8,128)(2,1)S(1)}, bf16[32,3712]{1,0:T(8,128)(2,1)S(1)}, u32[]{:S(2)}, u32[]{:S(2)}) collective-permute-start(bf16[32,3712]{1,0:T(8,128)(2,1)S(1)} %constant_dynamic-update-slice_fusion.10), channel_id=1, source_target_pairs={{0,2},{1,17},{2,0},{3,19},{4,6},{5,21},{6,4},{7,23},{8,10},{9,25},... | collective-permute-start | bytes 712712 | tf_op jit(solution)/shard_map/ppermute | solution.py:29
  75.8 9.6 %collective-permute-start.29 = (bf16[32,3712]{1,0:T(8,128)(2,1)S(1)}, bf16[32,3712]{1,0:T(8,128)(2,1)S(1)}, u32[]{:S(2)}, u32[]{:S(2)}) collective-permute-start(bf16[32,3712]{1,0:T(8,128)(2,1)S(1)} %constant_dynamic-update-slice_fusion.12), channel_id=1, source_target_pairs={{0,4},{1,3},{2,6},{3,1},{4,0},{5,7},{6,2},{7,5},{8,12},{9,11},{10,... | collective-permute-start | bytes 712712 | tf_op jit(solution)/shard_map/ppermute | solution.py:29
  78.2 8.9 %collective-permute-start.28 = (bf16[32,3712]{1,0:T(8,128)(2,1)S(1)}, bf16[32,3712]{1,0:T(8,128)(2,1)S(1)}, u32[]{:S(2)}, u32[]{:S(2)}) collective-permute-start(bf16[32,3712]{1,0:T(8,128)(2,1)S(1)} %constant_dynamic-update-slice_fusion.14), channel_id=1, source_target_pairs={{0,16},{1,5},{2,18},{3,7},{4,20},{5,1},{6,22},{7,3},{8,24},{9,13},... | collective-permute-start | bytes 712712 | tf_op jit(solution)/shard_map/ppermute | solution.py:29
  82.1 10.1 %collective-permute-start.36 = (bf16[64,3712]{1,0:T(8,128)(2,1)S(1)}, bf16[64,3712]{1,0:T(8,128)(2,1)S(1)}, u32[]{:S(2)}, u32[]{:S(2)}) collective-permute-start(bf16[64,3712]{1,0:T(8,128)(2,1)S(1)} %constant_dynamic-update-slice_fusion.16.refs_0_), channel_id=1, source_target_pairs={{0,2},{1,17},{2,0},{3,19},{4,6},{5,21},{6,4},{7,23},{8,10},{9,25},... | collective-permute-start | bytes 1425416 | tf_op jit(solution)/shard_map/ppermute | solution.py:29
  83.4 8.7 %collective-permute-start.35 = (bf16[64,3712]{1,0:T(8,128)(2,1)S(1)}, bf16[64,3712]{1,0:T(8,128)(2,1)S(1)}, u32[]{:S(2)}, u32[]{:S(2)}) collective-permute-start(bf16[64,3712]{1,0:T(8,128)(2,1)S(1)} %constant_dynamic-update-slice_fusion.18.refs_4_), channel_id=1, source_target_pairs={{0,4},{1,3},{2,6},{3,1},{4,0},{5,7},{6,2},{7,5},{8,12},{9,11},{10,... | collective-permute-start | bytes 1425416 | tf_op jit(solution)/shard_map/ppermute | solution.py:29
  85.4 10.1 %collective-permute-start.34 = (bf16[64,3712]{1,0:T(8,128)(2,1)S(1)}, bf16[64,3712]{1,0:T(8,128)(2,1)S(1)}, u32[]{:S(2)}, u32[]{:S(2)}) collective-permute-start(bf16[64,3712]{1,0:T(8,128)(2,1)S(1)} %constant_dynamic-update-slice_fusion.20.refs_8_), channel_id=1, source_target_pairs={{0,16},{1,5},{2,18},{3,7},{4,20},{5,1},{6,22},{7,3},{8,24},{9,13},... | collective-permute-start | bytes 1425416 | tf_op jit(solution)/shard_map/ppermute | solution.py:29
  87.2 8.7 %collective-permute-start.33 = (bf16[64,3712]{1,0:T(8,128)(2,1)S(1)}, bf16[64,3712]{1,0:T(8,128)(2,1)S(1)}, u32[]{:S(2)}, u32[]{:S(2)}) collective-permute-start(bf16[64,3712]{1,0:T(8,128)(2,1)S(1)} %constant_dynamic-update-slice_fusion.22.refs_0_), channel_id=1, source_target_pairs={{0,2},{1,17},{2,0},{3,19},{4,6},{5,21},{6,4},{7,23},{8,10},{9,25},... | collective-permute-start | bytes 1425416 | tf_op jit(solution)/shard_map/ppermute | solution.py:29
  88.5 7.6 %collective-permute-start.43 = (bf16[64,3712]{1,0:T(8,128)(2,1)S(1)}, bf16[64,3712]{1,0:T(8,128)(2,1)S(1)}, u32[]{:S(2)}, u32[]{:S(2)}) collective-permute-start(bf16[64,3712]{1,0:T(8,128)(2,1)S(1)} %constant_dynamic-update-slice_fusion.20.refs_8_), channel_id=1, source_target_pairs={{0,1},{1,0},{2,3},{3,2},{4,5},{5,4},{6,7},{7,6},{8,9},{9,8},{10,11... | collective-permute-start | bytes 1425416 | tf_op jit(solution)/shard_map/ppermute | solution.py:29
  92.1 4.3 %collective-permute-start.41 = (bf16[64,3712]{1,0:T(8,128)(2,1)S(1)}, bf16[64,3712]{1,0:T(8,128)(2,1)S(1)}, u32[]{:S(2)}, u32[]{:S(2)}) collective-permute-start(bf16[64,3712]{1,0:T(8,128)(2,1)S(1)} %constant_dynamic-update-slice_fusion.18.refs_4_), channel_id=1, source_target_pairs={{0,1},{1,0},{2,3},{3,2},{4,5},{5,4},{6,7},{7,6},{8,9},{9,8},{10,11... | collective-permute-start | bytes 1425416 | tf_op jit(solution)/shard_map/ppermute | solution.py:29
  92.1 4.4 %collective-permute-start.39 = (bf16[64,3712]{1,0:T(8,128)(2,1)S(1)}, bf16[64,3712]{1,0:T(8,128)(2,1)S(1)}, u32[]{:S(2)}, u32[]{:S(2)}) collective-permute-start(bf16[64,3712]{1,0:T(8,128)(2,1)S(1)} %constant_dynamic-update-slice_fusion.16.refs_0_), channel_id=1, source_target_pairs={{0,1},{1,0},{2,3},{3,2},{4,5},{5,4},{6,7},{7,6},{8,9},{9,8},{10,11... | collective-permute-start | bytes 1425416 | tf_op jit(solution)/shard_map/ppermute | solution.py:29
  95.5 2.5 %collective-permute-start.42 = (bf16[64,3712]{1,0:T(8,128)(2,1)S(1)}, bf16[64,3712]{1,0:T(8,128)(2,1)S(1)}, u32[]{:S(2)}, u32[]{:S(2)}) collective-permute-start(bf16[64,3712]{1,0:T(8,128)(2,1)S(1)} %collective-permute-done.35.refs_5_), channel_id=1, source_target_pairs={{0,1},{1,0},{2,3},{3,2},{4,5},{5,4},{6,7},{7,6},{8,9},{9,8},{10,11... | collective-permute-start | bytes 1425416 | tf_op jit(solution)/shard_map/ppermute | solution.py:29
  95.9 2.2 %collective-permute-start.44 = (bf16[64,3712]{1,0:T(8,128)(2,1)S(1)}, bf16[64,3712]{1,0:T(8,128)(2,1)S(1)}, u32[]{:S(2)}, u32[]{:S(2)}) collective-permute-start(bf16[64,3712]{1,0:T(8,128)(2,1)S(1)} %collective-permute-done.34.refs_9_), channel_id=1, source_target_pairs={{0,1},{1,0},{2,3},{3,2},{4,5},{5,4},{6,7},{7,6},{8,9},{9,8},{10,11... | collective-permute-start | bytes 1425416 | tf_op jit(solution)/shard_map/ppermute | solution.py:29
  96.1 2.7 %collective-permute-start.40 = (bf16[64,3712]{1,0:T(8,128)(2,1)S(1)}, bf16[64,3712]{1,0:T(8,128)(2,1)S(1)}, u32[]{:S(2)}, u32[]{:S(2)}) collective-permute-start(bf16[64,3712]{1,0:T(8,128)(2,1)S(1)} %collective-permute-done.36.refs_1_), channel_id=1, source_target_pairs={{0,1},{1,0},{2,3},{3,2},{4,5},{5,4},{6,7},{7,6},{8,9},{9,8},{10,11... | collective-permute-start | bytes 1425416 | tf_op jit(solution)/shard_map/ppermute | solution.py:29
  96.4 6.2 %collective-permute-start.37 = (bf16[64,3712]{1,0:T(8,128)(2,1)S(1)}, bf16[64,3712]{1,0:T(8,128)(2,1)S(1)}, u32[]{:S(2)}, u32[]{:S(2)}) collective-permute-start(bf16[64,3712]{1,0:T(8,128)(2,1)S(1)} %constant_dynamic-update-slice_fusion.22.refs_0_), channel_id=1, source_target_pairs={{0,1},{1,0},{2,3},{3,2},{4,5},{5,4},{6,7},{7,6},{8,9},{9,8},{10,11... | collective-permute-start | bytes 1425416 | tf_op jit(solution)/shard_map/ppermute | solution.py:29
  96.6 6.0 %collective-permute-start.38 = (bf16[64,3712]{1,0:T(8,128)(2,1)S(1)}, bf16[64,3712]{1,0:T(8,128)(2,1)S(1)}, u32[]{:S(2)}, u32[]{:S(2)}) collective-permute-start(bf16[64,3712]{1,0:T(8,128)(2,1)S(1)} %collective-permute-done.33.refs_1_), channel_id=1, source_target_pairs={{0,1},{1,0},{2,3},{3,2},{4,5},{5,4},{6,7},{7,6},{8,9},{9,8},{10,11... | collective-permute-start | bytes 1425416 | tf_op jit(solution)/shard_map/ppermute | solution.py:29
  (5 other events, 119.9 us)

commit v5 on v4

--- a/solution.py
+++ b/solution.py
@@ -16,6 +16,7 @@
 
 
 runs_per_chain = 2
+product_runs = 1
 slots = 3
 lags = (0, 0, 0, 0)
 
@@ -36,8 +37,9 @@
     return [turning[t:] + turning[:t] + shard_bits[-1:] for t in range(3)]
 
 
-def pieces_of(start, count):
-    ends = [start + count * (run + 1) // runs_per_chain for run in range(runs_per_chain)]
+def pieces_of(start, count, run_count=None):
+    run_count = run_count or runs_per_chain
+    ends = [start + count * (run + 1) // run_count for run in range(run_count)]
     return [(at, end - at) for at, end in zip([start] + ends, ends) if end > at]
 
 
@@ -164,7 +166,7 @@
     runs = [
         (chain, at, size)
         for chain, (start, count) in enumerate(spans)
-        for at, size in pieces_of(start, count)
+        for at, size in pieces_of(start, count, product_runs)
     ]
 
     def outgoing(index):
@@ -189,8 +191,8 @@
         slot = index % slots
         if index >= slots:
             outgoing(index - slots).wait()
-        for block in range(0, size, 2):
-            columns = slice(block * block_width, min(block + 2, size) * block_width)
+        for block in range(0, size, 4):
+            columns = slice(block * block_width, min(block + 4, size) * block_width)
             here = slice(columns.start + at * block_width, columns.stop + at * block_width)
             source = pl.ds(here.start - spans[chain][0] * block_width, here.stop - here.start)
             direction = jnp.concatenate(
@@ -207,7 +209,7 @@
 
 def apply_update(projector, position, weights, pieces, so_far, chosen, spans, block_width):
     rows, rank = projector.shape
-    longest = max(size for span in spans for _, size in pieces_of(*span)) * block_width
+    longest = max(size for span in spans for _, size in pieces_of(*span, product_runs)) * block_width
     whole = pl.BlockSpec(memory_space=pltpu.VMEM)
     anywhere = pl.BlockSpec(memory_space=pl.ANY)
     aliased = [] if so_far is None else [so_far]

time: 105 us -> 105 us (level)
  transfers between devices with their start and end apart: 45 -> 45, of which waited for: 15 -> 15; matrix products, arithmetic and copies ran while one was open for 12% -> 12% of each run, Pallas kernels for 4% -> 3%
where the time goes in v5:
time: 105 us
  starting transfers between devices  51.8 us (49%)
  waiting for transfers between devices  24.9 us (24%)
  Pallas kernels  13.7 us (13%)
  other arithmetic  12.6 us (12%)
  between operations  1.25 us (1%)
    ppermute x45, starting transfers between devices, swap(): lax.ppermute(array, both, [(i, i ^ 1 << bits[i % 2]) for i in range(size)])  51.8 us
    ppermute x45, waiting for transfers between devices, swap(): lax.ppermute(array, both, [(i, i ^ 1 << bits[i % 2]) for i in range(size)])  24.9 us
    convert_element_type x31, other arithmetic, added(): sum((term.astype(jnp.float32) for term in terms)).astype(jnp.bfloat16)  10.5 us
    pallas_call x1, Pallas kernels, prepare(): pl.pallas_call(functools.partial(prepare_kernel, spans, block_width, orde...  8.08 us
    pallas_call x2, Pallas kernels, apply_update(): pl.pallas_call(functools.partial(apply_kernel, chosen, spans, block_width...  5.59 us
  transfers between devices with their start and end apart: 45, of which 15 were waited for; matrix products, arithmetic and copies ran while one was open for 12% of the time, Pallas kernels for 3%

profile of v5, /device:TPU:0, one launch (start us, length us, event | category | flops | bytes accessed | tf_op | source)
XLA Modules:
  0.0 104.6 jit_solution(10653408112911287033)
XLA Ops:
  0.6 8.1 %prepare.1 = (bf16[128,3712]{1,0:T(8,128)(2,1)}, bf16[128,3712]{1,0:T(8,128)(2,1)}, bf16[128,3712]{1,0:T(8,128)(2,1)}, bf16[128,3712]{1,0:T(8,128)(2,1)}, bf16[1...) custom-call(s32[1]{0:T(128)} %bitcast.me_ref, ...), custom_call_target="tpu_custom_call" | custom-call | flops 1024 | bytes 1024 | tf_op jit(solution)/shard_map/prepare/pallas_call | solution.py:138
  9.9 2.3 %collective-permute-done = bf16[128,3712]{1,0:T(8,128)(2,1)S(1)} collective-permute-done((bf16[128,3712]{1,0:T(8,128)(2,1)}, bf16[128,3712]{1,0:T(8,128)(2,1)S(1)}, u32[]{:S(2)}, u32[]{:S(2)}) %collective-permute-start) | collective-permute-done | bytes 950304 | tf_op jit(solution)/shard_map/ppermute | solution.py:30
  12.2 1.1 %add_convert_fusion.7 = bf16[64,3712]{1,0:T(8,128)(2,1)S(1)} fusion(bf16[128,3712]{1,0:T(8,128)(2,1)S(1)} %collective-permute-done, bf16[128,3712]{1,0:T(8,128)(2,1)} %get-tuple-element.134), kind=kLoop, calls=%fused_computation.11 | loop fusion | flops 950272 | bytes 1425408 | tf_op jit(solution)/shard_map/convert_element_type | solution.py:234
  13.3 2.9 %collective-permute-start.1 = (bf16[64,3712]{1,0:T(8,128)(2,1)S(1)}, bf16[64,3712]{1,0:T(8,128)(2,1)S(1)}, u32[]{:S(2)}, u32[]{:S(2)}) collective-permute-start(bf16[64,3712]{1,0:T(8,128)(2,1)S(1)} %add_convert_fusion.7), channel_id=1, source_target_pairs={{0,2},{1,17},{2,0},{3,19},{4,6},{5,21},{6,4},{7,23},{8,10},{9,25},... | collective-permute-start | bytes 1425416 | tf_op jit(solution)/shard_map/ppermute | solution.py:30
  16.3 1.3 %add_convert_fusion.5 = bf16[64,3712]{1,0:T(8,128)(2,1)S(1)} fusion(bf16[128,3712]{1,0:T(8,128)(2,1)} %collective-permute-done.5, bf16[128,3712]{1,0:T(8,128)(2,1)} %get-tuple-element.152), kind=kLoop, calls=%fused_computation.9 | loop fusion | flops 950272 | bytes 1425408 | tf_op jit(solution)/shard_map/convert_element_type | solution.py:234
  17.5 1.6 %collective-permute-start.6 = (bf16[64,3712]{1,0:T(8,128)(2,1)S(1)}, bf16[64,3712]{1,0:T(8,128)(2,1)S(1)}, u32[]{:S(2)}, u32[]{:S(2)}) collective-permute-start(bf16[64,3712]{1,0:T(8,128)(2,1)S(1)} %add_convert_fusion.5), channel_id=1, source_target_pairs={{0,16},{1,5},{2,18},{3,7},{4,20},{5,1},{6,22},{7,3},{8,24},{9,13},... | collective-permute-start | bytes 1425416 | tf_op jit(solution)/shard_map/ppermute | solution.py:30
  19.1 1.3 %add_convert_fusion.3 = bf16[64,3712]{1,0:T(8,128)(2,1)S(1)} fusion(bf16[128,3712]{1,0:T(8,128)(2,1)} %collective-permute-done.10, bf16[128,3712]{1,0:T(8,128)(2,1)} %get-tuple-element.170), kind=kLoop, calls=%fused_computation.7 | loop fusion | flops 950272 | bytes 1425408 | tf_op jit(solution)/shard_map/convert_element_type | solution.py:234
  20.4 1.6 %collective-permute-start.11 = (bf16[64,3712]{1,0:T(8,128)(2,1)S(1)}, bf16[64,3712]{1,0:T(8,128)(2,1)S(1)}, u32[]{:S(2)}, u32[]{:S(2)}) collective-permute-start(bf16[64,3712]{1,0:T(8,128)(2,1)S(1)} %add_convert_fusion.3), channel_id=1, source_target_pairs={{0,4},{1,3},{2,6},{3,1},{4,0},{5,7},{6,2},{7,5},{8,12},{9,11},{10,... | collective-permute-start | bytes 1425416 | tf_op jit(solution)/shard_map/ppermute | solution.py:30
  22.1 1.3 %add_convert_fusion.1 = bf16[64,3712]{1,0:T(8,128)(2,1)S(1)} fusion(bf16[128,3712]{1,0:T(8,128)(2,1)} %collective-permute-done.15, bf16[128,3712]{1,0:T(8,128)(2,1)} %get-tuple-element.188), kind=kLoop, calls=%fused_computation.5 | loop fusion | flops 950272 | bytes 1425408 | tf_op jit(solution)/shard_map/convert_element_type | solution.py:234
  23.4 0.6 collective-permute-start.16
  24.0 1.1 %add_convert_fusion.6 = bf16[64,3712]{1,0:T(8,128)(2,1)S(1)} fusion(bf16[128,3712]{1,0:T(8,128)(2,1)S(1)} %collective-permute-done, bf16[128,3712]{1,0:T(8,128)(2,1)} %get-tuple-element.134), kind=kLoop, calls=%fused_computation.10 | loop fusion | flops 950272 | bytes 1425408 | tf_op jit(solution)/shard_map/convert_element_type | solution.py:234
  25.1 1.3 %add_convert_fusion.4 = bf16[64,3712]{1,0:T(8,128)(2,1)S(1)} fusion(bf16[128,3712]{1,0:T(8,128)(2,1)} %collective-permute-done.5, bf16[128,3712]{1,0:T(8,128)(2,1)} %get-tuple-element.152), kind=kLoop, calls=%fused_computation.8 | loop fusion | flops 950272 | bytes 1425408 | tf_op jit(solution)/shard_map/convert_element_type | solution.py:234
  26.4 1.1 %add_convert_fusion.2 = bf16[64,3712]{1,0:T(8,128)(2,1)S(1)} fusion(bf16[128,3712]{1,0:T(8,128)(2,1)} %collective-permute-done.10, bf16[128,3712]{1,0:T(8,128)(2,1)S(1)} %copy-done.5), kind=kLoop, calls=%fused_computation.6 | loop fusion | flops 950272 | bytes 1425408 | tf_op jit(solution)/shard_map/convert_element_type | solution.py:234
  27.5 1.1 %add_convert_fusion = bf16[64,3712]{1,0:T(8,128)(2,1)S(1)} fusion(bf16[128,3712]{1,0:T(8,128)(2,1)} %collective-permute-done.15, bf16[128,3712]{1,0:T(8,128)(2,1)S(1)} %copy-done.4), kind=kLoop, calls=%fused_computation.4 | loop fusion | flops 950272 | bytes 1425408 | tf_op jit(solution)/shard_map/convert_element_type | solution.py:234
  29.3 0.7 collective-permute-done.6
  30.1 2.7 %collective-permute-start.7 = (bf16[32,3712]{1,0:T(8,128)(2,1)S(1)}, bf16[32,3712]{1,0:T(8,128)(2,1)S(1)}, u32[]{:S(2)}, u32[]{:S(2)}) collective-permute-start(bf16[32,3712]{1,0:T(8,128)(2,1)S(1)} %add_convert_fusion.13), channel_id=1, source_target_pairs={{0,4},{1,3},{2,6},{3,1},{4,0},{5,7},{6,2},{7,5},{8,12},{9,11},{10,... | collective-permute-start | bytes 712712 | tf_op jit(solution)/shard_map/ppermute | solution.py:30
  32.9 0.9 collective-permute-start.12
  33.8 1.4 %collective-permute-done.16 = bf16[64,3712]{1,0:T(8,128)(2,1)S(1)} collective-permute-done((bf16[64,3712]{1,0:T(8,128)(2,1)S(1)}, bf16[64,3712]{1,0:T(8,128)(2,1)S(1)}, u32[]{:S(2)}, u32[]{:S(2)}) %collective-permute-start.16) | collective-permute-done | bytes 475168 | tf_op jit(solution)/shard_map/ppermute | solution.py:30
  35.3 2.5 %collective-permute-start.17 = (bf16[32,3712]{1,0:T(8,128)(2,1)S(1)}, bf16[32,3712]{1,0:T(8,128)(2,1)S(1)}, u32[]{:S(2)}, u32[]{:S(2)}) collective-permute-start(bf16[32,3712]{1,0:T(8,128)(2,1)S(1)} %add_convert_fusion.9), channel_id=1, source_target_pairs={{0,16},{1,5},{2,18},{3,7},{4,20},{5,1},{6,22},{7,3},{8,24},{9,13},... | collective-permute-start | bytes 712712 | tf_op jit(solution)/shard_map/ppermute | solution.py:30
  38.1 1.6 %collective-permute-start.3 = (bf16[16,3712]{1,0:T(8,128)(2,1)S(1)}, bf16[16,3712]{1,0:T(8,128)(2,1)S(1)}, u32[]{:S(2)}, u32[]{:S(2)}) collective-permute-start(bf16[16,3712]{1,0:T(8,128)(2,1)S(1)} %add_convert_fusion.23), channel_id=1, source_target_pairs={{0,4},{1,3},{2,6},{3,1},{4,0},{5,7},{6,2},{7,5},{8,12},{9,11},{10,... | collective-permute-start | bytes 356360 | tf_op jit(solution)/shard_map/ppermute | solution.py:30
  39.8 1.6 %collective-permute-start.8 = (bf16[16,3712]{1,0:T(8,128)(2,1)S(1)}, bf16[16,3712]{1,0:T(8,128)(2,1)S(1)}, u32[]{:S(2)}, u32[]{:S(2)}) collective-permute-start(bf16[16,3712]{1,0:T(8,128)(2,1)S(1)} %add_convert_fusion.21), channel_id=1, source_target_pairs={{0,2},{1,17},{2,0},{3,19},{4,6},{5,21},{6,4},{7,23},{8,10},{9,25},... | collective-permute-start | bytes 356360 | tf_op jit(solution)/shard_map/ppermute | solution.py:30
  41.5 1.6 %collective-permute-done.17 = bf16[32,3712]{1,0:T(8,128)(2,1)S(1)} collective-permute-done((bf16[32,3712]{1,0:T(8,128)(2,1)S(1)}, bf16[32,3712]{1,0:T(8,128)(2,1)S(1)}, u32[]{:S(2)}, u32[]{:S(2)}) %collective-permute-start.17) | collective-permute-done | bytes 237600 | tf_op jit(solution)/shard_map/ppermute | solution.py:30
  43.1 1.8 %collective-permute-start.18 = (bf16[16,3712]{1,0:T(8,128)(2,1)S(1)}, bf16[16,3712]{1,0:T(8,128)(2,1)S(1)}, u32[]{:S(2)}, u32[]{:S(2)}) collective-permute-start(bf16[16,3712]{1,0:T(8,128)(2,1)S(1)} %add_convert_fusion.17), channel_id=1, source_target_pairs={{0,4},{1,3},{2,6},{3,1},{4,0},{5,7},{6,2},{7,5},{8,12},{9,11},{10,... | collective-permute-start | bytes 356360 | tf_op jit(solution)/shard_map/ppermute | solution.py:30
  45.1 2.7 %collective-permute-start.4 = (bf16[8,3712]{1,0:T(8,128)(2,1)S(1)}, bf16[8,3712]{1,0:T(8,128)(2,1)S(1)}, u32[]{:S(2)}, u32[]{:S(2)}) collective-permute-start(bf16[8,3712]{1,0:T(8,128)(2,1)S(1)} %add_convert_fusion.35), channel_id=1, source_target_pairs={{0,8},{1,9},{2,10},{3,11},{4,12},{5,13},{6,14},{7,15},{8,0},{9,1},... | collective-permute-start | bytes 178184 | tf_op jit(solution)/shard_map/ppermute | solution.py:30
  48.7 3.3 %collective-permute-start.19 = (bf16[8,3712]{1,0:T(8,128)(2,1)S(1)}, bf16[8,3712]{1,0:T(8,128)(2,1)S(1)}, u32[]{:S(2)}, u32[]{:S(2)}) collective-permute-start(bf16[8,3712]{1,0:T(8,128)(2,1)S(1)} %add_convert_fusion.29), channel_id=1, source_target_pairs={{0,8},{1,9},{2,10},{3,11},{4,12},{5,13},{6,14},{7,15},{8,0},{9,1},... | collective-permute-start | bytes 178184 | tf_op jit(solution)/shard_map/ppermute | solution.py:30
  52.1 3.8 %collective-permute-done.19 = bf16[8,3712]{1,0:T(8,128)(2,1)S(1)} collective-permute-done((bf16[8,3712]{1,0:T(8,128)(2,1)S(1)}, bf16[8,3712]{1,0:T(8,128)(2,1)S(1)}, u32[]{:S(2)}, u32[]{:S(2)}) %collective-permute-start.19) | collective-permute-done | bytes 59424 | tf_op jit(solution)/shard_map/ppermute | solution.py:30
  56.0 1.2 %collective-permute-start.23 = (bf16[8,3712]{1,0:T(8,128)(2,1)S(1)}, bf16[8,3712]{1,0:T(8,128)(2,1)S(1)}, u32[]{:S(2)}, u32[]{:S(2)}) collective-permute-start(bf16[8,3712]{1,0:T(8,128)(2,1)S(1)} %get-tuple-element.210), channel_id=1, source_target_pairs={{0,8},{1,9},{2,10},{3,11},{4,12},{5,13},{6,14},{7,15},{8,0},{9,1},... | collective-permute-start | bytes 178184 | tf_op jit(solution)/shard_map/ppermute | solution.py:30
  57.2 1.5 %collective-permute-done.14 = bf16[8,3712]{1,0:T(8,128)(2,1)S(1)} collective-permute-done((bf16[8,3712]{1,0:T(8,128)(2,1)S(1)}, bf16[8,3712]{1,0:T(8,128)(2,1)S(1)}, u32[]{:S(2)}, u32[]{:S(2)}) %collective-permute-start.14) | collective-permute-done | bytes 59424 | tf_op jit(solution)/shard_map/ppermute | solution.py:30
  59.3 2.7 %collective-permute-start.21 = (bf16[8,3712]{1,0:T(8,128)(2,1)S(1)}, bf16[8,3712]{1,0:T(8,128)(2,1)S(1)}, u32[]{:S(2)}, u32[]{:S(2)}) collective-permute-start(bf16[8,3712]{1,0:T(8,128)(2,1)S(1)} %get-tuple-element.214), channel_id=1, source_target_pairs={{0,8},{1,9},{2,10},{3,11},{4,12},{5,13},{6,14},{7,15},{8,0},{9,1},... | collective-permute-start | bytes 178184 | tf_op jit(solution)/shard_map/ppermute | solution.py:30
  62.5 3.9 %collective-permute-start.32 = (bf16[8,14848]{1,0:T(8,128)(2,1)S(1)}, bf16[8,14848]{1,0:T(8,128)(2,1)S(1)}, u32[]{:S(2)}, u32[]{:S(2)}) collective-permute-start(bf16[8,14848]{1,0:T(8,128)(2,1)S(1)} %pad_maximum_fusion), channel_id=1, source_target_pairs={{0,16},{1,17},{2,18},{3,19},{4,20},{5,21},{6,22},{7,23},{8,24},{9,... | collective-permute-start | bytes 712712 | tf_op jit(solution)/shard_map/ppermute | solution.py:30
  66.4 1.1 %collective-permute-start.27 = (bf16[16,3712]{1,0:T(8,128)(2,1)S(1)}, bf16[16,3712]{1,0:T(8,128)(2,1)S(1)}, u32[]{:S(2)}, u32[]{:S(2)}) collective-permute-start(bf16[16,3712]{1,0:T(8,128)(2,1)S(1)} %constant_dynamic-update-slice_fusion), channel_id=1, source_target_pairs={{0,4},{1,3},{2,6},{3,1},{4,0},{5,7},{6,2},{7,5},{8,12},{9,11},{10,... | collective-permute-start | bytes 356360 | tf_op jit(solution)/shard_map/ppermute | solution.py:30
  67.8 2.6 %collective-permute-start.25 = (bf16[16,3712]{1,0:T(8,128)(2,1)S(1)}, bf16[16,3712]{1,0:T(8,128)(2,1)S(1)}, u32[]{:S(2)}, u32[]{:S(2)}) collective-permute-start(bf16[16,3712]{1,0:T(8,128)(2,1)S(1)} %constant_dynamic-update-slice_fusion.4), channel_id=1, source_target_pairs={{0,2},{1,17},{2,0},{3,19},{4,6},{5,21},{6,4},{7,23},{8,10},{9,25},... | collective-permute-start | bytes 356360 | tf_op jit(solution)/shard_map/ppermute | solution.py:30
  70.5 1.9 %collective-permute-done.27 = bf16[16,3712]{1,0:T(8,128)(2,1)S(1)} collective-permute-done((bf16[16,3712]{1,0:T(8,128)(2,1)S(1)}, bf16[16,3712]{1,0:T(8,128)(2,1)S(1)}, u32[]{:S(2)}, u32[]{:S(2)}) %collective-permute-start.27) | collective-permute-done | bytes 118816 | tf_op jit(solution)/shard_map/ppermute | solution.py:30
  72.7 2.0 %collective-permute-done.26 = bf16[16,3712]{1,0:T(8,128)(2,1)S(1)} collective-permute-done((bf16[16,3712]{1,0:T(8,128)(2,1)S(1)}, bf16[16,3712]{1,0:T(8,128)(2,1)S(1)}, u32[]{:S(2)}, u32[]{:S(2)}) %collective-permute-start.26) | collective-permute-done | bytes 118816 | tf_op jit(solution)/shard_map/ppermute | solution.py:30
  74.7 1.0 collective-permute-start.30
  75.8 2.4 %collective-permute-start.29 = (bf16[32,3712]{1,0:T(8,128)(2,1)S(1)}, bf16[32,3712]{1,0:T(8,128)(2,1)S(1)}, u32[]{:S(2)}, u32[]{:S(2)}) collective-permute-start(bf16[32,3712]{1,0:T(8,128)(2,1)S(1)} %constant_dynamic-update-slice_fusion.12), channel_id=1, source_target_pairs={{0,4},{1,3},{2,6},{3,1},{4,0},{5,7},{6,2},{7,5},{8,12},{9,11},{10,... | collective-permute-start | bytes 712712 | tf_op jit(solution)/shard_map/ppermute | solution.py:30
  78.2 2.2 %collective-permute-start.28 = (bf16[32,3712]{1,0:T(8,128)(2,1)S(1)}, bf16[32,3712]{1,0:T(8,128)(2,1)S(1)}, u32[]{:S(2)}, u32[]{:S(2)}) collective-permute-start(bf16[32,3712]{1,0:T(8,128)(2,1)S(1)} %constant_dynamic-update-slice_fusion.14), channel_id=1, source_target_pairs={{0,16},{1,5},{2,18},{3,7},{4,20},{5,1},{6,22},{7,3},{8,24},{9,13},... | collective-permute-start | bytes 712712 | tf_op jit(solution)/shard_map/ppermute | solution.py:30
  80.5 1.5 %fusion.1 = (f32[16,14848]{1,0:T(8,128)}, f32[16,14848]{1,0:T(8,128)}) fusion(bf16[16,14848]{1,0:T(8,128)(2,1)S(1)} %maximum_select_fusion, f32[16,14848]{1,0:T(8,128)S(1)} %copy-done.2, f32[16,14848]{1,0:T(8,128)S(1)} %copy-done.3), kind=kLoop, calls=%fused_computation.3 | loop fusion | flops 1900544 | bytes 4276224 | tf_op jit(solution)/shard_map/add | solution.py:239
  82.1 0.9 collective-permute-start.36
  83.4 2.0 %collective-permute-start.35 = (bf16[64,3712]{1,0:T(8,128)(2,1)S(1)}, bf16[64,3712]{1,0:T(8,128)(2,1)S(1)}, u32[]{:S(2)}, u32[]{:S(2)}) collective-permute-start(bf16[64,3712]{1,0:T(8,128)(2,1)S(1)} %constant_dynamic-update-slice_fusion.18.refs_4_), channel_id=1, source_target_pairs={{0,4},{1,3},{2,6},{3,1},{4,0},{5,7},{6,2},{7,5},{8,12},{9,11},{10,... | collective-permute-start | bytes 1425416 | tf_op jit(solution)/shard_map/ppermute | solution.py:30
  85.4 1.7 %collective-permute-start.34 = (bf16[64,3712]{1,0:T(8,128)(2,1)S(1)}, bf16[64,3712]{1,0:T(8,128)(2,1)S(1)}, u32[]{:S(2)}, u32[]{:S(2)}) collective-permute-start(bf16[64,3712]{1,0:T(8,128)(2,1)S(1)} %constant_dynamic-update-slice_fusion.20.refs_8_), channel_id=1, source_target_pairs={{0,16},{1,5},{2,18},{3,7},{4,20},{5,1},{6,22},{7,3},{8,24},{9,13},... | collective-permute-start | bytes 1425416 | tf_op jit(solution)/shard_map/ppermute | solution.py:30
  87.2 1.3 %collective-permute-start.33 = (bf16[64,3712]{1,0:T(8,128)(2,1)S(1)}, bf16[64,3712]{1,0:T(8,128)(2,1)S(1)}, u32[]{:S(2)}, u32[]{:S(2)}) collective-permute-start(bf16[64,3712]{1,0:T(8,128)(2,1)S(1)} %constant_dynamic-update-slice_fusion.22.refs_0_), channel_id=1, source_target_pairs={{0,2},{1,17},{2,0},{3,19},{4,6},{5,21},{6,4},{7,23},{8,10},{9,25},... | collective-permute-start | bytes 1425416 | tf_op jit(solution)/shard_map/ppermute | solution.py:30
  88.5 3.6 %collective-permute-done.35.refs_5_ = bf16[64,3712]{1,0:T(8,128)(2,1)S(1)} collective-permute-done((bf16[64,3712]{1,0:T(8,128)(2,1)S(1)}, bf16[64,3712]{1,0:T(8,128)(2,1)S(1)}, u32[]{:S(2)}, u32[]{:S(2)}) %collective-permute-start.35) | collective-permute-done | bytes 475168 | tf_op jit(solution)/shard_map/ppermute | solution.py:30
  92.6 2.9 %collective-permute-done.34.refs_9_ = bf16[64,3712]{1,0:T(8,128)(2,1)S(1)} collective-permute-done((bf16[64,3712]{1,0:T(8,128)(2,1)S(1)}, bf16[64,3712]{1,0:T(8,128)(2,1)S(1)}, u32[]{:S(2)}, u32[]{:S(2)}) %collective-permute-start.34) | collective-permute-done | bytes 475168 | tf_op jit(solution)/shard_map/ppermute | solution.py:30
  96.9 1.1 %collective-permute-done.44.refs_11_ = bf16[64,3712]{1,0:T(8,128)(2,1)S(1)} collective-permute-done((bf16[64,3712]{1,0:T(8,128)(2,1)S(1)}, bf16[64,3712]{1,0:T(8,128)(2,1)S(1)}, u32[]{:S(2)}, u32[]{:S(2)}) %collective-permute-start.44) | collective-permute-done | bytes 475168 | tf_op jit(solution)/shard_map/ppermute | solution.py:30
  98.1 0.7 collective-permute-done.40.refs_3_
  98.8 3.4 %apply_update.2.refs_4_ = bf16[256,14848]{1,0:T(8,128)(2,1)} custom-call(bf16[256,256]{1,0:T(8,128)(2,1)S(1)} %copy-done, s32[4,1,256]{2,1,0:T(1,128)S(1)} %copy-done.1, bf16[256,14848]{1,0:T(8,128)(2,1)S(1)} %bitcast.7, bf16[64,3712]{1,0:T(8,128)(2,1)S(1)} %constant_dynamic-update-slice_fusion.16.refs_0_, ...), custom_call_target="tpu_custom_call" | custom-call | flops 1024 | bytes 1024 | tf_op jit(solution)/shard_map/apply_update/pallas_call | solution.py:216
  102.2 2.2 %apply_update.3 = bf16[256,14848]{1,0:T(8,128)(2,1)} custom-call(bf16[256,256]{1,0:T(8,128)(2,1)S(1)} %copy-done, s32[4,1,256]{2,1,0:T(1,128)S(1)} %copy-done.1, bf16[256,14848]{1,0:T(8,128)(2,1)S(1)} %bitcast.7, bf16[64,3712]{1,0:T(8,128)(2,1)S(1)} %constant_dynamic-update-slice_fusion.22.refs_0_, ...), custom_call_target="tpu_custom_call", output_to_operand_aliasing={{}: (7, {})} | custom-call | flops 1024 | bytes 1024 | tf_op jit(solution)/shard_map/apply_update/pallas_call | solution.py:216
  (124 shorter events, 8.1 us)
Async XLA Ops:
  8.7 3.4 %collective-permute-start = (bf16[128,3712]{1,0:T(8,128)(2,1)}, bf16[128,3712]{1,0:T(8,128)(2,1)S(1)}, u32[]{:S(2)}, u32[]{:S(2)}) collective-permute-start(bf16[128,3712]{1,0:T(8,128)(2,1)} %get-tuple-element.131), channel_id=1, source_target_pairs={{0,1},{1,0},{2,3},{3,2},{4,5},{5,4},{6,7},{7,6},{8,9},{9,8},{10,11... | collective-permute-start | bytes 2850824 | tf_op jit(solution)/shard_map/ppermute | solution.py:30
  9.3 7.0 %collective-permute-start.5 = (bf16[128,3712]{1,0:T(8,128)(2,1)}, bf16[128,3712]{1,0:T(8,128)(2,1)}, u32[]{:S(2)}, u32[]{:S(2)}) collective-permute-start(bf16[128,3712]{1,0:T(8,128)(2,1)} %get-tuple-element.149), channel_id=1, source_target_pairs={{0,1},{1,0},{2,3},{3,2},{4,5},{5,4},{6,7},{7,6},{8,9},{9,8},{10,11... | collective-permute-start | bytes 2850824 | tf_op jit(solution)/shard_map/ppermute | solution.py:30
  9.3 9.8 %collective-permute-start.10 = (bf16[128,3712]{1,0:T(8,128)(2,1)}, bf16[128,3712]{1,0:T(8,128)(2,1)}, u32[]{:S(2)}, u32[]{:S(2)}) collective-permute-start(bf16[128,3712]{1,0:T(8,128)(2,1)} %get-tuple-element.167), channel_id=1, source_target_pairs={{0,1},{1,0},{2,3},{3,2},{4,5},{5,4},{6,7},{7,6},{8,9},{9,8},{10,11... | collective-permute-start | bytes 2850824 | tf_op jit(solution)/shard_map/ppermute | solution.py:30
  9.8 12.3 %collective-permute-start.15 = (bf16[128,3712]{1,0:T(8,128)(2,1)}, bf16[128,3712]{1,0:T(8,128)(2,1)}, u32[]{:S(2)}, u32[]{:S(2)}) collective-permute-start(bf16[128,3712]{1,0:T(8,128)(2,1)} %get-tuple-element.185), channel_id=1, source_target_pairs={{0,1},{1,0},{2,3},{3,2},{4,5},{5,4},{6,7},{7,6},{8,9},{9,8},{10,11... | collective-permute-start | bytes 2850824 | tf_op jit(solution)/shard_map/ppermute | solution.py:30
  13.3 15.4 %collective-permute-start.1 = (bf16[64,3712]{1,0:T(8,128)(2,1)S(1)}, bf16[64,3712]{1,0:T(8,128)(2,1)S(1)}, u32[]{:S(2)}, u32[]{:S(2)}) collective-permute-start(bf16[64,3712]{1,0:T(8,128)(2,1)S(1)} %add_convert_fusion.7), channel_id=1, source_target_pairs={{0,2},{1,17},{2,0},{3,19},{4,6},{5,21},{6,4},{7,23},{8,10},{9,25},... | collective-permute-start | bytes 1425416 | tf_op jit(solution)/shard_map/ppermute | solution.py:30
  17.5 12.5 %collective-permute-start.6 = (bf16[64,3712]{1,0:T(8,128)(2,1)S(1)}, bf16[64,3712]{1,0:T(8,128)(2,1)S(1)}, u32[]{:S(2)}, u32[]{:S(2)}) collective-permute-start(bf16[64,3712]{1,0:T(8,128)(2,1)S(1)} %add_convert_fusion.5), channel_id=1, source_target_pairs={{0,16},{1,5},{2,18},{3,7},{4,20},{5,1},{6,22},{7,3},{8,24},{9,13},... | collective-permute-start | bytes 1425416 | tf_op jit(solution)/shard_map/ppermute | solution.py:30
  20.4 12.4 %collective-permute-start.11 = (bf16[64,3712]{1,0:T(8,128)(2,1)S(1)}, bf16[64,3712]{1,0:T(8,128)(2,1)S(1)}, u32[]{:S(2)}, u32[]{:S(2)}) collective-permute-start(bf16[64,3712]{1,0:T(8,128)(2,1)S(1)} %add_convert_fusion.3), channel_id=1, source_target_pairs={{0,4},{1,3},{2,6},{3,1},{4,0},{5,7},{6,2},{7,5},{8,12},{9,11},{10,... | collective-permute-start | bytes 1425416 | tf_op jit(solution)/shard_map/ppermute | solution.py:30
  23.4 11.8 %collective-permute-start.16 = (bf16[64,3712]{1,0:T(8,128)(2,1)S(1)}, bf16[64,3712]{1,0:T(8,128)(2,1)S(1)}, u32[]{:S(2)}, u32[]{:S(2)}) collective-permute-start(bf16[64,3712]{1,0:T(8,128)(2,1)S(1)} %add_convert_fusion.1), channel_id=1, source_target_pairs={{0,2},{1,17},{2,0},{3,19},{4,6},{5,21},{6,4},{7,23},{8,10},{9,25},... | collective-permute-start | bytes 1425416 | tf_op jit(solution)/shard_map/ppermute | solution.py:30
  28.8 9.3 %collective-permute-start.2 = (bf16[32,3712]{1,0:T(8,128)(2,1)S(1)}, bf16[32,3712]{1,0:T(8,128)(2,1)S(1)}, u32[]{:S(2)}, u32[]{:S(2)}) collective-permute-start(bf16[32,3712]{1,0:T(8,128)(2,1)S(1)} %add_convert_fusion.15), channel_id=1, source_target_pairs={{0,16},{1,5},{2,18},{3,7},{4,20},{5,1},{6,22},{7,3},{8,24},{9,13},... | collective-permute-start | bytes 712712 | tf_op jit(solution)/shard_map/ppermute | solution.py:30
  30.1 9.7 %collective-permute-start.7 = (bf16[32,3712]{1,0:T(8,128)(2,1)S(1)}, bf16[32,3712]{1,0:T(8,128)(2,1)S(1)}, u32[]{:S(2)}, u32[]{:S(2)}) collective-permute-start(bf16[32,3712]{1,0:T(8,128)(2,1)S(1)} %add_convert_fusion.13), channel_id=1, source_target_pairs={{0,4},{1,3},{2,6},{3,1},{4,0},{5,7},{6,2},{7,5},{8,12},{9,11},{10,... | collective-permute-start | bytes 712712 | tf_op jit(solution)/shard_map/ppermute | solution.py:30
  32.9 8.5 %collective-permute-start.12 = (bf16[32,3712]{1,0:T(8,128)(2,1)S(1)}, bf16[32,3712]{1,0:T(8,128)(2,1)S(1)}, u32[]{:S(2)}, u32[]{:S(2)}) collective-permute-start(bf16[32,3712]{1,0:T(8,128)(2,1)S(1)} %add_convert_fusion.11), channel_id=1, source_target_pairs={{0,2},{1,17},{2,0},{3,19},{4,6},{5,21},{6,4},{7,23},{8,10},{9,25},... | collective-permute-start | bytes 712712 | tf_op jit(solution)/shard_map/ppermute | solution.py:30
  35.3 7.8 %collective-permute-start.17 = (bf16[32,3712]{1,0:T(8,128)(2,1)S(1)}, bf16[32,3712]{1,0:T(8,128)(2,1)S(1)}, u32[]{:S(2)}, u32[]{:S(2)}) collective-permute-start(bf16[32,3712]{1,0:T(8,128)(2,1)S(1)} %add_convert_fusion.9), channel_id=1, source_target_pairs={{0,16},{1,5},{2,18},{3,7},{4,20},{5,1},{6,22},{7,3},{8,24},{9,13},... | collective-permute-start | bytes 712712 | tf_op jit(solution)/shard_map/ppermute | solution.py:30
  38.1 6.9 %collective-permute-start.3 = (bf16[16,3712]{1,0:T(8,128)(2,1)S(1)}, bf16[16,3712]{1,0:T(8,128)(2,1)S(1)}, u32[]{:S(2)}, u32[]{:S(2)}) collective-permute-start(bf16[16,3712]{1,0:T(8,128)(2,1)S(1)} %add_convert_fusion.23), channel_id=1, source_target_pairs={{0,4},{1,3},{2,6},{3,1},{4,0},{5,7},{6,2},{7,5},{8,12},{9,11},{10,... | collective-permute-start | bytes 356360 | tf_op jit(solution)/shard_map/ppermute | solution.py:30
  39.8 8.0 %collective-permute-start.8 = (bf16[16,3712]{1,0:T(8,128)(2,1)S(1)}, bf16[16,3712]{1,0:T(8,128)(2,1)S(1)}, u32[]{:S(2)}, u32[]{:S(2)}) collective-permute-start(bf16[16,3712]{1,0:T(8,128)(2,1)S(1)} %add_convert_fusion.21), channel_id=1, source_target_pairs={{0,2},{1,17},{2,0},{3,19},{4,6},{5,21},{6,4},{7,23},{8,10},{9,25},... | collective-permute-start | bytes 356360 | tf_op jit(solution)/shard_map/ppermute | solution.py:30
  41.4 10.6 %collective-permute-start.13 = (bf16[16,3712]{1,0:T(8,128)(2,1)S(1)}, bf16[16,3712]{1,0:T(8,128)(2,1)S(1)}, u32[]{:S(2)}, u32[]{:S(2)}) collective-permute-start(bf16[16,3712]{1,0:T(8,128)(2,1)S(1)} %add_convert_fusion.19), channel_id=1, source_target_pairs={{0,16},{1,5},{2,18},{3,7},{4,20},{5,1},{6,22},{7,3},{8,24},{9,13},... | collective-permute-start | bytes 356360 | tf_op jit(solution)/shard_map/ppermute | solution.py:30
  43.1 5.5 %collective-permute-start.18 = (bf16[16,3712]{1,0:T(8,128)(2,1)S(1)}, bf16[16,3712]{1,0:T(8,128)(2,1)S(1)}, u32[]{:S(2)}, u32[]{:S(2)}) collective-permute-start(bf16[16,3712]{1,0:T(8,128)(2,1)S(1)} %add_convert_fusion.17), channel_id=1, source_target_pairs={{0,4},{1,3},{2,6},{3,1},{4,0},{5,7},{6,2},{7,5},{8,12},{9,11},{10,... | collective-permute-start | bytes 356360 | tf_op jit(solution)/shard_map/ppermute | solution.py:30
  45.1 16.9 %collective-permute-start.4 = (bf16[8,3712]{1,0:T(8,128)(2,1)S(1)}, bf16[8,3712]{1,0:T(8,128)(2,1)S(1)}, u32[]{:S(2)}, u32[]{:S(2)}) collective-permute-start(bf16[8,3712]{1,0:T(8,128)(2,1)S(1)} %add_convert_fusion.35), channel_id=1, source_target_pairs={{0,8},{1,9},{2,10},{3,11},{4,12},{5,13},{6,14},{7,15},{8,0},{9,1},... | collective-permute-start | bytes 178184 | tf_op jit(solution)/shard_map/ppermute | solution.py:30
  47.8 11.4 %collective-permute-start.9 = (bf16[8,3712]{1,0:T(8,128)(2,1)S(1)}, bf16[8,3712]{1,0:T(8,128)(2,1)S(1)}, u32[]{:S(2)}, u32[]{:S(2)}) collective-permute-start(bf16[8,3712]{1,0:T(8,128)(2,1)S(1)} %add_convert_fusion.33), channel_id=1, source_target_pairs={{0,8},{1,9},{2,10},{3,11},{4,12},{5,13},{6,14},{7,15},{8,0},{9,1},... | collective-permute-start | bytes 178184 | tf_op jit(solution)/shard_map/ppermute | solution.py:30
  48.6 50.1 %slice-start = ((s8[7602176]{0:T(1024)(128)(4,1)}), s8[4194304]{0:T(1024)(128)(4,1)S(1)}, s32[]{:S(2)}) async-start(s8[7602176]{0:T(1024)(128)(4,1)} %bitcast.6), calls=%async_computation | async-start | bytes 8388608
  48.7 50.1 %copy-start = (bf16[256,256]{1,0:T(8,128)(2,1)S(1)}, bf16[256,256]{1,0:T(8,128)(2,1)}, u32[]{:S(2)}) copy-start(bf16[256,256]{1,0:T(8,128)(2,1)} %projector_ref.3) | copy-start | bytes 393220
  48.7 50.1 %copy-start.1 = (s32[4,1,256]{2,1,0:T(1,128)S(1)}, s32[4,1,256]{2,1,0:T(1,128)}, u32[]{:S(2)}) copy-start(s32[4,1,256]{2,1,0:T(1,128)} %get-tuple-element.129.position_ref) | copy-start | bytes 12292
  48.7 7.2 %collective-permute-start.19 = (bf16[8,3712]{1,0:T(8,128)(2,1)S(1)}, bf16[8,3712]{1,0:T(8,128)(2,1)S(1)}, u32[]{:S(2)}, u32[]{:S(2)}) collective-permute-start(bf16[8,3712]{1,0:T(8,128)(2,1)S(1)} %add_convert_fusion.29), channel_id=1, source_target_pairs={{0,8},{1,9},{2,10},{3,11},{4,12},{5,13},{6,14},{7,15},{8,0},{9,1},... | collective-permute-start | bytes 178184 | tf_op jit(solution)/shard_map/ppermute | solution.py:30
  52.0 6.8 %collective-permute-start.14 = (bf16[8,3712]{1,0:T(8,128)(2,1)S(1)}, bf16[8,3712]{1,0:T(8,128)(2,1)S(1)}, u32[]{:S(2)}, u32[]{:S(2)}) collective-permute-start(bf16[8,3712]{1,0:T(8,128)(2,1)S(1)} %add_convert_fusion.31), channel_id=1, source_target_pairs={{0,8},{1,9},{2,10},{3,11},{4,12},{5,13},{6,14},{7,15},{8,0},{9,1},... | collective-permute-start | bytes 178184 | tf_op jit(solution)/shard_map/ppermute | solution.py:30
  56.0 10.4 %collective-permute-start.23 = (bf16[8,3712]{1,0:T(8,128)(2,1)S(1)}, bf16[8,3712]{1,0:T(8,128)(2,1)S(1)}, u32[]{:S(2)}, u32[]{:S(2)}) collective-permute-start(bf16[8,3712]{1,0:T(8,128)(2,1)S(1)} %get-tuple-element.210), channel_id=1, source_target_pairs={{0,8},{1,9},{2,10},{3,11},{4,12},{5,13},{6,14},{7,15},{8,0},{9,1},... | collective-permute-start | bytes 178184 | tf_op jit(solution)/shard_map/ppermute | solution.py:30
  58.9 8.6 %collective-permute-start.22 = (bf16[8,3712]{1,0:T(8,128)(2,1)S(1)}, bf16[8,3712]{1,0:T(8,128)(2,1)S(1)}, u32[]{:S(2)}, u32[]{:S(2)}) collective-permute-start(bf16[8,3712]{1,0:T(8,128)(2,1)S(1)} %get-tuple-element.212), channel_id=1, source_target_pairs={{0,8},{1,9},{2,10},{3,11},{4,12},{5,13},{6,14},{7,15},{8,0},{9,1},... | collective-permute-start | bytes 178184 | tf_op jit(solution)/shard_map/ppermute | solution.py:30
  59.3 8.5 %collective-permute-start.21 = (bf16[8,3712]{1,0:T(8,128)(2,1)S(1)}, bf16[8,3712]{1,0:T(8,128)(2,1)S(1)}, u32[]{:S(2)}, u32[]{:S(2)}) collective-permute-start(bf16[8,3712]{1,0:T(8,128)(2,1)S(1)} %get-tuple-element.214), channel_id=1, source_target_pairs={{0,8},{1,9},{2,10},{3,11},{4,12},{5,13},{6,14},{7,15},{8,0},{9,1},... | collective-permute-start | bytes 178184 | tf_op jit(solution)/shard_map/ppermute | solution.py:30
  62.1 8.2 %collective-permute-start.20 = (bf16[8,3712]{1,0:T(8,128)(2,1)S(1)}, bf16[8,3712]{1,0:T(8,128)(2,1)S(1)}, u32[]{:S(2)}, u32[]{:S(2)}) collective-permute-start(bf16[8,3712]{1,0:T(8,128)(2,1)S(1)} %get-tuple-element.216), channel_id=1, source_target_pairs={{0,8},{1,9},{2,10},{3,11},{4,12},{5,13},{6,14},{7,15},{8,0},{9,1},... | collective-permute-start | bytes 178184 | tf_op jit(solution)/shard_map/ppermute | solution.py:30
  62.5 17.9 %collective-permute-start.32 = (bf16[8,14848]{1,0:T(8,128)(2,1)S(1)}, bf16[8,14848]{1,0:T(8,128)(2,1)S(1)}, u32[]{:S(2)}, u32[]{:S(2)}) collective-permute-start(bf16[8,14848]{1,0:T(8,128)(2,1)S(1)} %pad_maximum_fusion), channel_id=1, source_target_pairs={{0,16},{1,17},{2,18},{3,19},{4,20},{5,21},{6,22},{7,23},{8,24},{9,... | collective-permute-start | bytes 712712 | tf_op jit(solution)/shard_map/ppermute | solution.py:30
  66.4 5.9 %collective-permute-start.27 = (bf16[16,3712]{1,0:T(8,128)(2,1)S(1)}, bf16[16,3712]{1,0:T(8,128)(2,1)S(1)}, u32[]{:S(2)}, u32[]{:S(2)}) collective-permute-start(bf16[16,3712]{1,0:T(8,128)(2,1)S(1)} %constant_dynamic-update-slice_fusion), channel_id=1, source_target_pairs={{0,4},{1,3},{2,6},{3,1},{4,0},{5,7},{6,2},{7,5},{8,12},{9,11},{10,... | collective-permute-start | bytes 356360 | tf_op jit(solution)/shard_map/ppermute | solution.py:30
  67.5 7.2 %collective-permute-start.26 = (bf16[16,3712]{1,0:T(8,128)(2,1)S(1)}, bf16[16,3712]{1,0:T(8,128)(2,1)S(1)}, u32[]{:S(2)}, u32[]{:S(2)}) collective-permute-start(bf16[16,3712]{1,0:T(8,128)(2,1)S(1)} %constant_dynamic-update-slice_fusion.2), channel_id=1, source_target_pairs={{0,16},{1,5},{2,18},{3,7},{4,20},{5,1},{6,22},{7,3},{8,24},{9,13},... | collective-permute-start | bytes 356360 | tf_op jit(solution)/shard_map/ppermute | solution.py:30
  67.8 8.0 %collective-permute-start.25 = (bf16[16,3712]{1,0:T(8,128)(2,1)S(1)}, bf16[16,3712]{1,0:T(8,128)(2,1)S(1)}, u32[]{:S(2)}, u32[]{:S(2)}) collective-permute-start(bf16[16,3712]{1,0:T(8,128)(2,1)S(1)} %constant_dynamic-update-slice_fusion.4), channel_id=1, source_target_pairs={{0,2},{1,17},{2,0},{3,19},{4,6},{5,21},{6,4},{7,23},{8,10},{9,25},... | collective-permute-start | bytes 356360 | tf_op jit(solution)/shard_map/ppermute | solution.py:30
  70.4 7.8 %collective-permute-start.24 = (bf16[16,3712]{1,0:T(8,128)(2,1)S(1)}, bf16[16,3712]{1,0:T(8,128)(2,1)S(1)}, u32[]{:S(2)}, u32[]{:S(2)}) collective-permute-start(bf16[16,3712]{1,0:T(8,128)(2,1)S(1)} %constant_dynamic-update-slice_fusion.6), channel_id=1, source_target_pairs={{0,4},{1,3},{2,6},{3,1},{4,0},{5,7},{6,2},{7,5},{8,12},{9,11},{10,... | collective-permute-start | bytes 356360 | tf_op jit(solution)/shard_map/ppermute | solution.py:30
  72.4 9.6 %collective-permute-start.31 = (bf16[32,3712]{1,0:T(8,128)(2,1)S(1)}, bf16[32,3712]{1,0:T(8,128)(2,1)S(1)}, u32[]{:S(2)}, u32[]{:S(2)}) collective-permute-start(bf16[32,3712]{1,0:T(8,128)(2,1)S(1)} %constant_dynamic-update-slice_fusion.8), channel_id=1, source_target_pairs={{0,16},{1,5},{2,18},{3,7},{4,20},{5,1},{6,22},{7,3},{8,24},{9,13},... | collective-permute-start | bytes 712712 | tf_op jit(solution)/shard_map/ppermute | solution.py:30
  74.7 8.6 %collective-permute-start.30 = (bf16[32,3712]{1,0:T(8,128)(2,1)S(1)}, bf16[32,3712]{1,0:T(8,128)(2,1)S(1)}, u32[]{:S(2)}, u32[]{:S(2)}) collective-permute-start(bf16[32,3712]{1,0:T(8,128)(2,1)S(1)} %constant_dynamic-update-slice_fusion.10), channel_id=1, source_target_pairs={{0,2},{1,17},{2,0},{3,19},{4,6},{5,21},{6,4},{7,23},{8,10},{9,25},... | collective-permute-start | bytes 712712 | tf_op jit(solution)/shard_map/ppermute | solution.py:30
  75.8 9.6 %collective-permute-start.29 = (bf16[32,3712]{1,0:T(8,128)(2,1)S(1)}, bf16[32,3712]{1,0:T(8,128)(2,1)S(1)}, u32[]{:S(2)}, u32[]{:S(2)}) collective-permute-start(bf16[32,3712]{1,0:T(8,128)(2,1)S(1)} %constant_dynamic-update-slice_fusion.12), channel_id=1, source_target_pairs={{0,4},{1,3},{2,6},{3,1},{4,0},{5,7},{6,2},{7,5},{8,12},{9,11},{10,... | collective-permute-start | bytes 712712 | tf_op jit(solution)/shard_map/ppermute | solution.py:30
  78.2 8.9 %collective-permute-start.28 = (bf16[32,3712]{1,0:T(8,128)(2,1)S(1)}, bf16[32,3712]{1,0:T(8,128)(2,1)S(1)}, u32[]{:S(2)}, u32[]{:S(2)}) collective-permute-start(bf16[32,3712]{1,0:T(8,128)(2,1)S(1)} %constant_dynamic-update-slice_fusion.14), channel_id=1, source_target_pairs={{0,16},{1,5},{2,18},{3,7},{4,20},{5,1},{6,22},{7,3},{8,24},{9,13},... | collective-permute-start | bytes 712712 | tf_op jit(solution)/shard_map/ppermute | solution.py:30
  82.1 10.1 %collective-permute-start.36 = (bf16[64,3712]{1,0:T(8,128)(2,1)S(1)}, bf16[64,3712]{1,0:T(8,128)(2,1)S(1)}, u32[]{:S(2)}, u32[]{:S(2)}) collective-permute-start(bf16[64,3712]{1,0:T(8,128)(2,1)S(1)} %constant_dynamic-update-slice_fusion.16.refs_0_), channel_id=1, source_target_pairs={{0,2},{1,17},{2,0},{3,19},{4,6},{5,21},{6,4},{7,23},{8,10},{9,25},... | collective-permute-start | bytes 1425416 | tf_op jit(solution)/shard_map/ppermute | solution.py:30
  83.4 8.7 %collective-permute-start.35 = (bf16[64,3712]{1,0:T(8,128)(2,1)S(1)}, bf16[64,3712]{1,0:T(8,128)(2,1)S(1)}, u32[]{:S(2)}, u32[]{:S(2)}) collective-permute-start(bf16[64,3712]{1,0:T(8,128)(2,1)S(1)} %constant_dynamic-update-slice_fusion.18.refs_4_), channel_id=1, source_target_pairs={{0,4},{1,3},{2,6},{3,1},{4,0},{5,7},{6,2},{7,5},{8,12},{9,11},{10,... | collective-permute-start | bytes 1425416 | tf_op jit(solution)/shard_map/ppermute | solution.py:30
  85.4 10.1 %collective-permute-start.34 = (bf16[64,3712]{1,0:T(8,128)(2,1)S(1)}, bf16[64,3712]{1,0:T(8,128)(2,1)S(1)}, u32[]{:S(2)}, u32[]{:S(2)}) collective-permute-start(bf16[64,3712]{1,0:T(8,128)(2,1)S(1)} %constant_dynamic-update-slice_fusion.20.refs_8_), channel_id=1, source_target_pairs={{0,16},{1,5},{2,18},{3,7},{4,20},{5,1},{6,22},{7,3},{8,24},{9,13},... | collective-permute-start | bytes 1425416 | tf_op jit(solution)/shard_map/ppermute | solution.py:30
  87.2 8.7 %collective-permute-start.33 = (bf16[64,3712]{1,0:T(8,128)(2,1)S(1)}, bf16[64,3712]{1,0:T(8,128)(2,1)S(1)}, u32[]{:S(2)}, u32[]{:S(2)}) collective-permute-start(bf16[64,3712]{1,0:T(8,128)(2,1)S(1)} %constant_dynamic-update-slice_fusion.22.refs_0_), channel_id=1, source_target_pairs={{0,2},{1,17},{2,0},{3,19},{4,6},{5,21},{6,4},{7,23},{8,10},{9,25},... | collective-permute-start | bytes 1425416 | tf_op jit(solution)/shard_map/ppermute | solution.py:30
  88.5 7.6 %collective-permute-start.43 = (bf16[64,3712]{1,0:T(8,128)(2,1)S(1)}, bf16[64,3712]{1,0:T(8,128)(2,1)S(1)}, u32[]{:S(2)}, u32[]{:S(2)}) collective-permute-start(bf16[64,3712]{1,0:T(8,128)(2,1)S(1)} %constant_dynamic-update-slice_fusion.20.refs_8_), channel_id=1, source_target_pairs={{0,1},{1,0},{2,3},{3,2},{4,5},{5,4},{6,7},{7,6},{8,9},{9,8},{10,11... | collective-permute-start | bytes 1425416 | tf_op jit(solution)/shard_map/ppermute | solution.py:30
  92.1 4.3 %collective-permute-start.41 = (bf16[64,3712]{1,0:T(8,128)(2,1)S(1)}, bf16[64,3712]{1,0:T(8,128)(2,1)S(1)}, u32[]{:S(2)}, u32[]{:S(2)}) collective-permute-start(bf16[64,3712]{1,0:T(8,128)(2,1)S(1)} %constant_dynamic-update-slice_fusion.18.refs_4_), channel_id=1, source_target_pairs={{0,1},{1,0},{2,3},{3,2},{4,5},{5,4},{6,7},{7,6},{8,9},{9,8},{10,11... | collective-permute-start | bytes 1425416 | tf_op jit(solution)/shard_map/ppermute | solution.py:30
  92.1 4.4 %collective-permute-start.39 = (bf16[64,3712]{1,0:T(8,128)(2,1)S(1)}, bf16[64,3712]{1,0:T(8,128)(2,1)S(1)}, u32[]{:S(2)}, u32[]{:S(2)}) collective-permute-start(bf16[64,3712]{1,0:T(8,128)(2,1)S(1)} %constant_dynamic-update-slice_fusion.16.refs_0_), channel_id=1, source_target_pairs={{0,1},{1,0},{2,3},{3,2},{4,5},{5,4},{6,7},{7,6},{8,9},{9,8},{10,11... | collective-permute-start | bytes 1425416 | tf_op jit(solution)/shard_map/ppermute | solution.py:30
  95.5 2.5 %collective-permute-start.42 = (bf16[64,3712]{1,0:T(8,128)(2,1)S(1)}, bf16[64,3712]{1,0:T(8,128)(2,1)S(1)}, u32[]{:S(2)}, u32[]{:S(2)}) collective-permute-start(bf16[64,3712]{1,0:T(8,128)(2,1)S(1)} %collective-permute-done.35.refs_5_), channel_id=1, source_target_pairs={{0,1},{1,0},{2,3},{3,2},{4,5},{5,4},{6,7},{7,6},{8,9},{9,8},{10,11... | collective-permute-start | bytes 1425416 | tf_op jit(solution)/shard_map/ppermute | solution.py:30
  95.9 2.2 %collective-permute-start.44 = (bf16[64,3712]{1,0:T(8,128)(2,1)S(1)}, bf16[64,3712]{1,0:T(8,128)(2,1)S(1)}, u32[]{:S(2)}, u32[]{:S(2)}) collective-permute-start(bf16[64,3712]{1,0:T(8,128)(2,1)S(1)} %collective-permute-done.34.refs_9_), channel_id=1, source_target_pairs={{0,1},{1,0},{2,3},{3,2},{4,5},{5,4},{6,7},{7,6},{8,9},{9,8},{10,11... | collective-permute-start | bytes 1425416 | tf_op jit(solution)/shard_map/ppermute | solution.py:30
  96.1 2.7 %collective-permute-start.40 = (bf16[64,3712]{1,0:T(8,128)(2,1)S(1)}, bf16[64,3712]{1,0:T(8,128)(2,1)S(1)}, u32[]{:S(2)}, u32[]{:S(2)}) collective-permute-start(bf16[64,3712]{1,0:T(8,128)(2,1)S(1)} %collective-permute-done.36.refs_1_), channel_id=1, source_target_pairs={{0,1},{1,0},{2,3},{3,2},{4,5},{5,4},{6,7},{7,6},{8,9},{9,8},{10,11... | collective-permute-start | bytes 1425416 | tf_op jit(solution)/shard_map/ppermute | solution.py:30
  96.4 5.8 %collective-permute-start.37 = (bf16[64,3712]{1,0:T(8,128)(2,1)S(1)}, bf16[64,3712]{1,0:T(8,128)(2,1)S(1)}, u32[]{:S(2)}, u32[]{:S(2)}) collective-permute-start(bf16[64,3712]{1,0:T(8,128)(2,1)S(1)} %constant_dynamic-update-slice_fusion.22.refs_0_), channel_id=1, source_target_pairs={{0,1},{1,0},{2,3},{3,2},{4,5},{5,4},{6,7},{7,6},{8,9},{9,8},{10,11... | collective-permute-start | bytes 1425416 | tf_op jit(solution)/shard_map/ppermute | solution.py:30
  96.6 5.6 %collective-permute-start.38 = (bf16[64,3712]{1,0:T(8,128)(2,1)S(1)}, bf16[64,3712]{1,0:T(8,128)(2,1)S(1)}, u32[]{:S(2)}, u32[]{:S(2)}) collective-permute-start(bf16[64,3712]{1,0:T(8,128)(2,1)S(1)} %collective-permute-done.33.refs_1_), channel_id=1, source_target_pairs={{0,1},{1,0},{2,3},{3,2},{4,5},{5,4},{6,7},{7,6},{8,9},{9,8},{10,11... | collective-permute-start | bytes 1425416 | tf_op jit(solution)/shard_map/ppermute | solution.py:30
  (5 other events, 119.9 us)
